TPU v7x, 256 devices: a whole 4x4x8 slice. The times are simulated.
256 devices in a mesh: seg: 64 (over y_hi, x, z), fsdp: 4 (over y_lo, core).
Axes of the slice: x: 4, y: 4 (y_hi: 2, y_lo: 2; y = y_hi * 2 + y_lo), z: 8, core: 2. Of those that a mesh axis runs over, the one named last changes fastest.
Arguments:
- tokens: bfloat16 [4, 8192, 4096], P('fsdp', 'seg'), may hold values from -6 to 6
- w_kv: bfloat16 [4096, 4096], P('fsdp'), may hold values from -0.09375 to 0.09375
- q_state: bfloat16 [256, 2048], P('fsdp'), may hold values from -400 to 400
- decay: float32 [64, 2048], P('seg'), may hold values from 0 to 1
Outputs:
- states: bfloat16 [4, 64, 256, 2048], P('fsdp', 'seg')
All inputs are finite; a program needn't handle non-finite values.
Results may differ from a plain program's by a relative error of at most 0.011.
Values may be sent and summed in bfloat16 or wider, within the bound.
No kernel may reach another device: no remote copies, remote signals or barrier semaphores. Data moves between devices by JAX's collectives and lax.ppermute only.
A program may use at most 320 MiB of HBM per device.

v0:
```python
import math

import jax
import jax.numpy as jnp
from jax import lax
from jax.sharding import PartitionSpec as P

HEADS = 16
HS = 128
S = 256


def entering(value, axis, combine, identity):
    peers, index = (lax.axis_size(axis), lax.axis_index(axis))
    everything = jax.tree.map(lambda part: lax.all_gather(part, axis), value)
    start = jax.tree.map(
        lambda part, zero: jnp.broadcast_to(jnp.asarray(zero, part.dtype), part.shape),
        value,
        identity,
    )

    def hop(k, before):
        reached = k < index
        new = combine(before, jax.tree.map(lambda part: part[k], everything))
        return jax.tree.map(lambda a, b: jnp.where(reached, a, b), new, before)

    return lax.fori_loop(0, peers, hop, start)


def merge_recurrent_state(earlier, later):
    return (earlier[0] * later[0], later[0][None, :] * earlier[1] + later[1])


def body(tokens, w_kv, q_state, decay):
    own_tokens = tokens[0]
    tok_count = own_tokens.shape[0]
    seg_count = decay.shape[0]
    seg_len = tok_count // seg_count
    feature_width = q_state.shape[1]
    row_piece = lax.all_gather(w_kv, "fsdp", axis=0, tiled=True)
    query_piece = lax.all_gather(q_state, "fsdp", axis=0, tiled=True)
    summed = jnp.dot(own_tokens, row_piece, preferred_element_type=jnp.float32)
    rounded_kv = summed.astype(jnp.bfloat16)
    key_heads = rounded_kv[:, :feature_width].reshape(seg_count, seg_len, HEADS, HS)
    value_heads = rounded_kv[:, feature_width:].reshape(seg_count, seg_len, HEADS, HS)
    query = query_piece.reshape(S, HEADS, HS)
    scores = jnp.einsum("rhe,gthe->ghrt", query, key_heads, preferred_element_type=jnp.float32) * (
        1.0 / math.sqrt(HS)
    )
    weights = jax.nn.softmax(scores, axis=-1).astype(jnp.bfloat16)
    update = jnp.einsum("ghrt,gthe->grhe", weights, value_heads, preferred_element_type=jnp.float32)
    update = update.reshape(seg_count, S, feature_width)
    local_decay = decay[0]
    local_state = update[0]
    identity = (jnp.ones_like(local_decay), jnp.zeros_like(local_state))
    cumulative_decay, carried = entering(
        (local_decay, local_state), "seg", merge_recurrent_state, identity
    )
    running = carried
    running = decay[0][None, :] * running + update[0]
    outputs = [running.astype(jnp.bfloat16)]
    return jnp.stack(outputs, axis=0)[None]


def solution(mesh):
    return jax.shard_map(
        body,
        mesh=mesh,
        in_specs=(P("fsdp", "seg", None), P("fsdp", None), P("fsdp", None), P("seg", None)),
        out_specs=P("fsdp", "seg", None, None),
        check_vma=False,
    )
```

profile of v0, /device:TPU:1, one launch (start us, length us, event | category | flops | bytes accessed | tf_op | source)
XLA Modules:
  0.0 1723.0 jit_solution(9441040339327262813)
XLA Ops:
  8.1 28.6 %all-gather.7.cloned.1.call-done = bf16[256,2048]{1,0:T(8,128)(2,1)} async-done(((bf16[64,2048]{1,0:T(8,128)(2,1)}), bf16[256,2048]{1,0:T(8,128)(2,1)}) %all-gather.7.cloned.1.call-update) | async-done | bytes 1048592 | tf_op jit(solution)/shard_map/all_gather | solution.py:41
  38.1 294.8 %all-gather.5.cloned.1.call-done = bf16[4096,4096]{1,0:T(8,128)(2,1)} async-done(((bf16[1024,4096]{1,0:T(8,128)(2,1)}), bf16[4096,4096]{1,0:T(8,128)(2,1)}) %all-gather.5.cloned.1.call-update) | async-done | bytes 33554448 | tf_op jit(solution)/shard_map/all_gather | solution.py:40
  333.0 13.0 convolution_convert_fusion
  351.5 159.9 %all-gather = f32[64,1,2048]{2,1,0:T(1,128)S(1)} all-gather(f32[1,1,2048]{2,1,0:T(1,128)S(1)} %bitcast.61), channel_id=1, replica_groups=mesh['seg'=64,'fsdp'=4] {'seg'}, dimensions={0}, use_global_device_ids=true | all-gather | bytes 532480 | tf_op jit(solution)/shard_map/all_gather | solution.py:15
  515.3 922.3 %all-gather.9.cloned.1.call-done = f32[64,256,2048]{2,1,0:T(8,128)} async-done(((f32[1,256,2048]{2,1,0:T(8,128)}), f32[64,256,2048]{2,1,0:T(8,128)}) %all-gather.9.cloned.1.call-update) | async-done | bytes 134217744 | tf_op jit(solution)/shard_map/all_gather | solution.py:15
  1437.6 276.0 %while.14 = (s32[]{:T(128)}, f32[256,2048]{1,0:T(8,128)S(1)}, s32[]{:T(128)}, f32[64,2048]{1,0:T(8,128)}, f32[64,256,2048]{2,1,0:T(8,128)}, /*index=5*/s32[]{:T(128)}, s32[]{:T(128)}) while((s32[]{:T(128)}, f32[256,2048]{1,0:T(8,128)S(1)}, s32[]{:T(128)}, f32[64,2048]{1,0:T(8,128)}, f32[64,256,2048]{2,1,0:T(8,128)}, ...), condition=%wide.region_3.4_spmd.clone, body=%wide.region_2.3_spmd.clone.sunk | while | flops 2097156 | bytes 6316137 | solution.py:27
  1438.5 3.4 fusion.17
  1442.8 3.4 fusion.17
  1447.1 3.4 fusion.17
  1451.4 3.4 fusion.17
  1455.7 3.4 fusion.17
  1460.0 3.4 fusion.17
  1464.3 3.4 fusion.17
  1468.6 3.4 fusion.17
  1473.0 3.4 fusion.17
  1477.3 3.4 fusion.17
  1481.6 3.4 fusion.17
  1485.9 3.4 fusion.17
  1490.2 3.4 fusion.17
  1494.5 3.4 fusion.17
  1498.8 3.4 fusion.17
  1503.1 3.4 fusion.17
  1507.5 3.4 fusion.17
  1511.8 3.4 fusion.17
  1516.1 3.4 fusion.17
  1520.4 3.4 fusion.17
  1524.7 3.4 fusion.17
  1529.0 3.4 fusion.17
  1533.3 3.4 fusion.17
  1537.6 3.4 fusion.17
  1542.0 3.4 fusion.17
  1546.3 3.4 fusion.17
  1550.6 3.4 fusion.17
  1554.9 3.4 fusion.17
  1559.2 3.4 fusion.17
  1563.5 3.4 fusion.17
  1567.8 3.4 fusion.17
  1572.1 3.4 fusion.17
  1576.5 3.4 fusion.17
  1580.8 3.4 fusion.17
  1585.1 3.4 fusion.17
  1589.4 3.4 fusion.17
  1593.7 3.4 fusion.17
  1598.0 3.4 fusion.17
  1602.3 3.4 fusion.17
  1606.6 3.4 fusion.17
  1610.9 3.4 fusion.17
  1615.3 3.4 fusion.17
  1619.6 3.4 fusion.17
  1623.9 3.4 fusion.17
  1628.2 3.4 fusion.17
  1632.5 3.4 fusion.17
  1636.8 3.4 fusion.17
  1641.1 3.4 fusion.17
  1645.4 3.4 fusion.17
  1649.8 3.4 fusion.17
  1654.1 3.4 fusion.17
  1658.4 3.4 fusion.17
  1662.7 3.4 fusion.17
  1667.0 3.4 fusion.17
  1671.3 3.4 fusion.17
  1675.6 3.4 fusion.17
  1679.9 3.4 fusion.17
  1688.6 3.4 fusion.17
  (95 shorter events, 90.4 us)
Async XLA Ops:
  6.5 326.5 %copy-start = (bf16[1,128,4096]{2,1,0:T(8,128)(2,1)S(1)}, bf16[1,128,4096]{2,1,0:T(8,128)(2,1)}, u32[]{:S(2)}) copy-start(bf16[1,128,4096]{2,1,0:T(8,128)(2,1)} %param.6) | copy-start | bytes 3145732
  6.5 30.1 %all-gather.7.cloned.1.call-start = ((), (), s32[]{:S(2)}) async-start(), calls=%async_computation.1 | async-start | bytes 1310720 | tf_op jit(solution)/shard_map/all_gather | solution.py:41
  7.3 325.7 %all-gather.5.cloned.1.call-start = ((), (), s32[]{:S(2)}) async-start(), calls=%async_computation | async-start | bytes 41943040 | tf_op jit(solution)/shard_map/all_gather | solution.py:40
  8.0 1429.6 %all-gather.9.cloned.1.call-start = ((), (), s32[]{:S(2)}) async-start(), calls=%async_computation.2 | async-start | bytes 136314880 | tf_op jit(solution)/shard_map/all_gather | solution.py:15
  347.1 1.0 copy-start.2
  348.8 2.0 copy-start.1
  350.8 0.7 copy-start.3
Sparse Core Ops, SparseCore 0:
  9.2 27.4 all-gather.6
  38.5 294.4 all-gather.4
  351.0 1086.5 all-gather.8
where the time goes:
time: 1730 us; the launch traced here: 1720 us
  waiting for transfers between devices  1250 us (72%)
  other arithmetic  224 us (13%)
  blocking collectives  160 us (9%)
  local copies, waits for them, and re-layouts  63.9 us (4%)
    all_gather x1, waiting for transfers between devices, entering(): everything = jax.tree.map(lambda part: lax.all_gather(part, axis), value)  922 us
    all_gather x1, waiting for transfers between devices, body(): row_piece = lax.all_gather(w_kv, 'fsdp', axis=0, tiled=True)  295 us
    select_n x64, other arithmetic, hop(): return jax.tree.map(lambda a, b: jnp.where(reached, a, b), new, before)  220 us
    all_gather x1, blocking collectives, entering(): everything = jax.tree.map(lambda part: lax.all_gather(part, axis), value)  160 us
    dynamic_slice x64, local copies, waits for them, and re-layouts, hop(): new = combine(before, jax.tree.map(lambda part: part[k], everything))  54.5 us
  transfers between devices with their start and end apart: 3, of which 3 were waited for; matrix products, arithmetic and copies ran while one was open for 0% of the time, Pallas kernels for 0%

commit v1 on v0

v1 whole, which is shorter than its diff:
```python
import functools
import math

import jax
import jax.numpy as jnp
from jax import lax
from jax.experimental import pallas as pl
from jax.experimental.pallas import tpu as pltpu
from jax.sharding import PartitionSpec as P

HEADS = 16
HS = 128
S = 256
SEG = 64
TOK = 128
D = 4096
HD = 2048
QUARTER = D // 4
HALF = HD // 2
BOTH = ("seg", "fsdp")
BF = jnp.bfloat16
F32 = jnp.float32


def flat(y, x, z, core):
    return (((y // 2) * 4 + x) * 8 + z) * 4 + (y % 2) * 2 + core


def moves(dy, dc):
    pairs = []
    for y in range(4):
        for x in range(4):
            for z in range(8):
                for core in range(2):
                    pairs.append((flat(y, x, z, core), flat((y + dy) % 4, x, z, (core + dc) % 2)))
    return pairs


UP, DOWN = moves(1, 0), moves(-1, 0)
UP_X, DOWN_X = moves(1, 1), moves(-1, 1)
SIB = moves(0, 1)


def send(value, pairs):
    return lax.ppermute(value, BOTH, pairs)


TILE = 512


def project_kernel(core_ref, *refs, splits):
    pieces = refs[: len(splits)]
    w_ref, sk_ref, sv_ref = refs[len(splits) : len(splits) + 3]
    outs = refs[len(splits) + 3 : -1]
    x_ref = refs[-1]
    step = pl.program_id(0)
    core = core_ref[0]

    @pl.when(step == 0)
    def _():
        at = 0
        for piece, rows in zip(pieces, splits):
            x_ref[at : at + rows, :] = piece[...]
            at += rows

    own = pl.ds(pl.multiple_of(core * QUARTER, QUARTER), QUARTER)
    other = pl.ds(pl.multiple_of((1 - core) * QUARTER, QUARTER), QUARTER)

    def emit(sib):
        total = jnp.dot(x_ref[:, own], w_ref[...], preferred_element_type=F32)
        total += jnp.dot(x_ref[:, other], sib[...], preferred_element_type=F32)
        at = 0
        for out in outs:
            rows = out.shape[0]
            out[...] = total[at : at + rows].astype(out.dtype)
            at += rows

    half = HALF // TILE

    @pl.when(step < half)
    def _():
        emit(sk_ref)

    @pl.when(step >= half)
    def _():
        emit(sv_ref)


def project(core, pieces, w, sib_k, sib_v, out_rows, dtype):
    half = HALF // TILE
    splits = [p.shape[0] for p in pieces]
    total = sum(splits)

    def w_map(j, core_ref):
        return (0, (j // half) * (HD // TILE) + core_ref[0] * half + j % half)

    return pl.pallas_call(
        functools.partial(project_kernel, splits=splits),
        grid_spec=pltpu.PrefetchScalarGridSpec(
            num_scalar_prefetch=1,
            grid=(2 * half,),
            in_specs=[pl.BlockSpec(p.shape, lambda j, c: (0, 0)) for p in pieces]
            + [
                pl.BlockSpec((QUARTER, TILE), w_map),
                pl.BlockSpec((QUARTER, TILE), lambda j, c: (0, jnp.minimum(j, half - 1))),
                pl.BlockSpec((QUARTER, TILE), lambda j, c: (0, jnp.maximum(j - half, 0))),
            ],
            out_specs=[pl.BlockSpec((rows, TILE), lambda j, c: (0, j)) for rows in out_rows],
            scratch_shapes=[pltpu.VMEM((total, 2 * QUARTER), BF)],
        ),
        out_shape=[jax.ShapeDtypeStruct((rows, HD), dtype) for rows in out_rows],
        compiler_params=pltpu.CompilerParams(vmem_limit_bytes=40 << 20),
        cost_estimate=pl.CostEstimate(
            flops=2 * total * 2 * QUARTER * HD, bytes_accessed=2 * 2 * QUARTER * HD + total * HD * 8, transcendentals=0
        ),
    )(core, *pieces, w, sib_k, sib_v)


def one_head(q, k, v):
    scores = lax.dot_general(q, k, (((1,), (1,)), ((), ())), preferred_element_type=F32) * (1.0 / math.sqrt(HS))
    scores = jnp.exp(scores - jnp.max(scores, axis=1, keepdims=True))
    weights = (scores / jnp.sum(scores, axis=1, keepdims=True)).astype(BF)
    return jnp.dot(weights, v, preferred_element_type=F32).astype(BF)


def attend_kernel(core_ref, *refs):
    q_own, q_other, out_ref = refs[-3:]
    core = core_ref[0]
    j = pl.program_id(0)
    for at, q_ref, half in ((0, q_own, core), (6, q_other, 1 - core)):
        ak, av, pk, pv, mk, mv = refs[at : at + 6]
        k = (ak[...] + jnp.concatenate([pk[...], mk[...]], axis=0).astype(F32)).astype(BF)
        v = (av[...] + jnp.concatenate([pv[...], mv[...]], axis=0).astype(F32)).astype(BF)
        out_ref[half * (HEADS // 2) + j] = one_head(q_ref[...], k, v)


def attend(core, own, other, q):
    heads = HEADS // 2
    in_specs, args = [], []
    for local, up, down in (own, other):
        for part in (local, up, down):
            for shift in (0, heads):
                in_specs.append(pl.BlockSpec((part.shape[0], HS), lambda j, c, shift=shift: (0, j + shift)))
                args.append(part)
    in_specs.append(pl.BlockSpec((S, HS), lambda j, c: (0, c[0] * heads + j)))
    in_specs.append(pl.BlockSpec((S, HS), lambda j, c: (0, (1 - c[0]) * heads + j)))
    return pl.pallas_call(
        attend_kernel,
        grid_spec=pltpu.PrefetchScalarGridSpec(
            num_scalar_prefetch=1,
            grid=(heads,),
            in_specs=in_specs,
            out_specs=pl.BlockSpec((HEADS, S, HS), lambda j, c: (0, 0, 0)),
        ),
        out_shape=jax.ShapeDtypeStruct((HEADS, S, HS), BF),
        compiler_params=pltpu.CompilerParams(vmem_limit_bytes=32 << 20),
        cost_estimate=pl.CostEstimate(flops=4 * HEADS * S * TOK * HS, bytes_accessed=5 << 20, transcendentals=HEADS * S * TOK),
    )(core, *args, q, q)


SCAN_STEP = 16


def scan_kernel(decay_ref, update_ref, out_ref, carry_ref):
    @pl.when(pl.program_id(0) == 0)
    def _():
        carry_ref[...] = jnp.zeros_like(carry_ref)

    carry = carry_ref[...]
    for i in range(SCAN_STEP):
        carry = decay_ref[i] * carry + update_ref[i].astype(F32)
        out_ref[i] = carry.astype(BF)
    carry_ref[...] = carry


def scan(decay, update):
    rows = update.shape[1]
    return pl.pallas_call(
        scan_kernel,
        grid=(SEG // SCAN_STEP,),
        in_specs=[
            pl.BlockSpec((SCAN_STEP, 1, HS), lambda i: (i, 0, 0)),
            pl.BlockSpec((SCAN_STEP, rows, HS), lambda i: (i, 0, 0)),
        ],
        out_specs=pl.BlockSpec((SCAN_STEP, rows, HS), lambda i: (i, 0, 0)),
        out_shape=jax.ShapeDtypeStruct(update.shape, BF),
        scratch_shapes=[pltpu.VMEM((rows, HS), F32)],
        cost_estimate=pl.CostEstimate(flops=2 * update.size, bytes_accessed=4 * update.size, transcendentals=0),
    )(decay, update)


def gather_queries(q, y_lo, core):
    rows = q.shape[0] // 2
    far = jnp.concatenate([send(q[:rows], UP), send(q[rows:], DOWN)], axis=0)
    pair = jnp.concatenate([q, far], axis=0)
    sib = send(pair, SIB)
    near0 = jnp.where(core == 0, pair, sib)
    near1 = jnp.where(core == 0, sib, pair)
    n = q.shape[0]
    mine = jnp.concatenate([near0[:n], near1[:n]], axis=0)
    theirs = jnp.concatenate([near0[n:], near1[n:]], axis=0)
    return jnp.concatenate([jnp.where(y_lo == 0, mine, theirs), jnp.where(y_lo == 0, theirs, mine)], axis=0)


def body(tokens, w_kv, q_state, decay):
    own_tokens = tokens[0]
    place = lax.axis_index("fsdp")
    y_lo, core = place // 2, place % 2
    core_arg = core.astype(jnp.int32).reshape(1)
    away = lax.dynamic_slice_in_dim(own_tokens, (1 - y_lo) * 2 * QUARTER, 2 * QUARTER, axis=1)
    home = lax.dynamic_slice_in_dim(own_tokens, y_lo * 2 * QUARTER, 2 * QUARTER, axis=1)
    lower = send(away[: TOK // 2], UP)
    upper = send(away[TOK // 2 :], DOWN)
    sib_k = send(lax.dynamic_slice_in_dim(w_kv, (1 - core) * HALF, HALF, axis=1), SIB)
    sib_v = send(lax.dynamic_slice_in_dim(w_kv, HD + (1 - core) * HALF, HALF, axis=1), SIB)
    sib_home = send(home, SIB)
    gate = jnp.repeat(decay[0].reshape(HEADS, 1, HS), S // 64, axis=0)
    gate = lax.all_to_all(gate, "seg", 0, 0, tiled=True)
    query = gather_queries(q_state, y_lo, core)
    lower_sib, upper_sib = send(lower, SIB), send(upper, SIB)

    half_rows = TOK // 2
    far = project(core_arg, [lower, lower_sib, upper, upper_sib], w_kv, sib_k, sib_v, [half_rows] * 4, BF)
    own_up, own_down = send(far[0], DOWN), send(far[2], UP)
    other_up, other_down = send(far[1], DOWN_X), send(far[3], UP_X)
    near, near_sib = project(core_arg, [home, sib_home], w_kv, sib_k, sib_v, [TOK] * 2, F32)
    near_other = send(near_sib, SIB)
    update = attend(core_arg, (near, own_up, own_down), (near_other, other_up, other_down), query)
    update = lax.all_to_all(update.reshape(SEG, S // 4, HS), "seg", 0, 0, tiled=True)
    states = scan(gate, update)
    states = lax.all_to_all(states, "seg", 0, 0, tiled=True)
    states = states.reshape(HEADS, S, HS).transpose(1, 0, 2).reshape(S, HD)
    return states[None, None]


def solution(mesh):
    return jax.shard_map(
        body,
        mesh=mesh,
        in_specs=(P("fsdp", "seg", None), P("fsdp", None), P("fsdp", None), P("seg", None)),
        out_specs=P("fsdp", "seg", None, None),
        check_vma=False,
    )
```

time: 1730 us -> 160 us (0.09)
  waiting for transfers between devices: 1250 us -> 19.1 us
  other arithmetic: 224 us -> 1.6 us
  blocking collectives: 160 us -> 73.2 us
  local copies, waits for them, and re-layouts: 63.9 us -> 11.3 us
  starting transfers between devices: 0.08 us -> 28.6 us
  Pallas kernels: 0 us -> 22.7 us
    all_gather x3 -> x0, waiting for transfers between devices: 1250 us -> none  [the longest x1 922 us: entering(): everything = jax.tree.map(lambda part: lax.all_gather(part, axis), value)]
    select_n x64 -> x2, other arithmetic: 220 us -> 1.5 us  [the longest x1 1.27 us: gather_queries(): near0 = jnp.where(core == 0, pair, sib)]
    all_gather x1 -> x0, blocking collectives: 160 us -> none  [entering(): everything = jax.tree.map(lambda part: lax.all_gather(part, axis), value)]
    all_to_all x0 -> x2, blocking collectives: none -> 73.2 us  [the longest x1 38.7 us: body(): lax.all_to_all(update.reshape(SEG, S // 4, HS), 'seg', 0, 0, tiled=True)]
    dynamic_slice x64 -> x2, local copies, waits for them, and re-layouts: 54.5 us -> 5.79 us  [the longest x1 4.72 us: body(): lax.dynamic_slice_in_dim(w_kv, HD + (1 - core) * HALF, HALF, axis=1)]
    pallas_call x0 -> x4, Pallas kernels: none -> 22.7 us  [the longest x2 11.5 us: project(): pl.pallas_call(functools.partial(project_kernel, splits=splits), grid_spe...]
    ppermute x0 -> x15, waiting for transfers between devices: none -> 19.1 us  [send(): return lax.ppermute(value, BOTH, pairs)]
    ppermute x0 -> x15, starting transfers between devices: none -> 18.1 us  [send(): return lax.ppermute(value, BOTH, pairs)]
  transfers between devices with their start and end apart: 3 -> 16, of which waited for: 3 -> 6; matrix products, arithmetic and copies ran while one was open for 0% -> 4% of each run, Pallas kernels for 0% -> 12%
where the time goes in v1:
time: 160 us; the launch traced here: 157 us
  blocking collectives  73.2 us (46%)
  starting transfers between devices  28.6 us (18%)
  Pallas kernels  22.7 us (14%)
  waiting for transfers between devices  19.1 us (12%)
  local copies, waits for them, and re-layouts  11.3 us (7%)
  other arithmetic  1.6 us (1%)
    all_to_all x1, blocking collectives, body(): lax.all_to_all(update.reshape(SEG, S // 4, HS), 'seg', 0, 0, tiled=True)  38.7 us
    all_to_all x1, blocking collectives, body(): states = lax.all_to_all(states, 'seg', 0, 0, tiled=True)  34.5 us
    ppermute x15, waiting for transfers between devices, send(): return lax.ppermute(value, BOTH, pairs)  19.1 us
    ppermute x15, starting transfers between devices, send(): return lax.ppermute(value, BOTH, pairs)  18.1 us
    pallas_call x2, Pallas kernels, project(): pl.pallas_call(functools.partial(project_kernel, splits=splits), grid_spe...  11.5 us
    all_to_all x1, starting transfers between devices, body(): gate = lax.all_to_all(gate, 'seg', 0, 0, tiled=True)  10.5 us
    pallas_call x1, Pallas kernels, attend(): pl.pallas_call(attend_kernel, grid_spec=pltpu.PrefetchScalarGridSpec(num_...  7.72 us
    dynamic_slice x1, local copies, waits for them, and re-layouts, body(): lax.dynamic_slice_in_dim(w_kv, HD + (1 - core) * HALF, HALF, axis=1)  4.72 us
  transfers between devices with their start and end apart: 16, of which 6 were waited for; matrix products, arithmetic and copies ran while one was open for 4% of the time, Pallas kernels for 12%

profile of v1, /device:TPU:1, one launch (start us, length us, event | category | flops | bytes accessed | tf_op | source)
XLA Modules:
  0.0 156.6 jit_solution(8271871563881811803)
XLA Ops:
  0.0 0.0 copy-start.1
  0.0 0.0 copy-start
  0.0 4.7 %constant_dynamic-slice_fusion = (bf16[1024,1024]{1,0:T(8,128)(2,1)}, bf16[1024,1024]{1,0:T(8,128)(2,1)}) fusion(bf16[1024,4096]{1,0:T(8,128)(2,1)} %refs_4_.1, s32[]{:T(128)S(6)} %select_n.49, s32[]{:T(128)S(6)} %select_n.48), kind=kLoop, calls=%fused_computation.13 | loop fusion | bytes 8388616 | tf_op jit(solution)/shard_map/dynamic_slice | solution.py:215
  4.7 0.0 copy-start.3
  4.7 3.2 %collective-permute-start.1 = (bf16[1024,1024]{1,0:T(8,128)(2,1)}, bf16[1024,1024]{1,0:T(8,128)(2,1)S(1)}, u32[]{:S(2)}, u32[]{:S(2)}) collective-permute-start(bf16[1024,1024]{1,0:T(8,128)(2,1)} %get-tuple-element.18), channel_id=1, source_target_pairs={{0,1},{1,0},{4,5},{5,4},{8,9},{9,8},{12,13},{13,12},{16,17},{17,16... | collective-permute-start | bytes 6291464 | tf_op jit(solution)/shard_map/ppermute | solution.py:45
  8.0 0.0 collective-permute-start.2
  8.0 0.0 copy-done.1
  8.0 0.1 collective-permute-start.12
  8.1 2.7 %collective-permute-start.13 = (bf16[32,2048]{1,0:T(8,128)(2,1)S(1)}, bf16[32,2048]{1,0:T(8,128)(2,1)S(1)}, u32[]{:S(2)}, u32[]{:S(2)}) collective-permute-start(bf16[32,2048]{1,0:T(8,128)(2,1)S(1)} %get-tuple-element.29), channel_id=1, source_target_pairs={{0,130},{1,131},{4,134},{5,135},{8,138},{9,139},{12,142},{13,143},... | collective-permute-start | bytes 393224 | tf_op jit(solution)/shard_map/ppermute | solution.py:45
  10.8 0.7 constant_dynamic-update-slice_fusion.2
  11.5 2.4 %collective-permute-done.12 = bf16[32,2048]{1,0:T(8,128)(2,1)S(1)} collective-permute-done((bf16[32,2048]{1,0:T(8,128)(2,1)S(1)}, bf16[32,2048]{1,0:T(8,128)(2,1)S(1)}, u32[]{:S(2)}, u32[]{:S(2)}) %collective-permute-start.12) | collective-permute-done | bytes 131104 | tf_op jit(solution)/shard_map/ppermute | solution.py:45
  13.8 0.7 constant_dynamic-update-slice_fusion.1
  14.5 0.0 collective-permute-done.13
  14.5 0.7 constant_dynamic-update-slice_fusion
  15.2 1.4 collective-permute-start.14
  16.5 0.0 copy-done
  16.5 0.7 dynamic-slice_bitcast_fusion.1
  17.3 0.0 collective-permute-start.3
  17.3 2.7 %collective-permute-start.5 = (bf16[64,2048]{1,0:T(8,128)(2,1)}, bf16[64,2048]{1,0:T(8,128)(2,1)}, u32[]{:S(2)}, u32[]{:S(2)}) collective-permute-start(bf16[64,2048]{1,0:T(8,128)(2,1)} %get-tuple-element.23), channel_id=1, source_target_pairs={{0,130},{1,131},{4,134},{5,135},{8,138},{9,139},{12,142},{13,143},... | collective-permute-start | bytes 786440 | tf_op jit(solution)/shard_map/ppermute | solution.py:45
  19.9 1.1 dynamic-slice_bitcast_fusion.refs_0_
  21.0 5.4 %collective-permute-done.3.refs_0_ = bf16[64,2048]{1,0:T(8,128)(2,1)S(1)} collective-permute-done((bf16[64,2048]{1,0:T(8,128)(2,1)S(1)}, bf16[64,2048]{1,0:T(8,128)(2,1)S(1)}, u32[]{:S(2)}, u32[]{:S(2)}) %collective-permute-start.3) | collective-permute-done | bytes 262176 | tf_op jit(solution)/shard_map/ppermute | solution.py:45
  26.4 0.8 collective-permute-start
  27.2 0.0 copy-done.3
  27.2 0.6 broadcast_in_dim.5
  27.8 10.5 %all-to-all-start = ((f32[64,1,128]{2,1,0:T(1,128)}), f32[64,1,128]{2,1,0:T(1,128)S(1)}, u32[]{:S(2)}, u32[]{:S(2)}) async-start(f32[64,1,128]{2,1,0:T(1,128)} %bitcast.1), calls=%async_computation | async-start | bytes 65536 | tf_op jit(solution)/shard_map/all_to_all | solution.py:218
  38.3 0.0 collective-permute-done.5.refs_2_
  38.3 0.4 collective-permute-start.4
  38.7 0.0 collective-permute-done.14
  38.7 0.2 collective-permute-start.6
  38.9 1.3 broadcast_select_fusion.1
  40.2 0.0 collective-permute-done.refs_1_
  40.2 0.0 collective-permute-done.1.refs_3_.refs_5_
  40.2 0.0 collective-permute-done.2.refs_4_.refs_6_
  40.2 5.7 %shard_map.46 = (f32[128,2048]{1,0:T(8,128)S(1)}, f32[128,2048]{1,0:T(8,128)S(1)}) custom-call(s32[1]{0:T(128)} %bitcast.2.core_ref, bf16[128,2048]{1,0:T(8,128)(2,1)S(1)} %dynamic-slice_bitcast_fusion.refs_0_, bf16[128,2048]{1,0:T(8,128)(2,1)S(1)} %collective-permute-done.refs_1_, bf16[1024,4096]{1,0:T(8,128)(2,1)} %refs_4_.1, ...), custom_call_target="tpu_custom_call" | custom-call | flops 2147483648 | bytes 12582912 | tf_op jit(solution)/shard_map/pallas_call | solution.py:97
  45.9 0.4 collective-permute-start.9
  46.3 0.1 fusion
  46.4 0.0 collective-permute-done.4.refs_1_
  46.4 0.0 collective-permute-done.6.refs_3_
  46.4 5.7 %shard_map.47 = (bf16[64,2048]{1,0:T(8,128)(2,1)S(1)}, bf16[64,2048]{1,0:T(8,128)(2,1)S(1)}, bf16[64,2048]{1,0:T(8,128)(2,1)S(1)}, bf16[64,2048]{1,0:T(8,128)(2,1)S(1)}) custom-call(s32[1]{0:T(128)} %bitcast.2.core_ref, bf16[64,2048]{1,0:T(8,128)(2,1)S(1)} %collective-permute-done.3.refs_0_, bf16[64,2048]{1,0:T(8,128)(2,1)S(1)} %collective-permute-done.4.refs_1_, ...), custom_call_target="tpu_custom_call" | custom-call | flops 2147483648 | bytes 12582912 | tf_op jit(solution)/shard_map/pallas_call | solution.py:97
  52.2 3.1 %collective-permute-start.7 = (bf16[64,2048]{1,0:T(8,128)(2,1)S(1)}, bf16[64,2048]{1,0:T(8,128)(2,1)S(1)}, u32[]{:S(2)}, u32[]{:S(2)}) collective-permute-start(bf16[64,2048]{1,0:T(8,128)(2,1)S(1)} %get-tuple-element.12), channel_id=1, source_target_pairs={{0,130},{1,131},{4,134},{5,135},{8,138},{9,139},{12,142},{13,143},... | collective-permute-start | bytes 786440 | tf_op jit(solution)/shard_map/ppermute | solution.py:45
  55.3 0.0 collective-permute-start.8
  55.3 3.2 %collective-permute-start.10 = (bf16[64,2048]{1,0:T(8,128)(2,1)S(1)}, bf16[64,2048]{1,0:T(8,128)(2,1)S(1)}, u32[]{:S(2)}, u32[]{:S(2)}) collective-permute-start(bf16[64,2048]{1,0:T(8,128)(2,1)S(1)} %get-tuple-element.15), channel_id=1, source_target_pairs={{0,131},{1,130},{4,135},{5,134},{8,139},{9,138},{12,143},{13,142},... | collective-permute-start | bytes 786440 | tf_op jit(solution)/shard_map/ppermute | solution.py:45
  58.5 0.0 collective-permute-start.11
  58.5 0.2 broadcast_select_fusion.3
  58.7 0.1 pad_maximum_fusion.refs_12_.refs_13_
  58.9 2.1 %collective-permute-done.7.refs_2_.refs_3_ = bf16[64,2048]{1,0:T(8,128)(2,1)S(1)} collective-permute-done((bf16[64,2048]{1,0:T(8,128)(2,1)S(1)}, bf16[64,2048]{1,0:T(8,128)(2,1)S(1)}, u32[]{:S(2)}, u32[]{:S(2)}) %collective-permute-start.7) | collective-permute-done | bytes 262176 | tf_op jit(solution)/shard_map/ppermute | solution.py:45
  61.0 3.1 %collective-permute-done.8.refs_4_.refs_5_ = bf16[64,2048]{1,0:T(8,128)(2,1)S(1)} collective-permute-done((bf16[64,2048]{1,0:T(8,128)(2,1)S(1)}, bf16[64,2048]{1,0:T(8,128)(2,1)S(1)}, u32[]{:S(2)}, u32[]{:S(2)}) %collective-permute-start.8) | collective-permute-done | bytes 262176 | tf_op jit(solution)/shard_map/ppermute | solution.py:45
  64.0 2.5 %collective-permute-done.10.refs_8_.refs_9_ = bf16[64,2048]{1,0:T(8,128)(2,1)S(1)} collective-permute-done((bf16[64,2048]{1,0:T(8,128)(2,1)S(1)}, bf16[64,2048]{1,0:T(8,128)(2,1)S(1)}, u32[]{:S(2)}, u32[]{:S(2)}) %collective-permute-start.10) | collective-permute-done | bytes 262176 | tf_op jit(solution)/shard_map/ppermute | solution.py:45
  66.6 3.6 %collective-permute-done.11.refs_10_.refs_11_ = bf16[64,2048]{1,0:T(8,128)(2,1)S(1)} collective-permute-done((bf16[64,2048]{1,0:T(8,128)(2,1)S(1)}, bf16[64,2048]{1,0:T(8,128)(2,1)S(1)}, u32[]{:S(2)}, u32[]{:S(2)}) %collective-permute-start.11) | collective-permute-done | bytes 262176 | tf_op jit(solution)/shard_map/ppermute | solution.py:45
  70.2 0.0 collective-permute-done.9.refs_6_.refs_7_
  70.2 7.7 %shard_map.48 = bf16[16,256,128]{2,1,0:T(8,128)(2,1)S(1)} custom-call(s32[1]{0:T(128)} %bitcast.2.core_ref, f32[128,2048]{1,0:T(8,128)S(1)} %get-tuple-element.11.refs_0_.refs_1_, f32[128,2048]{1,0:T(8,128)S(1)} %get-tuple-element.11.refs_0_.refs_1_, bf16[64,2048]{1,0:T(8,128)(2,1)S(1)} %collective-permute-done.7.refs_2_.refs_3_, ...), custom_call_target="tpu_custom_call" | custom-call | flops 268435456 | bytes 5242880 | tf_op jit(solution)/shard_map/pallas_call | solution.py:147
  77.9 0.0 all-to-all-done.decay_ref
  77.9 0.0 copy-start.2
  77.9 38.7 %all_to_all.15.update_ref = bf16[64,64,128]{2,1,0:T(8,128)(2,1)} all-to-all(bf16[64,64,128]{2,1,0:T(8,128)(2,1)S(1)} %bitcast.13), channel_id=1, replica_groups=mesh['seg'=64,'fsdp'=4] {'seg'}, dimensions={0} | all-to-all | bytes 2097152 | tf_op jit(solution)/shard_map/all_to_all | solution.py:229
  116.7 0.0 copy-done.2
  116.7 3.5 %shard_map.49 = bf16[64,64,128]{2,1,0:T(8,128)(2,1)} custom-call(f32[64,1,128]{2,1,0:T(1,128)} %copy-done.2, bf16[64,64,128]{2,1,0:T(8,128)(2,1)} %all_to_all.15.update_ref), custom_call_target="tpu_custom_call" | custom-call | flops 1048576 | bytes 2097152 | tf_op jit(solution)/shard_map/pallas_call | solution.py:178
  120.2 34.5 %all_to_all.16 = bf16[64,64,128]{2,1,0:T(8,128)(2,1)S(1)} all-to-all(bf16[64,64,128]{2,1,0:T(8,128)(2,1)} %shard_map.49), channel_id=1, replica_groups=mesh['seg'=64,'fsdp'=4] {'seg'}, dimensions={0} | all-to-all | bytes 2097152 | tf_op jit(solution)/shard_map/all_to_all | solution.py:231
  154.6 0.7 copy.5
  155.3 1.3 broadcast_in_dim_reshape.3
  (1 shorter events, 0.0 us)
Async XLA Ops:
  0.0 8.0 %copy-start.1 = (bf16[64,2048]{1,0:T(8,128)(2,1)S(1)}, bf16[64,2048]{1,0:T(8,128)(2,1)}, u32[]{:S(2)}) copy-start(bf16[64,2048]{1,0:T(8,128)(2,1)} %param.6) | copy-start | bytes 786436
  0.0 16.5 %copy-start = (bf16[1,128,4096]{2,1,0:T(8,128)(2,1)S(1)}, bf16[1,128,4096]{2,1,0:T(8,128)(2,1)}, u32[]{:S(2)}) copy-start(bf16[1,128,4096]{2,1,0:T(8,128)(2,1)} %param.4) | copy-start | bytes 3145732
  4.7 22.5 %copy-start.3 = (f32[1,2048]{1,0:T(1,128)S(1)}, f32[1,2048]{1,0:T(1,128)}, u32[]{:S(2)}) copy-start(f32[1,2048]{1,0:T(1,128)} %param.7) | copy-start | bytes 24580
  4.7 35.5 %collective-permute-start.1 = (bf16[1024,1024]{1,0:T(8,128)(2,1)}, bf16[1024,1024]{1,0:T(8,128)(2,1)S(1)}, u32[]{:S(2)}, u32[]{:S(2)}) collective-permute-start(bf16[1024,1024]{1,0:T(8,128)(2,1)} %get-tuple-element.18), channel_id=1, source_target_pairs={{0,1},{1,0},{4,5},{5,4},{8,9},{9,8},{12,13},{13,12},{16,17},{17,16... | collective-permute-start | bytes 6291464 | tf_op jit(solution)/shard_map/ppermute | solution.py:45
  8.0 32.2 %collective-permute-start.2 = (bf16[1024,1024]{1,0:T(8,128)(2,1)}, bf16[1024,1024]{1,0:T(8,128)(2,1)}, u32[]{:S(2)}, u32[]{:S(2)}) collective-permute-start(bf16[1024,1024]{1,0:T(8,128)(2,1)} %get-tuple-element.17), channel_id=1, source_target_pairs={{0,1},{1,0},{4,5},{5,4},{8,9},{9,8},{12,13},{13,12},{16,17},{17,16... | collective-permute-start | bytes 6291464 | tf_op jit(solution)/shard_map/ppermute | solution.py:45
  8.0 5.8 %collective-permute-start.12 = (bf16[32,2048]{1,0:T(8,128)(2,1)S(1)}, bf16[32,2048]{1,0:T(8,128)(2,1)S(1)}, u32[]{:S(2)}, u32[]{:S(2)}) collective-permute-start(bf16[32,2048]{1,0:T(8,128)(2,1)S(1)} %get-tuple-element.30), channel_id=1, source_target_pairs={{0,2},{1,3},{4,6},{5,7},{8,10},{9,11},{12,14},{13,15},{16,18},{17,... | collective-permute-start | bytes 393224 | tf_op jit(solution)/shard_map/ppermute | solution.py:45
  8.1 6.4 %collective-permute-start.13 = (bf16[32,2048]{1,0:T(8,128)(2,1)S(1)}, bf16[32,2048]{1,0:T(8,128)(2,1)S(1)}, u32[]{:S(2)}, u32[]{:S(2)}) collective-permute-start(bf16[32,2048]{1,0:T(8,128)(2,1)S(1)} %get-tuple-element.29), channel_id=1, source_target_pairs={{0,130},{1,131},{4,134},{5,135},{8,138},{9,139},{12,142},{13,143},... | collective-permute-start | bytes 393224 | tf_op jit(solution)/shard_map/ppermute | solution.py:45
  15.2 23.5 %collective-permute-start.14 = (bf16[128,2048]{1,0:T(8,128)(2,1)}, bf16[128,2048]{1,0:T(8,128)(2,1)}, u32[]{:S(2)}, u32[]{:S(2)}) collective-permute-start(bf16[128,2048]{1,0:T(8,128)(2,1)} %constant_dynamic-update-slice_fusion), channel_id=1, source_target_pairs={{0,1},{1,0},{4,5},{5,4},{8,9},{9,8},{12,13},{13,12},{16,17},{17,16... | collective-permute-start | bytes 1572872 | tf_op jit(solution)/shard_map/ppermute | solution.py:45
  17.3 9.1 %collective-permute-start.3 = (bf16[64,2048]{1,0:T(8,128)(2,1)S(1)}, bf16[64,2048]{1,0:T(8,128)(2,1)S(1)}, u32[]{:S(2)}, u32[]{:S(2)}) collective-permute-start(bf16[64,2048]{1,0:T(8,128)(2,1)S(1)} %get-tuple-element.24), channel_id=1, source_target_pairs={{0,2},{1,3},{4,6},{5,7},{8,10},{9,11},{12,14},{13,15},{16,18},{17,... | collective-permute-start | bytes 786440 | tf_op jit(solution)/shard_map/ppermute | solution.py:45
  17.3 21.0 %collective-permute-start.5 = (bf16[64,2048]{1,0:T(8,128)(2,1)}, bf16[64,2048]{1,0:T(8,128)(2,1)}, u32[]{:S(2)}, u32[]{:S(2)}) collective-permute-start(bf16[64,2048]{1,0:T(8,128)(2,1)} %get-tuple-element.23), channel_id=1, source_target_pairs={{0,130},{1,131},{4,134},{5,135},{8,138},{9,139},{12,142},{13,143},... | collective-permute-start | bytes 786440 | tf_op jit(solution)/shard_map/ppermute | solution.py:45
  26.4 13.8 %collective-permute-start = (bf16[128,2048]{1,0:T(8,128)(2,1)S(1)}, bf16[128,2048]{1,0:T(8,128)(2,1)S(1)}, u32[]{:S(2)}, u32[]{:S(2)}) collective-permute-start(bf16[128,2048]{1,0:T(8,128)(2,1)S(1)} %dynamic-slice_bitcast_fusion.refs_0_), channel_id=1, source_target_pairs={{0,1},{1,0},{4,5},{5,4},{8,9},{9,8},{12,13},{13,12},{16,17},{17,16... | collective-permute-start | bytes 1572872 | tf_op jit(solution)/shard_map/ppermute | solution.py:45
  27.8 50.1 %all-to-all-start = ((f32[64,1,128]{2,1,0:T(1,128)}), f32[64,1,128]{2,1,0:T(1,128)S(1)}, u32[]{:S(2)}, u32[]{:S(2)}) async-start(f32[64,1,128]{2,1,0:T(1,128)} %bitcast.1), calls=%async_computation | async-start | bytes 65536 | tf_op jit(solution)/shard_map/all_to_all | solution.py:218
  38.3 8.1 %collective-permute-start.4 = (bf16[64,2048]{1,0:T(8,128)(2,1)S(1)}, bf16[64,2048]{1,0:T(8,128)(2,1)S(1)}, u32[]{:S(2)}, u32[]{:S(2)}) collective-permute-start(bf16[64,2048]{1,0:T(8,128)(2,1)S(1)} %collective-permute-done.3.refs_0_), channel_id=1, source_target_pairs={{0,1},{1,0},{4,5},{5,4},{8,9},{9,8},{12,13},{13,12},{16,17},{17,16... | collective-permute-start | bytes 786440 | tf_op jit(solution)/shard_map/ppermute | solution.py:45
  38.7 7.7 %collective-permute-start.6 = (bf16[64,2048]{1,0:T(8,128)(2,1)}, bf16[64,2048]{1,0:T(8,128)(2,1)S(1)}, u32[]{:S(2)}, u32[]{:S(2)}) collective-permute-start(bf16[64,2048]{1,0:T(8,128)(2,1)} %collective-permute-done.5.refs_2_), channel_id=1, source_target_pairs={{0,1},{1,0},{4,5},{5,4},{8,9},{9,8},{12,13},{13,12},{16,17},{17,16... | collective-permute-start | bytes 786440 | tf_op jit(solution)/shard_map/ppermute | solution.py:45
  45.9 24.2 %collective-permute-start.9 = (f32[128,2048]{1,0:T(8,128)S(1)}, f32[128,2048]{1,0:T(8,128)S(1)}, u32[]{:S(2)}, u32[]{:S(2)}) collective-permute-start(f32[128,2048]{1,0:T(8,128)S(1)} %get-tuple-element.14), channel_id=1, source_target_pairs={{0,1},{1,0},{4,5},{5,4},{8,9},{9,8},{12,13},{13,12},{16,17},{17,16... | collective-permute-start | bytes 3145736 | tf_op jit(solution)/shard_map/ppermute | solution.py:45
  52.2 8.8 %collective-permute-start.7 = (bf16[64,2048]{1,0:T(8,128)(2,1)S(1)}, bf16[64,2048]{1,0:T(8,128)(2,1)S(1)}, u32[]{:S(2)}, u32[]{:S(2)}) collective-permute-start(bf16[64,2048]{1,0:T(8,128)(2,1)S(1)} %get-tuple-element.12), channel_id=1, source_target_pairs={{0,130},{1,131},{4,134},{5,135},{8,138},{9,139},{12,142},{13,143},... | collective-permute-start | bytes 786440 | tf_op jit(solution)/shard_map/ppermute | solution.py:45
  55.3 8.7 %collective-permute-start.8 = (bf16[64,2048]{1,0:T(8,128)(2,1)S(1)}, bf16[64,2048]{1,0:T(8,128)(2,1)S(1)}, u32[]{:S(2)}, u32[]{:S(2)}) collective-permute-start(bf16[64,2048]{1,0:T(8,128)(2,1)S(1)} %get-tuple-element.13), channel_id=1, source_target_pairs={{0,2},{1,3},{4,6},{5,7},{8,10},{9,11},{12,14},{13,15},{16,18},{17,... | collective-permute-start | bytes 786440 | tf_op jit(solution)/shard_map/ppermute | solution.py:45
  55.3 11.3 %collective-permute-start.10 = (bf16[64,2048]{1,0:T(8,128)(2,1)S(1)}, bf16[64,2048]{1,0:T(8,128)(2,1)S(1)}, u32[]{:S(2)}, u32[]{:S(2)}) collective-permute-start(bf16[64,2048]{1,0:T(8,128)(2,1)S(1)} %get-tuple-element.15), channel_id=1, source_target_pairs={{0,131},{1,130},{4,135},{5,134},{8,139},{9,138},{12,143},{13,142},... | collective-permute-start | bytes 786440 | tf_op jit(solution)/shard_map/ppermute | solution.py:45
  58.5 11.7 %collective-permute-start.11 = (bf16[64,2048]{1,0:T(8,128)(2,1)S(1)}, bf16[64,2048]{1,0:T(8,128)(2,1)S(1)}, u32[]{:S(2)}, u32[]{:S(2)}) collective-permute-start(bf16[64,2048]{1,0:T(8,128)(2,1)S(1)} %get-tuple-element.16), channel_id=1, source_target_pairs={{0,3},{1,2},{4,7},{5,6},{8,11},{9,10},{12,15},{13,14},{16,19},{17,... | collective-permute-start | bytes 786440 | tf_op jit(solution)/shard_map/ppermute | solution.py:45
  77.9 38.8 %copy-start.2 = (f32[64,1,128]{2,1,0:T(1,128)}, f32[64,1,128]{2,1,0:T(1,128)S(1)}, u32[]{:S(2)}) copy-start(f32[64,1,128]{2,1,0:T(1,128)S(1)} %all-to-all-done.decay_ref) | copy-start | bytes 98308

commit v2 on v0

v2 whole, which is shorter than its diff:
```python
import functools
import math

import jax
import jax.numpy as jnp
from jax import lax
from jax.experimental import pallas as pl
from jax.experimental.pallas import tpu as pltpu
from jax.sharding import PartitionSpec as P

HEADS = 16
HS = 128
S = 256
SEG = 64
TOK = 128
D = 4096
HD = 2048
QUARTER = D // 4
HALF = HD // 2
BOTH = ("seg", "fsdp")
BF = jnp.bfloat16
F32 = jnp.float32


def flat(y, x, z, core):
    return (((y // 2) * 4 + x) * 8 + z) * 4 + (y % 2) * 2 + core


def moves(dy, dc):
    pairs = []
    for y in range(4):
        for x in range(4):
            for z in range(8):
                for core in range(2):
                    pairs.append((flat(y, x, z, core), flat((y + dy) % 4, x, z, (core + dc) % 2)))
    return pairs


UP, DOWN, SIB = moves(1, 0), moves(-1, 0), moves(0, 1)


def send(value, pairs):
    return lax.ppermute(value, BOTH, pairs)


TILE = 256
WIDE = 2 * QUARTER
PART = TOK // 2
Q_ROWS = S // 4
BLOCK = S // 4
GATE_ROWS = 8

ANY = pl.BlockSpec(memory_space=pl.ANY)
HBM = pl.BlockSpec(memory_space=pltpu.HBM)
VMEM = pl.BlockSpec(memory_space=pltpu.VMEM)


def here(value):
    return pltpu.with_memory_space_constraint(value, pltpu.VMEM)


def far_away(value):
    return pltpu.with_memory_space_constraint(value, pltpu.HBM)


def position():
    fsdp = lax.axis_index("fsdp")
    return fsdp % 2, fsdp // 2


def half_of(which, size):
    return pl.ds(pl.multiple_of(which * size, size), size)


def run_copies(pairs, sems):
    todo = [pltpu.make_async_copy(a, b, sems.at[i]) for i, (a, b) in enumerate(pairs)]
    for c in todo:
        c.start()
    for c in todo:
        c.wait()


PARAMS = pltpu.CompilerParams(vmem_limit_bytes=8 << 20)


def cost(flops, nbytes, exps=0):
    return pl.CostEstimate(flops=flops, bytes_accessed=nbytes, transcendentals=exps)


CUT_ROWS = 256


def cut_pairs(w_ref, out_ref, half):
    pairs = []
    for v in range(2):
        cols = pl.ds(pl.multiple_of(v * HD + half * HALF, HALF), HALF)
        for r in range(0, QUARTER, CUT_ROWS):
            rows = slice(r, r + CUT_ROWS)
            pairs.append((w_ref.at[rows, cols], out_ref.at[rows, v * HALF : (v + 1) * HALF]))
    return pairs


CUT_COPIES = 2 * QUARTER // CUT_ROWS


def sort_kernel(tokens_ref, q_ref, w_ref, up_ref, down_ref, sib_ref, w_out, sems):
    core, y_lo = position()
    home, away = half_of(y_lo, WIDE), half_of(1 - y_lo, WIDE)
    run_copies(
        [
            (tokens_ref.at[:PART, away], up_ref),
            (tokens_ref.at[PART:, away], down_ref),
            (tokens_ref.at[:PART, home], sib_ref.at[:PART]),
            (tokens_ref.at[PART:, home], sib_ref.at[PART:TOK]),
            (q_ref, sib_ref.at[TOK:]),
        ]
        + cut_pairs(w_ref, w_out, 1 - core),
        sems,
    )


def sort_inputs(tokens, q, w):
    shapes = [(PART, WIDE), (PART, WIDE), (TOK + Q_ROWS, WIDE), (QUARTER, HD)]
    return pl.pallas_call(
        sort_kernel,
        in_specs=[HBM] * 3,
        out_specs=[VMEM] * 4,
        out_shape=[pltpu.VMEM(shape, BF) for shape in shapes],
        scratch_shapes=[pltpu.SemaphoreType.DMA((5 + CUT_COPIES,))],
        compiler_params=PARAMS,
        cost_estimate=cost(0, 12 << 20),
    )(far_away(tokens), far_away(q), far_away(w))


def project_kernel(*refs, rows, extra):
    n = len(rows)
    pieces, w_ref, sib_ref, outs = refs[:n], refs[n], refs[n + 1], refs[n + 2 + extra : n + 4 + extra]
    x_ref, own_w, own_sems, x_sems = refs[n + 4 + extra :]
    core, _ = position()
    pairs, start = [], 0
    for piece, count in zip(pieces, rows):
        pairs.append((piece.at[:count], x_ref.at[start : start + count]))
        start += count
    half = start // 2
    for ref, out in zip(refs[n + 2 : n + 2 + extra], outs):
        for i in range(2):
            block = slice(TOK + i * Q_ROWS // 2, TOK + (i + 1) * Q_ROWS // 2)
            pairs.append((ref.at[block, half_of(core, HALF)], out.at[half:, i * HALF : (i + 1) * HALF]))
    x_copies = [pltpu.make_async_copy(a, b, x_sems.at[i]) for i, (a, b) in enumerate(pairs)]
    own_copies = [pltpu.make_async_copy(a, b, own_sems.at[i]) for i, (a, b) in enumerate(cut_pairs(w_ref, own_w, core))]
    for copy in x_copies[:n]:
        copy.start()
    for copy in own_copies:
        copy.start()
    for copy in x_copies[n:]:
        copy.start()
    for copy in x_copies[:n]:
        copy.wait()
    x_own, x_other = x_ref[:, half_of(core, QUARTER)], x_ref[:, half_of(1 - core, QUARTER)]
    for v in range(2):
        cols = slice(v * HALF, (v + 1) * HALF)
        mine = slice(v * CUT_COPIES // 2, (v + 1) * CUT_COPIES // 2)
        total = jnp.dot(x_other, sib_ref[:, cols], preferred_element_type=F32)
        for copy in own_copies[mine]:
            copy.wait()
        total += jnp.dot(x_own, own_w[:, cols], preferred_element_type=F32)
        for i, out in enumerate(outs):
            out[:half, cols] = total[i * half : (i + 1) * half].astype(out.dtype)
    for copy in x_copies[n:]:
        copy.wait()


def project(pieces, w, sib_w, dtype, queries=()):
    rows = [count for _, count in pieces]
    total = sum(rows)
    height = total // 2 + (Q_ROWS // 2 if queries else 0)
    args = [p for p, _ in pieces] + [far_away(w), sib_w, *queries]
    return pl.pallas_call(
        functools.partial(project_kernel, rows=rows, extra=len(queries)),
        in_specs=[ANY] * len(pieces) + [HBM, VMEM] + [ANY] * len(queries),
        out_specs=[VMEM] * 2,
        out_shape=[pltpu.VMEM((height, HD), dtype) for _ in range(2)],
        scratch_shapes=[
            pltpu.VMEM((total, WIDE), BF),
            pltpu.VMEM((QUARTER, HD), BF),
            pltpu.SemaphoreType.DMA((CUT_COPIES,)),
            pltpu.SemaphoreType.DMA((len(pieces) + 4,)),
        ],
        compiler_params=pltpu.CompilerParams(vmem_limit_bytes=14 << 20),
        cost_estimate=cost(2 * total * WIDE * HD, 4 * WIDE * HD),
    )(*args)


def one_head(q, k, v):
    scores = lax.dot_general(q, k, (((1,), (1,)), ((), ())), preferred_element_type=F32) * (1.0 / math.sqrt(HS))
    scores = jnp.exp(scores - jnp.max(scores, axis=1, keepdims=True))
    weights = (scores / jnp.sum(scores, axis=1, keepdims=True)).astype(BF)
    return jnp.dot(weights, v, preferred_element_type=F32).astype(BF)


def attend_kernel(near0, near1, low_ref, up_ref, own_ref, sib_ref, gate_ref, out_ref):
    core, y_lo = position()
    place = y_lo * 2 + core
    for head in range(HEADS // 2):
        q_cols = pl.ds(pl.multiple_of(core * HALF + head * HS, HS), HS)
        k_cols, v_cols = slice(head * HS, (head + 1) * HS), slice(HALF + head * HS, HALF + (head + 1) * HS)
        parts = [own_ref[TOK:, q_cols], sib_ref[TOK:, q_cols]]
        for ref in (up_ref, low_ref):
            parts += [ref[TOK:, k_cols], ref[TOK:, v_cols]]
        q = jnp.concatenate(parts, axis=0)
        gate = gate_ref[:, q_cols]
        terms = []
        for _ in range(3):
            terms.append(gate.astype(BF))
            gate = gate - terms[-1].astype(F32)
        gate = jnp.concatenate([t.astype(F32) for t in terms] + [jnp.zeros((GATE_ROWS - 3, HS), F32)], axis=0).astype(BF)
        for batch, near in enumerate((near0, near1)):
            rows = slice(batch * PART, (batch + 1) * PART)

            def total(cols):
                far = jnp.concatenate([low_ref[rows, cols], up_ref[rows, cols]], axis=0)
                return (near[:, cols] + far.astype(F32)).astype(BF)

            update = one_head(q, total(k_cols), total(v_cols))
            for i in range(S // BLOCK):
                at = (batch * (HEADS // 2) + head) * (S // BLOCK) + (place ^ i)
                out_ref[at, :BLOCK] = update[i * BLOCK : (i + 1) * BLOCK]
                out_ref[at, BLOCK:] = gate


def attend(near, far, queries, gate):
    args = [*near, *far, *queries, gate]
    return pl.pallas_call(
        attend_kernel,
        in_specs=[VMEM] * len(args),
        out_specs=VMEM,
        out_shape=pltpu.VMEM((SEG, BLOCK + GATE_ROWS, HS), BF),
        compiler_params=PARAMS,
        cost_estimate=cost(8 * HEADS // 2 * S * TOK * HS, 6 << 20, HEADS * S * TOK),
    )(*args)


def scan_kernel(update_ref, out_ref):
    def step(i, carry):
        terms = update_ref[i, BLOCK:].astype(F32)
        gate = terms[0:1] + terms[1:2] + terms[2:3]
        carry = gate * carry + update_ref[i, :BLOCK].astype(F32)
        out_ref[i] = carry.astype(BF)
        return carry

    lax.fori_loop(0, SEG, step, jnp.zeros((BLOCK, HS), F32), unroll=8)


def scan(update):
    return pl.pallas_call(
        scan_kernel,
        in_specs=[VMEM],
        out_specs=VMEM,
        out_shape=pltpu.VMEM((SEG, BLOCK, HS), BF),
        compiler_params=PARAMS,
        cost_estimate=cost(2 * SEG * BLOCK * HS, 4 * SEG * BLOCK * HS),
    )(here(update))


def place_kernel(own_ref, other_ref, out_ref, sems):
    core, _ = position()
    pairs = []
    for batch, (ref, half) in enumerate(((own_ref, core), (other_ref, 1 - core))):
        for j in range(HEADS // 2):
            cols = pl.ds(pl.multiple_of(half * HALF + j * HS, HS), HS)
            pairs.append((ref.at[batch, j], out_ref.at[:, cols]))
    run_copies(pairs, sems)


def place(own, other):
    return pl.pallas_call(
        place_kernel,
        in_specs=[VMEM, VMEM],
        out_specs=ANY,
        out_shape=jax.ShapeDtypeStruct((S, HD), BF),
        scratch_shapes=[pltpu.SemaphoreType.DMA((HEADS,))],
        compiler_params=PARAMS,
        cost_estimate=cost(0, 4 * S * HD),
    )(here(own), here(other))


def spread(value):
    return lax.all_to_all(value, "seg", 0, 0, tiled=True)


def body(tokens, w_kv, q_state, decay):
    to_up, to_down, to_sib, to_sib_w = sort_inputs(tokens[0], q_state, w_kv)
    low, up, sib, sib_w = send(to_up, UP), send(to_down, DOWN), send(to_sib, SIB), send(to_sib_w, SIB)
    low_sib, up_sib = send(low, SIB), send(up, SIB)

    away = [(part, PART) for part in (low, low_sib, up, up_sib)]
    lower, upper = project(away, w_kv, sib_w, BF, (sib, to_sib))
    far = send(lower, DOWN), send(upper, UP)
    near = project([(to_sib, TOK), (sib, TOK)], w_kv, sib_w, F32)
    states = spread(scan(spread(attend(near, far, (to_sib, sib), decay))))
    other = send(states, SIB)
    shape = (2, HEADS // 2, S, HS)
    return place(states.reshape(shape), other.reshape(shape))[None, None]


def solution(mesh):
    return jax.shard_map(
        body,
        mesh=mesh,
        in_specs=(P("fsdp", "seg", None), P("fsdp", None), P("fsdp", None), P("seg", None)),
        out_specs=P("fsdp", "seg", None, None),
        check_vma=False,
    )
```

time: 1730 us -> 125 us (0.07)
  waiting for transfers between devices: 1250 us -> 22.3 us
  other arithmetic: 224 us -> 0 us
  blocking collectives: 160 us -> 73.3 us
  local copies, waits for them, and re-layouts: 63.9 us -> 0.01 us
    all_gather x3 -> x0, waiting for transfers between devices: 1250 us -> none  [the longest x1 922 us: entering(): everything = jax.tree.map(lambda part: lax.all_gather(part, axis), value)]
    select_n x64 -> x0, other arithmetic: 220 us -> none  [hop(): return jax.tree.map(lambda a, b: jnp.where(reached, a, b), new, before)]
    all_gather x1 -> x0, blocking collectives: 160 us -> none  [entering(): everything = jax.tree.map(lambda part: lax.all_gather(part, axis), value)]
    all_to_all x0 -> x2, blocking collectives: none -> 73.3 us  [spread(): return lax.all_to_all(value, 'seg', 0, 0, tiled=True)]
    dynamic_slice x64 -> x0, local copies, waits for them, and re-layouts: 54.5 us -> none  [hop(): new = combine(before, jax.tree.map(lambda part: part[k], everything))]
    ppermute x0 -> x9, waiting for transfers between devices: none -> 22.3 us  [send(): return lax.ppermute(value, BOTH, pairs)]
  transfers between devices with their start and end apart: 3 -> 9, of which waited for: 3 -> 6; matrix products, arithmetic and copies ran while one was open for 0% -> 0% of each run, Pallas kernels for 0% -> 3%
where the time goes in v2:
time: 125 us
  blocking collectives  73.3 us (59%)
  waiting for transfers between devices  22.3 us (18%)
  starting transfers between devices  14.7 us (12%)
  Pallas kernels  14.5 us (12%)
    all_to_all x2, blocking collectives, spread(): return lax.all_to_all(value, 'seg', 0, 0, tiled=True)  73.3 us
    ppermute x9, waiting for transfers between devices, send(): return lax.ppermute(value, BOTH, pairs)  22.3 us
    ppermute x9, starting transfers between devices, send(): return lax.ppermute(value, BOTH, pairs)  14.7 us
    pallas_call x2, Pallas kernels, project(): pl.pallas_call(functools.partial(project_kernel, rows=rows, extra=len(que...  8.73 us
    pallas_call x1, Pallas kernels, sort_inputs(): pl.pallas_call(sort_kernel, in_specs=[HBM] * 3, out_specs=[VMEM] * 4, out...  2.67 us
  transfers between devices with their start and end apart: 9, of which 6 were waited for; matrix products, arithmetic and copies ran while one was open for 0% of the time, Pallas kernels for 3%

profile of v2, /device:TPU:1, one launch (start us, length us, event | category | flops | bytes accessed | tf_op | source)
XLA Modules:
  0.0 124.9 jit_solution(6344786651530642966)
XLA Ops:
  0.0 2.7 %shard_map.46 = (bf16[64,2048]{1,0:T(8,128)(2,1)S(1)}, bf16[64,2048]{1,0:T(8,128)(2,1)S(1)}, bf16[192,2048]{1,0:T(8,128)(2,1)S(1)}, bf16[1024,2048]{1,0:T(8,128)(2,1)S(1)}) custom-call(bf16[128,4096]{1,0:T(8,128)(2,1)} %bitcast.6, bf16[64,2048]{1,0:T(8,128)(2,1)} %q_ref.1, bf16[1024,4096]{1,0:T(8,128)(2,1)} %refs_4_.1), custom_call_target="tpu_custom_call" | custom-call | bytes 12582912 | tf_op jit(solution)/shard_map/pallas_call | solution.py:124
  2.7 3.3 %collective-permute-start.1 = (bf16[1024,2048]{1,0:T(8,128)(2,1)S(1)}, bf16[1024,2048]{1,0:T(8,128)(2,1)S(1)}, u32[]{:S(2)}, u32[]{:S(2)}) collective-permute-start(bf16[1024,2048]{1,0:T(8,128)(2,1)S(1)} %get-tuple-element.14), channel_id=1, source_target_pairs={{0,1},{1,0},{4,5},{5,4},{8,9},{9,8},{12,13},{13,12},{16,17},{17,16... | collective-permute-start | bytes 12582920 | tf_op jit(solution)/shard_map/ppermute | solution.py:43
  6.0 0.1 collective-permute-start
  6.1 0.0 collective-permute-start.2
  6.1 2.7 %collective-permute-start.4 = (bf16[64,2048]{1,0:T(8,128)(2,1)S(1)}, bf16[64,2048]{1,0:T(8,128)(2,1)S(1)}, u32[]{:S(2)}, u32[]{:S(2)}) collective-permute-start(bf16[64,2048]{1,0:T(8,128)(2,1)S(1)} %get-tuple-element.18), channel_id=1, source_target_pairs={{0,130},{1,131},{4,134},{5,135},{8,138},{9,139},{12,142},{13,143},... | collective-permute-start | bytes 786440 | tf_op jit(solution)/shard_map/ppermute | solution.py:43
  8.8 6.0 %collective-permute-done.2.refs_0_ = bf16[64,2048]{1,0:T(8,128)(2,1)S(1)} collective-permute-done((bf16[64,2048]{1,0:T(8,128)(2,1)S(1)}, bf16[64,2048]{1,0:T(8,128)(2,1)S(1)}, u32[]{:S(2)}, u32[]{:S(2)}) %collective-permute-start.2) | collective-permute-done | bytes 262176 | tf_op jit(solution)/shard_map/ppermute | solution.py:43
  14.8 1.2 collective-permute-start.3
  16.0 0.0 collective-permute-done.4.refs_2_
  16.0 0.0 collective-permute-start.5
  16.0 1.2 collective-permute-done.3.refs_1_
  17.2 0.4 collective-permute-done.5.refs_3_
  17.6 0.0 collective-permute-done.refs_1_.refs_6_.sib_ref
  17.6 0.0 collective-permute-done.1.refs_3_.refs_5_
  17.6 4.4 %shard_map.48 = (bf16[160,2048]{1,0:T(8,128)(2,1)S(1)}, bf16[160,2048]{1,0:T(8,128)(2,1)S(1)}) custom-call(bf16[64,2048]{1,0:T(8,128)(2,1)S(1)} %collective-permute-done.2.refs_0_, bf16[64,2048]{1,0:T(8,128)(2,1)S(1)} %collective-permute-done.3.refs_1_, bf16[64,2048]{1,0:T(8,128)(2,1)S(1)} %collective-permute-done.4.refs_2_, ...), custom_call_target="tpu_custom_call" | custom-call | flops 2147483648 | bytes 16777216 | tf_op jit(solution)/shard_map/pallas_call | solution.py:178
  22.0 2.4 %collective-permute-start.6 = (bf16[160,2048]{1,0:T(8,128)(2,1)S(1)}, bf16[160,2048]{1,0:T(8,128)(2,1)S(1)}, u32[]{:S(2)}, u32[]{:S(2)}) collective-permute-start(bf16[160,2048]{1,0:T(8,128)(2,1)S(1)} %get-tuple-element.19), channel_id=1, source_target_pairs={{0,130},{1,131},{4,134},{5,135},{8,138},{9,139},{12,142},{13,143},... | collective-permute-start | bytes 1966088 | tf_op jit(solution)/shard_map/ppermute | solution.py:43
  24.4 0.0 copy-start
  24.4 0.0 collective-permute-start.7
  24.4 4.4 %shard_map.47 = (f32[128,2048]{1,0:T(8,128)S(1)}, f32[128,2048]{1,0:T(8,128)S(1)}) custom-call(bf16[192,2048]{1,0:T(8,128)(2,1)S(1)} %get-tuple-element.13.refs_0_.refs_7_.own_ref, bf16[192,2048]{1,0:T(8,128)(2,1)S(1)} %collective-permute-done.refs_1_.refs_6_.sib_ref, bf16[1024,4096]{1,0:T(8,128)(2,1)} %refs_4_.1, ...), custom_call_target="tpu_custom_call" | custom-call | flops 2147483648 | bytes 16777216 | tf_op jit(solution)/shard_map/pallas_call | solution.py:178
  28.7 9.4 %collective-permute-done.6.low_ref = bf16[160,2048]{1,0:T(8,128)(2,1)S(1)} collective-permute-done((bf16[160,2048]{1,0:T(8,128)(2,1)S(1)}, bf16[160,2048]{1,0:T(8,128)(2,1)S(1)}, u32[]{:S(2)}, u32[]{:S(2)}) %collective-permute-start.6) | collective-permute-done | bytes 655392 | tf_op jit(solution)/shard_map/ppermute | solution.py:43
  38.1 3.1 %collective-permute-done.7.up_ref = bf16[160,2048]{1,0:T(8,128)(2,1)S(1)} collective-permute-done((bf16[160,2048]{1,0:T(8,128)(2,1)S(1)}, bf16[160,2048]{1,0:T(8,128)(2,1)S(1)}, u32[]{:S(2)}, u32[]{:S(2)}) %collective-permute-start.7) | collective-permute-done | bytes 655392 | tf_op jit(solution)/shard_map/ppermute | solution.py:43
  41.2 0.0 copy-done
  41.2 1.7 %shard_map.49 = bf16[64,72,128]{2,1,0:T(8,128)(2,1)S(1)} custom-call(f32[128,2048]{1,0:T(8,128)S(1)} %get-tuple-element.15.near0, f32[128,2048]{1,0:T(8,128)S(1)} %get-tuple-element.16.near1, bf16[160,2048]{1,0:T(8,128)(2,1)S(1)} %collective-permute-done.6.low_ref, bf16[160,2048]{1,0:T(8,128)(2,1)S(1)} %collective-permute-done.7.up_ref, ...), custom_call_target="tpu_custom_call" | custom-call | flops 268435456 | bytes 6291456 | tf_op jit(solution)/shard_map/pallas_call | solution.py:233
  42.9 39.3 %all_to_all.10.update_ref = bf16[64,72,128]{2,1,0:T(8,128)(2,1)S(1)} all-to-all(bf16[64,72,128]{2,1,0:T(8,128)(2,1)S(1)} %shard_map.49), channel_id=1, replica_groups=mesh['seg'=64,'fsdp'=4] {'seg'}, dimensions={0} | all-to-all | bytes 2359296 | tf_op jit(solution)/shard_map/all_to_all | solution.py:288
  82.3 0.3 shard_map.50
  82.6 34.0 %all_to_all.11 = bf16[64,64,128]{2,1,0:T(8,128)(2,1)S(1)} all-to-all(bf16[64,64,128]{2,1,0:T(8,128)(2,1)S(1)} %shard_map.50), channel_id=1, replica_groups=mesh['seg'=64,'fsdp'=4] {'seg'}, dimensions={0} | all-to-all | bytes 2097152 | tf_op jit(solution)/shard_map/all_to_all | solution.py:288
  116.6 4.9 %collective-permute-start.8 = (bf16[64,64,128]{2,1,0:T(8,128)(2,1)S(1)}, bf16[64,64,128]{2,1,0:T(8,128)(2,1)S(1)}, u32[]{:S(2)}, u32[]{:S(2)}) collective-permute-start(bf16[64,64,128]{2,1,0:T(8,128)(2,1)S(1)} %all_to_all.11), channel_id=1, source_target_pairs={{0,1},{1,0},{4,5},{5,4},{8,9},{9,8},{12,13},{13,12},{16,17},{17,16... | collective-permute-start | bytes 3145736 | tf_op jit(solution)/shard_map/ppermute | solution.py:43
  121.5 2.3 %collective-permute-done.8 = bf16[64,64,128]{2,1,0:T(8,128)(2,1)S(1)} collective-permute-done((bf16[64,64,128]{2,1,0:T(8,128)(2,1)S(1)}, bf16[64,64,128]{2,1,0:T(8,128)(2,1)S(1)}, u32[]{:S(2)}, u32[]{:S(2)}) %collective-permute-start.8) | collective-permute-done | bytes 1048608 | tf_op jit(solution)/shard_map/ppermute | solution.py:43
  123.8 1.1 shard_map.51
Async XLA Ops:
  2.7 14.9 %collective-permute-start.1 = (bf16[1024,2048]{1,0:T(8,128)(2,1)S(1)}, bf16[1024,2048]{1,0:T(8,128)(2,1)S(1)}, u32[]{:S(2)}, u32[]{:S(2)}) collective-permute-start(bf16[1024,2048]{1,0:T(8,128)(2,1)S(1)} %get-tuple-element.14), channel_id=1, source_target_pairs={{0,1},{1,0},{4,5},{5,4},{8,9},{9,8},{12,13},{13,12},{16,17},{17,16... | collective-permute-start | bytes 12582920 | tf_op jit(solution)/shard_map/ppermute | solution.py:43
  6.0 11.6 %collective-permute-start = (bf16[192,2048]{1,0:T(8,128)(2,1)S(1)}, bf16[192,2048]{1,0:T(8,128)(2,1)S(1)}, u32[]{:S(2)}, u32[]{:S(2)}) collective-permute-start(bf16[192,2048]{1,0:T(8,128)(2,1)S(1)} %get-tuple-element.13.refs_0_.refs_7_.own_ref), channel_id=1, source_target_pairs={{0,1},{1,0},{4,5},{5,4},{8,9},{9,8},{12,13},{13,12},{16,17},{17,16... | collective-permute-start | bytes 2359304 | tf_op jit(solution)/shard_map/ppermute | solution.py:43
  6.1 8.7 %collective-permute-start.2 = (bf16[64,2048]{1,0:T(8,128)(2,1)S(1)}, bf16[64,2048]{1,0:T(8,128)(2,1)S(1)}, u32[]{:S(2)}, u32[]{:S(2)}) collective-permute-start(bf16[64,2048]{1,0:T(8,128)(2,1)S(1)} %get-tuple-element.17), channel_id=1, source_target_pairs={{0,2},{1,3},{4,6},{5,7},{8,10},{9,11},{12,14},{13,15},{16,18},{17,... | collective-permute-start | bytes 786440 | tf_op jit(solution)/shard_map/ppermute | solution.py:43
  6.1 9.9 %collective-permute-start.4 = (bf16[64,2048]{1,0:T(8,128)(2,1)S(1)}, bf16[64,2048]{1,0:T(8,128)(2,1)S(1)}, u32[]{:S(2)}, u32[]{:S(2)}) collective-permute-start(bf16[64,2048]{1,0:T(8,128)(2,1)S(1)} %get-tuple-element.18), channel_id=1, source_target_pairs={{0,130},{1,131},{4,134},{5,135},{8,138},{9,139},{12,142},{13,143},... | collective-permute-start | bytes 786440 | tf_op jit(solution)/shard_map/ppermute | solution.py:43
  14.8 2.4 %collective-permute-start.3 = (bf16[64,2048]{1,0:T(8,128)(2,1)S(1)}, bf16[64,2048]{1,0:T(8,128)(2,1)S(1)}, u32[]{:S(2)}, u32[]{:S(2)}) collective-permute-start(bf16[64,2048]{1,0:T(8,128)(2,1)S(1)} %collective-permute-done.2.refs_0_), channel_id=1, source_target_pairs={{0,1},{1,0},{4,5},{5,4},{8,9},{9,8},{12,13},{13,12},{16,17},{17,16... | collective-permute-start | bytes 786440 | tf_op jit(solution)/shard_map/ppermute | solution.py:43
  16.0 1.5 %collective-permute-start.5 = (bf16[64,2048]{1,0:T(8,128)(2,1)S(1)}, bf16[64,2048]{1,0:T(8,128)(2,1)S(1)}, u32[]{:S(2)}, u32[]{:S(2)}) collective-permute-start(bf16[64,2048]{1,0:T(8,128)(2,1)S(1)} %collective-permute-done.4.refs_2_), channel_id=1, source_target_pairs={{0,1},{1,0},{4,5},{5,4},{8,9},{9,8},{12,13},{13,12},{16,17},{17,16... | collective-permute-start | bytes 786440 | tf_op jit(solution)/shard_map/ppermute | solution.py:43
  22.0 16.1 %collective-permute-start.6 = (bf16[160,2048]{1,0:T(8,128)(2,1)S(1)}, bf16[160,2048]{1,0:T(8,128)(2,1)S(1)}, u32[]{:S(2)}, u32[]{:S(2)}) collective-permute-start(bf16[160,2048]{1,0:T(8,128)(2,1)S(1)} %get-tuple-element.19), channel_id=1, source_target_pairs={{0,130},{1,131},{4,134},{5,135},{8,138},{9,139},{12,142},{13,143},... | collective-permute-start | bytes 1966088 | tf_op jit(solution)/shard_map/ppermute | solution.py:43
  24.4 16.8 %copy-start = (f32[1,2048]{1,0:T(1,128)S(1)}, f32[1,2048]{1,0:T(1,128)}, u32[]{:S(2)}) copy-start(f32[1,2048]{1,0:T(1,128)} %gate_ref.1) | copy-start | bytes 24580
  24.4 16.8 %collective-permute-start.7 = (bf16[160,2048]{1,0:T(8,128)(2,1)S(1)}, bf16[160,2048]{1,0:T(8,128)(2,1)S(1)}, u32[]{:S(2)}, u32[]{:S(2)}) collective-permute-start(bf16[160,2048]{1,0:T(8,128)(2,1)S(1)} %get-tuple-element.20), channel_id=1, source_target_pairs={{0,2},{1,3},{4,6},{5,7},{8,10},{9,11},{12,14},{13,15},{16,18},{17,... | collective-permute-start | bytes 1966088 | tf_op jit(solution)/shard_map/ppermute | solution.py:43
  116.6 7.2 %collective-permute-start.8 = (bf16[64,64,128]{2,1,0:T(8,128)(2,1)S(1)}, bf16[64,64,128]{2,1,0:T(8,128)(2,1)S(1)}, u32[]{:S(2)}, u32[]{:S(2)}) collective-permute-start(bf16[64,64,128]{2,1,0:T(8,128)(2,1)S(1)} %all_to_all.11), channel_id=1, source_target_pairs={{0,1},{1,0},{4,5},{5,4},{8,9},{9,8},{12,13},{13,12},{16,17},{17,16... | collective-permute-start | bytes 3145736 | tf_op jit(solution)/shard_map/ppermute | solution.py:43

commit v3 on v2

--- a/solution.py
+++ b/solution.py
@@ -36,7 +36,7 @@
     return pairs
 
 
-UP, DOWN, SIB = moves(1, 0), moves(-1, 0), moves(0, 1)
+UP, DOWN, SIB, DOWN_X = moves(1, 0), moves(-1, 0), moves(0, 1), moves(-1, 1)
 
 
 def send(value, pairs):
@@ -90,20 +90,19 @@
 CUT_ROWS = 256
 
 
-def cut_pairs(w_ref, out_ref, half):
+def cut_pairs(w_ref, out_ref, half, values):
+    cols = pl.ds(pl.multiple_of(values * HD + half * HALF, HALF), HALF)
     pairs = []
-    for v in range(2):
-        cols = pl.ds(pl.multiple_of(v * HD + half * HALF, HALF), HALF)
-        for r in range(0, QUARTER, CUT_ROWS):
-            rows = slice(r, r + CUT_ROWS)
-            pairs.append((w_ref.at[rows, cols], out_ref.at[rows, v * HALF : (v + 1) * HALF]))
+    for r in range(0, QUARTER, CUT_ROWS):
+        rows = slice(r, r + CUT_ROWS)
+        pairs.append((w_ref.at[rows, cols], out_ref.at[rows]))
     return pairs
 
 
-CUT_COPIES = 2 * QUARTER // CUT_ROWS
-
-
-def sort_kernel(tokens_ref, q_ref, w_ref, up_ref, down_ref, sib_ref, w_out, sems):
+CUT_COPIES = QUARTER // CUT_ROWS
+
+
+def sort_kernel(tokens_ref, q_ref, w_ref, up_ref, down_ref, sib_ref, q_up_ref, q_down_ref, keys_out, values_out, sems):
     core, y_lo = position()
     home, away = half_of(y_lo, WIDE), half_of(1 - y_lo, WIDE)
     run_copies(
@@ -113,81 +112,77 @@
             (tokens_ref.at[:PART, home], sib_ref.at[:PART]),
             (tokens_ref.at[PART:, home], sib_ref.at[PART:TOK]),
             (q_ref, sib_ref.at[TOK:]),
+            (q_ref.at[:, half_of(core, HALF)], q_up_ref),
+            (q_ref.at[:, half_of(1 - core, HALF)], q_down_ref),
         ]
-        + cut_pairs(w_ref, w_out, 1 - core),
+        + cut_pairs(w_ref, keys_out, 1 - core, 0)
+        + cut_pairs(w_ref, values_out, 1 - core, 1),
         sems,
     )
 
 
 def sort_inputs(tokens, q, w):
-    shapes = [(PART, WIDE), (PART, WIDE), (TOK + Q_ROWS, WIDE), (QUARTER, HD)]
+    shapes = [(PART, WIDE), (PART, WIDE), (TOK + Q_ROWS, WIDE), (Q_ROWS, HALF), (Q_ROWS, HALF), (QUARTER, HALF), (QUARTER, HALF)]
     return pl.pallas_call(
         sort_kernel,
         in_specs=[HBM] * 3,
-        out_specs=[VMEM] * 4,
+        out_specs=[VMEM] * 7,
         out_shape=[pltpu.VMEM(shape, BF) for shape in shapes],
-        scratch_shapes=[pltpu.SemaphoreType.DMA((5 + CUT_COPIES,))],
+        scratch_shapes=[pltpu.SemaphoreType.DMA((7 + 2 * CUT_COPIES,))],
         compiler_params=PARAMS,
         cost_estimate=cost(0, 12 << 20),
     )(far_away(tokens), far_away(q), far_away(w))
 
 
-def project_kernel(*refs, rows, extra):
+def project_kernel(*refs, rows, extra, parts):
     n = len(rows)
-    pieces, w_ref, sib_ref, outs = refs[:n], refs[n], refs[n + 1], refs[n + 2 + extra : n + 4 + extra]
-    x_ref, own_w, own_sems, x_sems = refs[n + 4 + extra :]
+    pieces, w_ref, sib_refs = refs[:n], refs[n], refs[n + 1 : n + 1 + len(parts)]
+    refs = refs[n + 1 + len(parts) :]
+    outs, (x_ref, own_w, own_sems, x_sems) = refs[extra : extra + 2], refs[extra + 2 :]
     core, _ = position()
     pairs, start = [], 0
     for piece, count in zip(pieces, rows):
         pairs.append((piece.at[:count], x_ref.at[start : start + count]))
         start += count
     half = start // 2
-    for ref, out in zip(refs[n + 2 : n + 2 + extra], outs):
-        for i in range(2):
-            block = slice(TOK + i * Q_ROWS // 2, TOK + (i + 1) * Q_ROWS // 2)
-            pairs.append((ref.at[block, half_of(core, HALF)], out.at[half:, i * HALF : (i + 1) * HALF]))
     x_copies = [pltpu.make_async_copy(a, b, x_sems.at[i]) for i, (a, b) in enumerate(pairs)]
-    own_copies = [pltpu.make_async_copy(a, b, own_sems.at[i]) for i, (a, b) in enumerate(cut_pairs(w_ref, own_w, core))]
-    for copy in x_copies[:n]:
+    own_copies = []
+    for i, values in enumerate(parts):
+        for k, (a, b) in enumerate(cut_pairs(w_ref, own_w.at[i], core, values)):
+            own_copies.append(pltpu.make_async_copy(a, b, own_sems.at[i * CUT_COPIES + k]))
+    for copy in x_copies + own_copies:
         copy.start()
-    for copy in own_copies:
-        copy.start()
-    for copy in x_copies[n:]:
-        copy.start()
-    for copy in x_copies[:n]:
+    for copy in x_copies:
         copy.wait()
     x_own, x_other = x_ref[:, half_of(core, QUARTER)], x_ref[:, half_of(1 - core, QUARTER)]
-    for v in range(2):
-        cols = slice(v * HALF, (v + 1) * HALF)
-        mine = slice(v * CUT_COPIES // 2, (v + 1) * CUT_COPIES // 2)
-        total = jnp.dot(x_other, sib_ref[:, cols], preferred_element_type=F32)
-        for copy in own_copies[mine]:
+    for i in range(len(parts)):
+        cols = slice(i * HALF, (i + 1) * HALF)
+        total = jnp.dot(x_other, sib_refs[i][...], preferred_element_type=F32)
+        for copy in own_copies[i * CUT_COPIES : (i + 1) * CUT_COPIES]:
             copy.wait()
-        total += jnp.dot(x_own, own_w[:, cols], preferred_element_type=F32)
-        for i, out in enumerate(outs):
-            out[:half, cols] = total[i * half : (i + 1) * half].astype(out.dtype)
-    for copy in x_copies[n:]:
-        copy.wait()
-
-
-def project(pieces, w, sib_w, dtype, queries=()):
+        total += jnp.dot(x_own, own_w[i], preferred_element_type=F32)
+        for k, out in enumerate(outs):
+            out[:, cols] = total[k * half : (k + 1) * half].astype(out.dtype)
+
+
+def project(pieces, w, sib_w, parts, dtype, after=()):
     rows = [count for _, count in pieces]
     total = sum(rows)
-    height = total // 2 + (Q_ROWS // 2 if queries else 0)
-    args = [p for p, _ in pieces] + [far_away(w), sib_w, *queries]
-    return pl.pallas_call(
-        functools.partial(project_kernel, rows=rows, extra=len(queries)),
-        in_specs=[ANY] * len(pieces) + [HBM, VMEM] + [ANY] * len(queries),
+    wide = len(parts) * HALF
+    args = [p for p, _ in pieces] + [far_away(w), *[sib_w[i] for i in parts], *after]
+    return pl.pallas_call(
+        functools.partial(project_kernel, rows=rows, extra=len(after), parts=parts),
+        in_specs=[ANY] * len(pieces) + [HBM] + [VMEM] * len(parts) + [ANY] * len(after),
         out_specs=[VMEM] * 2,
-        out_shape=[pltpu.VMEM((height, HD), dtype) for _ in range(2)],
+        out_shape=[pltpu.VMEM((total // 2, wide), dtype) for _ in range(2)],
         scratch_shapes=[
             pltpu.VMEM((total, WIDE), BF),
-            pltpu.VMEM((QUARTER, HD), BF),
-            pltpu.SemaphoreType.DMA((CUT_COPIES,)),
-            pltpu.SemaphoreType.DMA((len(pieces) + 4,)),
+            pltpu.VMEM((len(parts), QUARTER, HALF), BF),
+            pltpu.SemaphoreType.DMA((len(parts) * CUT_COPIES,)),
+            pltpu.SemaphoreType.DMA((len(pieces),)),
         ],
         compiler_params=pltpu.CompilerParams(vmem_limit_bytes=14 << 20),
-        cost_estimate=cost(2 * total * WIDE * HD, 4 * WIDE * HD),
+        cost_estimate=cost(2 * total * WIDE * wide, 4 * WIDE * wide),
     )(*args)
 
 
@@ -198,17 +193,17 @@
     return jnp.dot(weights, v, preferred_element_type=F32).astype(BF)
 
 
-def attend_kernel(near0, near1, low_ref, up_ref, own_ref, sib_ref, gate_ref, out_ref):
+def attend_kernel(near0, near1, low_k, up_k, low_v, up_v, own_ref, sib_ref, q_up, q_down, gate_ref, out_ref):
     core, y_lo = position()
     place = y_lo * 2 + core
     for head in range(HEADS // 2):
-        q_cols = pl.ds(pl.multiple_of(core * HALF + head * HS, HS), HS)
-        k_cols, v_cols = slice(head * HS, (head + 1) * HS), slice(HALF + head * HS, HALF + (head + 1) * HS)
-        parts = [own_ref[TOK:, q_cols], sib_ref[TOK:, q_cols]]
-        for ref in (up_ref, low_ref):
-            parts += [ref[TOK:, k_cols], ref[TOK:, v_cols]]
-        q = jnp.concatenate(parts, axis=0)
-        gate = gate_ref[:, q_cols]
+        cols = slice(head * HS, (head + 1) * HS)
+        near_v = slice(HALF + head * HS, HALF + (head + 1) * HS)
+        global_cols = pl.ds(pl.multiple_of(core * HALF + head * HS, HS), HS)
+        q = jnp.concatenate(
+            [own_ref[TOK:, global_cols], sib_ref[TOK:, global_cols], q_up[:, cols], q_down[:, cols]], axis=0
+        )
+        gate = gate_ref[:, global_cols]
         terms = []
         for _ in range(3):
             terms.append(gate.astype(BF))
@@ -216,12 +211,9 @@
         gate = jnp.concatenate([t.astype(F32) for t in terms] + [jnp.zeros((GATE_ROWS - 3, HS), F32)], axis=0).astype(BF)
         for batch, near in enumerate((near0, near1)):
             rows = slice(batch * PART, (batch + 1) * PART)
-
-            def total(cols):
-                far = jnp.concatenate([low_ref[rows, cols], up_ref[rows, cols]], axis=0)
-                return (near[:, cols] + far.astype(F32)).astype(BF)
-
-            update = one_head(q, total(k_cols), total(v_cols))
+            k = near[:, cols] + jnp.concatenate([low_k[rows, cols], up_k[rows, cols]], axis=0).astype(F32)
+            v = near[:, near_v] + jnp.concatenate([low_v[rows, cols], up_v[rows, cols]], axis=0).astype(F32)
+            update = one_head(q, k.astype(BF), v.astype(BF))
             for i in range(S // BLOCK):
                 at = (batch * (HEADS // 2) + head) * (S // BLOCK) + (place ^ i)
                 out_ref[at, :BLOCK] = update[i * BLOCK : (i + 1) * BLOCK]
@@ -289,15 +281,19 @@
 
 
 def body(tokens, w_kv, q_state, decay):
-    to_up, to_down, to_sib, to_sib_w = sort_inputs(tokens[0], q_state, w_kv)
-    low, up, sib, sib_w = send(to_up, UP), send(to_down, DOWN), send(to_sib, SIB), send(to_sib_w, SIB)
+    to_up, to_down, to_sib, q_up, q_down, to_sib_k, to_sib_v = sort_inputs(tokens[0], q_state, w_kv)
+    low, up, sib = send(to_up, UP), send(to_down, DOWN), send(to_sib, SIB)
+    sib_w = send(to_sib_k, SIB), send(to_sib_v, SIB)
+    q_far = send(q_up, UP), send(q_down, DOWN_X)
     low_sib, up_sib = send(low, SIB), send(up, SIB)
 
     away = [(part, PART) for part in (low, low_sib, up, up_sib)]
-    lower, upper = project(away, w_kv, sib_w, BF, (sib, to_sib))
-    far = send(lower, DOWN), send(upper, UP)
-    near = project([(to_sib, TOK), (sib, TOK)], w_kv, sib_w, F32)
-    states = spread(scan(spread(attend(near, far, (to_sib, sib), decay))))
+    lower, upper = project(away, w_kv, sib_w, (0,), BF)
+    far_k = send(lower, DOWN), send(upper, UP)
+    lower, upper = project(away, w_kv, sib_w, (1,), BF)
+    far_v = send(lower, DOWN), send(upper, UP)
+    near = project([(to_sib, TOK), (sib, TOK)], w_kv, sib_w, (0, 1), F32, q_far)
+    states = spread(scan(spread(attend(near, far_k + far_v, (to_sib, sib) + q_far, decay))))
     other = send(states, SIB)
     shape = (2, HEADS // 2, S, HS)
     return place(states.reshape(shape), other.reshape(shape))[None, None]

time: 125 us -> 124 us (level)
  waiting for transfers between devices: 22.3 us -> 11.8 us
  starting transfers between devices: 14.7 us -> 19.6 us
  blocking collectives: 73.3 us -> 75.6 us
  Pallas kernels: 14.5 us -> 16.1 us
    ppermute x9 -> x14, waiting for transfers between devices: 22.3 us -> 11.8 us  [send(): return lax.ppermute(value, BOTH, pairs)]
    ppermute x9 -> x14, starting transfers between devices: 14.7 us -> 19.6 us  [send(): return lax.ppermute(value, BOTH, pairs)]
    all_to_all x2, blocking collectives: 73.3 us -> 75.6 us  [spread(): return lax.all_to_all(value, 'seg', 0, 0, tiled=True)]
    pallas_call x3 -> x4, Pallas kernels: 11.4 us -> 12.9 us  [the longest x3 10.1 us: project(): pl.pallas_call(functools.partial(project_kernel, rows=rows, extra=len(aft...]
  transfers between devices with their start and end apart: 9 -> 14, of which waited for: 6 -> 5; matrix products, arithmetic and copies ran while one was open for 0% -> 0% of each run, Pallas kernels for 3% -> 8%
where the time goes in v3:
time: 124 us; the launch traced here: 123 us
  blocking collectives  75.6 us (61%)
  starting transfers between devices  19.6 us (16%)
  Pallas kernels  16.1 us (13%)
  waiting for transfers between devices  11.8 us (10%)
    all_to_all x2, blocking collectives, spread(): return lax.all_to_all(value, 'seg', 0, 0, tiled=True)  75.6 us
    ppermute x14, starting transfers between devices, send(): return lax.ppermute(value, BOTH, pairs)  19.6 us
    ppermute x14, waiting for transfers between devices, send(): return lax.ppermute(value, BOTH, pairs)  11.8 us
    pallas_call x3, Pallas kernels, project(): pl.pallas_call(functools.partial(project_kernel, rows=rows, extra=len(aft...  10.1 us
    pallas_call x1, Pallas kernels, sort_inputs(): pl.pallas_call(sort_kernel, in_specs=[HBM] * 3, out_specs=[VMEM] * 7, out...  2.76 us
  transfers between devices with their start and end apart: 14, of which 5 were waited for; matrix products, arithmetic and copies ran while one was open for 0% of the time, Pallas kernels for 8%

profile of v3, /device:TPU:1, one launch (start us, length us, event | category | flops | bytes accessed | tf_op | source)
XLA Modules:
  0.0 123.4 jit_solution(546402510042849474)
XLA Ops:
  0.0 2.8 %shard_map.46 = (bf16[64,2048]{1,0:T(8,128)(2,1)S(1)}, bf16[64,2048]{1,0:T(8,128)(2,1)S(1)}, bf16[192,2048]{1,0:T(8,128)(2,1)S(1)}, bf16[64,1024]{1,0:T(8,128)(2...) custom-call(bf16[128,4096]{1,0:T(8,128)(2,1)} %bitcast.6, ...), custom_call_target="tpu_custom_call" | custom-call | bytes 12582912 | tf_op jit(solution)/shard_map/pallas_call | solution.py:126
  2.8 3.3 %collective-permute-start.2 = (bf16[1024,1024]{1,0:T(8,128)(2,1)S(1)}, bf16[1024,1024]{1,0:T(8,128)(2,1)S(1)}, u32[]{:S(2)}, u32[]{:S(2)}) collective-permute-start(bf16[1024,1024]{1,0:T(8,128)(2,1)S(1)} %get-tuple-element.20), channel_id=1, source_target_pairs={{0,1},{1,0},{4,5},{5,4},{8,9},{9,8},{12,13},{13,12},{16,17},{17,16... | collective-permute-start | bytes 6291464 | tf_op jit(solution)/shard_map/ppermute | solution.py:43
  6.1 0.1 collective-permute-start.1
  6.2 0.0 collective-permute-start.5
  6.2 2.7 %collective-permute-start.7 = (bf16[64,2048]{1,0:T(8,128)(2,1)S(1)}, bf16[64,2048]{1,0:T(8,128)(2,1)S(1)}, u32[]{:S(2)}, u32[]{:S(2)}) collective-permute-start(bf16[64,2048]{1,0:T(8,128)(2,1)S(1)} %get-tuple-element.26), channel_id=1, source_target_pairs={{0,130},{1,131},{4,134},{5,135},{8,138},{9,139},{12,142},{13,143},... | collective-permute-start | bytes 786440 | tf_op jit(solution)/shard_map/ppermute | solution.py:43
  8.9 1.0 collective-permute-start
  9.8 5.0 %collective-permute-done.5.refs_0_ = bf16[64,2048]{1,0:T(8,128)(2,1)S(1)} collective-permute-done((bf16[64,2048]{1,0:T(8,128)(2,1)S(1)}, bf16[64,2048]{1,0:T(8,128)(2,1)S(1)}, u32[]{:S(2)}, u32[]{:S(2)}) %collective-permute-start.5) | collective-permute-done | bytes 262176 | tf_op jit(solution)/shard_map/ppermute | solution.py:43
  14.9 1.2 %collective-permute-start.6 = (bf16[64,2048]{1,0:T(8,128)(2,1)S(1)}, bf16[64,2048]{1,0:T(8,128)(2,1)S(1)}, u32[]{:S(2)}, u32[]{:S(2)}) collective-permute-start(bf16[64,2048]{1,0:T(8,128)(2,1)S(1)} %collective-permute-done.5.refs_0_), channel_id=1, source_target_pairs={{0,1},{1,0},{4,5},{5,4},{8,9},{9,8},{12,13},{13,12},{16,17},{17,16... | collective-permute-start | bytes 786440 | tf_op jit(solution)/shard_map/ppermute | solution.py:43
  16.1 0.0 collective-permute-done.7.refs_2_
  16.1 0.0 collective-permute-start.8
  16.1 1.2 collective-permute-done.6.refs_1_
  17.3 0.0 collective-permute-start.3
  17.3 0.4 collective-permute-done.8.refs_3_
  17.7 2.8 %collective-permute-start.4 = (bf16[64,1024]{1,0:T(8,128)(2,1)S(1)}, bf16[64,1024]{1,0:T(8,128)(2,1)S(1)}, u32[]{:S(2)}, u32[]{:S(2)}) collective-permute-start(bf16[64,1024]{1,0:T(8,128)(2,1)S(1)} %get-tuple-element.22), channel_id=1, source_target_pairs={{0,131},{1,130},{4,135},{5,134},{8,139},{9,138},{12,143},{13,142},... | collective-permute-start | bytes 393224 | tf_op jit(solution)/shard_map/ppermute | solution.py:43
  20.5 0.0 collective-permute-done.2.refs_4_.refs_5_
  20.5 2.9 %shard_map.49 = (bf16[128,1024]{1,0:T(8,128)(2,1)S(1)}, bf16[128,1024]{1,0:T(8,128)(2,1)S(1)}) custom-call(bf16[64,2048]{1,0:T(8,128)(2,1)S(1)} %collective-permute-done.5.refs_0_, bf16[64,2048]{1,0:T(8,128)(2,1)S(1)} %collective-permute-done.6.refs_1_, bf16[64,2048]{1,0:T(8,128)(2,1)S(1)} %collective-permute-done.7.refs_2_, ...), custom_call_target="tpu_custom_call" | custom-call | flops 1073741824 | bytes 8388608 | tf_op jit(solution)/shard_map/pallas_call | solution.py:173
  23.4 0.1 collective-permute-start.11
  23.5 0.0 collective-permute-done.1.refs_3_.refs_5_
  23.5 1.4 %collective-permute-start.12 = (bf16[128,1024]{1,0:T(8,128)(2,1)S(1)}, bf16[128,1024]{1,0:T(8,128)(2,1)S(1)}, u32[]{:S(2)}, u32[]{:S(2)}) collective-permute-start(bf16[128,1024]{1,0:T(8,128)(2,1)S(1)} %get-tuple-element.30), channel_id=1, source_target_pairs={{0,2},{1,3},{4,6},{5,7},{8,10},{9,11},{12,14},{13,15},{16,18},{17,... | collective-permute-start | bytes 786440 | tf_op jit(solution)/shard_map/ppermute | solution.py:43
  25.0 2.9 %shard_map.48 = (bf16[128,1024]{1,0:T(8,128)(2,1)S(1)}, bf16[128,1024]{1,0:T(8,128)(2,1)S(1)}) custom-call(bf16[64,2048]{1,0:T(8,128)(2,1)S(1)} %collective-permute-done.5.refs_0_, bf16[64,2048]{1,0:T(8,128)(2,1)S(1)} %collective-permute-done.6.refs_1_, bf16[64,2048]{1,0:T(8,128)(2,1)S(1)} %collective-permute-done.7.refs_2_, ...), custom_call_target="tpu_custom_call" | custom-call | flops 1073741824 | bytes 8388608 | tf_op jit(solution)/shard_map/pallas_call | solution.py:173
  27.9 0.0 collective-permute-done.3.refs_5_.q_up
  27.9 0.1 collective-permute-start.10
  28.0 0.0 collective-permute-done.4.refs_6_.q_down
  28.0 0.0 copy-start
  28.0 2.6 %collective-permute-start.9 = (bf16[128,1024]{1,0:T(8,128)(2,1)S(1)}, bf16[128,1024]{1,0:T(8,128)(2,1)S(1)}, u32[]{:S(2)}, u32[]{:S(2)}) collective-permute-start(bf16[128,1024]{1,0:T(8,128)(2,1)S(1)} %get-tuple-element.27), channel_id=1, source_target_pairs={{0,130},{1,131},{4,134},{5,135},{8,138},{9,139},{12,142},{13,143},... | collective-permute-start | bytes 786440 | tf_op jit(solution)/shard_map/ppermute | solution.py:43
  30.7 0.0 collective-permute-done.refs_1_.sib_ref
  30.7 4.3 %shard_map.47 = (f32[128,2048]{1,0:T(8,128)S(1)}, f32[128,2048]{1,0:T(8,128)S(1)}) custom-call(bf16[192,2048]{1,0:T(8,128)(2,1)S(1)} %get-tuple-element.18.refs_0_.own_ref, bf16[192,2048]{1,0:T(8,128)(2,1)S(1)} %collective-permute-done.refs_1_.sib_ref, bf16[1024,4096]{1,0:T(8,128)(2,1)} %refs_4_.3, ...), custom_call_target="tpu_custom_call" | custom-call | flops 2147483648 | bytes 16777216 | tf_op jit(solution)/shard_map/pallas_call | solution.py:173
  35.0 0.0 collective-permute-done.11.low_v
  35.0 0.0 collective-permute-done.12.up_v
  35.0 3.0 %collective-permute-done.10.up_k = bf16[128,1024]{1,0:T(8,128)(2,1)S(1)} collective-permute-done((bf16[128,1024]{1,0:T(8,128)(2,1)S(1)}, bf16[128,1024]{1,0:T(8,128)(2,1)S(1)}, u32[]{:S(2)}, u32[]{:S(2)}) %collective-permute-start.10) | collective-permute-done | bytes 262176 | tf_op jit(solution)/shard_map/ppermute | solution.py:43
  38.0 0.0 collective-permute-done.9.low_k
  38.0 0.0 copy-done
  38.0 1.7 %shard_map.50 = bf16[64,72,128]{2,1,0:T(8,128)(2,1)S(1)} custom-call(f32[128,2048]{1,0:T(8,128)S(1)} %get-tuple-element.23.near0, f32[128,2048]{1,0:T(8,128)S(1)} %get-tuple-element.24.near1, bf16[128,1024]{1,0:T(8,128)(2,1)S(1)} %collective-permute-done.9.low_k, bf16[128,1024]{1,0:T(8,128)(2,1)S(1)} %collective-permute-done.10.up_k, ...), custom_call_target="tpu_custom_call" | custom-call | flops 268435456 | bytes 6291456 | tf_op jit(solution)/shard_map/pallas_call | solution.py:225
  39.8 40.6 %all_to_all.10.update_ref = bf16[64,72,128]{2,1,0:T(8,128)(2,1)S(1)} all-to-all(bf16[64,72,128]{2,1,0:T(8,128)(2,1)S(1)} %shard_map.50), channel_id=1, replica_groups=mesh['seg'=64,'fsdp'=4] {'seg'}, dimensions={0} | all-to-all | bytes 2359296 | tf_op jit(solution)/shard_map/all_to_all | solution.py:280
  80.3 0.3 shard_map.51
  80.7 35.0 %all_to_all.11 = bf16[64,64,128]{2,1,0:T(8,128)(2,1)S(1)} all-to-all(bf16[64,64,128]{2,1,0:T(8,128)(2,1)S(1)} %shard_map.51), channel_id=1, replica_groups=mesh['seg'=64,'fsdp'=4] {'seg'}, dimensions={0} | all-to-all | bytes 2097152 | tf_op jit(solution)/shard_map/all_to_all | solution.py:280
  115.7 4.1 %collective-permute-start.13 = (bf16[64,64,128]{2,1,0:T(8,128)(2,1)S(1)}, bf16[64,64,128]{2,1,0:T(8,128)(2,1)S(1)}, u32[]{:S(2)}, u32[]{:S(2)}) collective-permute-start(bf16[64,64,128]{2,1,0:T(8,128)(2,1)S(1)} %all_to_all.11), channel_id=1, source_target_pairs={{0,1},{1,0},{4,5},{5,4},{8,9},{9,8},{12,13},{13,12},{16,17},{17,16... | collective-permute-start | bytes 3145736 | tf_op jit(solution)/shard_map/ppermute | solution.py:43
  119.8 2.3 %collective-permute-done.13 = bf16[64,64,128]{2,1,0:T(8,128)(2,1)S(1)} collective-permute-done((bf16[64,64,128]{2,1,0:T(8,128)(2,1)S(1)}, bf16[64,64,128]{2,1,0:T(8,128)(2,1)S(1)}, u32[]{:S(2)}, u32[]{:S(2)}) %collective-permute-start.13) | collective-permute-done | bytes 1048608 | tf_op jit(solution)/shard_map/ppermute | solution.py:43
  122.1 1.1 shard_map.52
Async XLA Ops:
  2.8 17.7 %collective-permute-start.2 = (bf16[1024,1024]{1,0:T(8,128)(2,1)S(1)}, bf16[1024,1024]{1,0:T(8,128)(2,1)S(1)}, u32[]{:S(2)}, u32[]{:S(2)}) collective-permute-start(bf16[1024,1024]{1,0:T(8,128)(2,1)S(1)} %get-tuple-element.20), channel_id=1, source_target_pairs={{0,1},{1,0},{4,5},{5,4},{8,9},{9,8},{12,13},{13,12},{16,17},{17,16... | collective-permute-start | bytes 6291464 | tf_op jit(solution)/shard_map/ppermute | solution.py:43
  6.1 17.4 %collective-permute-start.1 = (bf16[1024,1024]{1,0:T(8,128)(2,1)S(1)}, bf16[1024,1024]{1,0:T(8,128)(2,1)S(1)}, u32[]{:S(2)}, u32[]{:S(2)}) collective-permute-start(bf16[1024,1024]{1,0:T(8,128)(2,1)S(1)} %get-tuple-element.19), channel_id=1, source_target_pairs={{0,1},{1,0},{4,5},{5,4},{8,9},{9,8},{12,13},{13,12},{16,17},{17,16... | collective-permute-start | bytes 6291464 | tf_op jit(solution)/shard_map/ppermute | solution.py:43
  6.2 8.7 %collective-permute-start.5 = (bf16[64,2048]{1,0:T(8,128)(2,1)S(1)}, bf16[64,2048]{1,0:T(8,128)(2,1)S(1)}, u32[]{:S(2)}, u32[]{:S(2)}) collective-permute-start(bf16[64,2048]{1,0:T(8,128)(2,1)S(1)} %get-tuple-element.25), channel_id=1, source_target_pairs={{0,2},{1,3},{4,6},{5,7},{8,10},{9,11},{12,14},{13,15},{16,18},{17,... | collective-permute-start | bytes 786440 | tf_op jit(solution)/shard_map/ppermute | solution.py:43
  6.2 9.9 %collective-permute-start.7 = (bf16[64,2048]{1,0:T(8,128)(2,1)S(1)}, bf16[64,2048]{1,0:T(8,128)(2,1)S(1)}, u32[]{:S(2)}, u32[]{:S(2)}) collective-permute-start(bf16[64,2048]{1,0:T(8,128)(2,1)S(1)} %get-tuple-element.26), channel_id=1, source_target_pairs={{0,130},{1,131},{4,134},{5,135},{8,138},{9,139},{12,142},{13,143},... | collective-permute-start | bytes 786440 | tf_op jit(solution)/shard_map/ppermute | solution.py:43
  8.9 21.8 %collective-permute-start = (bf16[192,2048]{1,0:T(8,128)(2,1)S(1)}, bf16[192,2048]{1,0:T(8,128)(2,1)S(1)}, u32[]{:S(2)}, u32[]{:S(2)}) collective-permute-start(bf16[192,2048]{1,0:T(8,128)(2,1)S(1)} %get-tuple-element.18.refs_0_.own_ref), channel_id=1, source_target_pairs={{0,1},{1,0},{4,5},{5,4},{8,9},{9,8},{12,13},{13,12},{16,17},{17,16... | collective-permute-start | bytes 2359304 | tf_op jit(solution)/shard_map/ppermute | solution.py:43
  14.9 2.4 %collective-permute-start.6 = (bf16[64,2048]{1,0:T(8,128)(2,1)S(1)}, bf16[64,2048]{1,0:T(8,128)(2,1)S(1)}, u32[]{:S(2)}, u32[]{:S(2)}) collective-permute-start(bf16[64,2048]{1,0:T(8,128)(2,1)S(1)} %collective-permute-done.5.refs_0_), channel_id=1, source_target_pairs={{0,1},{1,0},{4,5},{5,4},{8,9},{9,8},{12,13},{13,12},{16,17},{17,16... | collective-permute-start | bytes 786440 | tf_op jit(solution)/shard_map/ppermute | solution.py:43
  16.1 1.5 %collective-permute-start.8 = (bf16[64,2048]{1,0:T(8,128)(2,1)S(1)}, bf16[64,2048]{1,0:T(8,128)(2,1)S(1)}, u32[]{:S(2)}, u32[]{:S(2)}) collective-permute-start(bf16[64,2048]{1,0:T(8,128)(2,1)S(1)} %collective-permute-done.7.refs_2_), channel_id=1, source_target_pairs={{0,1},{1,0},{4,5},{5,4},{8,9},{9,8},{12,13},{13,12},{16,17},{17,16... | collective-permute-start | bytes 786440 | tf_op jit(solution)/shard_map/ppermute | solution.py:43
  17.3 10.6 %collective-permute-start.3 = (bf16[64,1024]{1,0:T(8,128)(2,1)S(1)}, bf16[64,1024]{1,0:T(8,128)(2,1)S(1)}, u32[]{:S(2)}, u32[]{:S(2)}) collective-permute-start(bf16[64,1024]{1,0:T(8,128)(2,1)S(1)} %get-tuple-element.21), channel_id=1, source_target_pairs={{0,2},{1,3},{4,6},{5,7},{8,10},{9,11},{12,14},{13,15},{16,18},{17,... | collective-permute-start | bytes 393224 | tf_op jit(solution)/shard_map/ppermute | solution.py:43
  17.7 10.3 %collective-permute-start.4 = (bf16[64,1024]{1,0:T(8,128)(2,1)S(1)}, bf16[64,1024]{1,0:T(8,128)(2,1)S(1)}, u32[]{:S(2)}, u32[]{:S(2)}) collective-permute-start(bf16[64,1024]{1,0:T(8,128)(2,1)S(1)} %get-tuple-element.22), channel_id=1, source_target_pairs={{0,131},{1,130},{4,135},{5,134},{8,139},{9,138},{12,143},{13,142},... | collective-permute-start | bytes 393224 | tf_op jit(solution)/shard_map/ppermute | solution.py:43
  23.4 11.6 %collective-permute-start.11 = (bf16[128,1024]{1,0:T(8,128)(2,1)S(1)}, bf16[128,1024]{1,0:T(8,128)(2,1)S(1)}, u32[]{:S(2)}, u32[]{:S(2)}) collective-permute-start(bf16[128,1024]{1,0:T(8,128)(2,1)S(1)} %get-tuple-element.29), channel_id=1, source_target_pairs={{0,130},{1,131},{4,134},{5,135},{8,138},{9,139},{12,142},{13,143},... | collective-permute-start | bytes 786440 | tf_op jit(solution)/shard_map/ppermute | solution.py:43
  23.5 11.5 %collective-permute-start.12 = (bf16[128,1024]{1,0:T(8,128)(2,1)S(1)}, bf16[128,1024]{1,0:T(8,128)(2,1)S(1)}, u32[]{:S(2)}, u32[]{:S(2)}) collective-permute-start(bf16[128,1024]{1,0:T(8,128)(2,1)S(1)} %get-tuple-element.30), channel_id=1, source_target_pairs={{0,2},{1,3},{4,6},{5,7},{8,10},{9,11},{12,14},{13,15},{16,18},{17,... | collective-permute-start | bytes 786440 | tf_op jit(solution)/shard_map/ppermute | solution.py:43
  27.9 10.1 %collective-permute-start.10 = (bf16[128,1024]{1,0:T(8,128)(2,1)S(1)}, bf16[128,1024]{1,0:T(8,128)(2,1)S(1)}, u32[]{:S(2)}, u32[]{:S(2)}) collective-permute-start(bf16[128,1024]{1,0:T(8,128)(2,1)S(1)} %get-tuple-element.28), channel_id=1, source_target_pairs={{0,2},{1,3},{4,6},{5,7},{8,10},{9,11},{12,14},{13,15},{16,18},{17,... | collective-permute-start | bytes 786440 | tf_op jit(solution)/shard_map/ppermute | solution.py:43
  28.0 10.0 %copy-start = (f32[1,2048]{1,0:T(1,128)S(1)}, f32[1,2048]{1,0:T(1,128)}, u32[]{:S(2)}) copy-start(f32[1,2048]{1,0:T(1,128)} %gate_ref.1) | copy-start | bytes 24580
  28.0 10.0 %collective-permute-start.9 = (bf16[128,1024]{1,0:T(8,128)(2,1)S(1)}, bf16[128,1024]{1,0:T(8,128)(2,1)S(1)}, u32[]{:S(2)}, u32[]{:S(2)}) collective-permute-start(bf16[128,1024]{1,0:T(8,128)(2,1)S(1)} %get-tuple-element.27), channel_id=1, source_target_pairs={{0,130},{1,131},{4,134},{5,135},{8,138},{9,139},{12,142},{13,143},... | collective-permute-start | bytes 786440 | tf_op jit(solution)/shard_map/ppermute | solution.py:43
  115.7 6.4 %collective-permute-start.13 = (bf16[64,64,128]{2,1,0:T(8,128)(2,1)S(1)}, bf16[64,64,128]{2,1,0:T(8,128)(2,1)S(1)}, u32[]{:S(2)}, u32[]{:S(2)}) collective-permute-start(bf16[64,64,128]{2,1,0:T(8,128)(2,1)S(1)} %all_to_all.11), channel_id=1, source_target_pairs={{0,1},{1,0},{4,5},{5,4},{8,9},{9,8},{12,13},{13,12},{16,17},{17,16... | collective-permute-start | bytes 3145736 | tf_op jit(solution)/shard_map/ppermute | solution.py:43

commit v4 on v3

v4 whole, which is shorter than its diff:
```python
import functools
import math

import jax
import jax.numpy as jnp
from jax import lax
from jax.experimental import pallas as pl
from jax.experimental.pallas import tpu as pltpu
from jax.sharding import PartitionSpec as P

HEADS = 16
HS = 128
S = 256
SEG = 64
TOK = 128
D = 4096
HD = 2048
QUARTER = D // 4
HALF = HD // 2
BOTH = ("seg", "fsdp")
BF = jnp.bfloat16
F32 = jnp.float32


def flat(y, x, z, core):
    return (((y // 2) * 4 + x) * 8 + z) * 4 + (y % 2) * 2 + core


def moves(steps, dc=0):
    pairs = []
    for y in range(4):
        for x in range(4):
            for z in range(8):
                for core in range(2):
                    pairs.append((flat(y, x, z, core), flat((y + steps[core]) % 4, x, z, (core + dc) % 2)))
    return pairs


OUT, BACK, SIB = moves((1, -1)), moves((-1, 1)), moves((0, 0), 1)


def send(value, pairs):
    return lax.ppermute(value, BOTH, pairs)


TILE = 256
WIDE = 2 * QUARTER
Q_ROWS = S // 4
BLOCK = S // 4
GATE_ROWS = 8

ANY = pl.BlockSpec(memory_space=pl.ANY)
HBM = pl.BlockSpec(memory_space=pltpu.HBM)
VMEM = pl.BlockSpec(memory_space=pltpu.VMEM)


def here(value):
    return pltpu.with_memory_space_constraint(value, pltpu.VMEM)


def far_away(value):
    return pltpu.with_memory_space_constraint(value, pltpu.HBM)


def position():
    fsdp = lax.axis_index("fsdp")
    return fsdp % 2, fsdp // 2


def half_of(which, size):
    return pl.ds(pl.multiple_of(which * size, size), size)


def run_copies(pairs, sems):
    todo = [pltpu.make_async_copy(a, b, sems.at[i]) for i, (a, b) in enumerate(pairs)]
    for c in todo:
        c.start()
    for c in todo:
        c.wait()


PARAMS = pltpu.CompilerParams(vmem_limit_bytes=8 << 20)


def cost(flops, nbytes, exps=0):
    return pl.CostEstimate(flops=flops, bytes_accessed=nbytes, transcendentals=exps)


CUT_ROWS = 256


def cut_pairs(w_ref, out_ref, half, values):
    cols = pl.ds(pl.multiple_of(values * HD + half * HALF, HALF), HALF)
    pairs = []
    for r in range(0, QUARTER, CUT_ROWS):
        rows = slice(r, r + CUT_ROWS)
        pairs.append((w_ref.at[rows, cols], out_ref.at[rows]))
    return pairs


CUT_COPIES = QUARTER // CUT_ROWS


def sort_kernel(tokens_ref, q_ref, w_ref, far_ref, sib_ref, keys_out, values_out, sems):
    core, y_lo = position()
    home, away = half_of(y_lo, WIDE), half_of(1 - y_lo, WIDE)
    half = TOK // 2
    run_copies(
        [
            (tokens_ref.at[:half, away], far_ref.at[:half]),
            (tokens_ref.at[half:, away], far_ref.at[half:]),
            (tokens_ref.at[:half, home], sib_ref.at[:half]),
            (tokens_ref.at[half:, home], sib_ref.at[half:TOK]),
            (q_ref, sib_ref.at[TOK:]),
        ]
        + cut_pairs(w_ref, keys_out, 1 - core, 0)
        + cut_pairs(w_ref, values_out, 1 - core, 1),
        sems,
    )


def sort_inputs(tokens, q, w):
    shapes = [(TOK, WIDE), (TOK + Q_ROWS, WIDE), (QUARTER, HALF), (QUARTER, HALF)]
    return pl.pallas_call(
        sort_kernel,
        in_specs=[HBM] * 3,
        out_specs=[VMEM] * 4,
        out_shape=[pltpu.VMEM(shape, BF) for shape in shapes],
        scratch_shapes=[pltpu.SemaphoreType.DMA((5 + 2 * CUT_COPIES,))],
        compiler_params=PARAMS,
        cost_estimate=cost(0, 12 << 20),
    )(far_away(tokens), far_away(q), far_away(w))


def join_kernel(far_ref, own_ref, sib_ref, after_ref, out_ref, q_ref, sems):
    del after_ref
    core, _ = position()
    cols = half_of(core, HALF)
    run_copies(
        [
            (far_ref, out_ref),
            (own_ref.at[TOK:, cols], q_ref.at[:Q_ROWS]),
            (sib_ref.at[TOK:, cols], q_ref.at[Q_ROWS:]),
        ],
        sems,
    )


def join(far, own, sib, after):
    return pl.pallas_call(
        join_kernel,
        in_specs=[ANY] * 4,
        out_specs=[VMEM] * 2,
        out_shape=[pltpu.VMEM((TOK, WIDE), BF), pltpu.VMEM((2 * Q_ROWS, HALF), BF)],
        scratch_shapes=[pltpu.SemaphoreType.DMA((3,))],
        compiler_params=PARAMS,
        cost_estimate=cost(0, 1 << 20),
    )(far, own, sib, after)


def cut_kernel(w_ref, after_ref, keys_out, values_out, sems):
    del after_ref
    core, _ = position()
    run_copies(cut_pairs(w_ref, keys_out, core, 0) + cut_pairs(w_ref, values_out, core, 1), sems)


def cut_weights(w, after):
    return pl.pallas_call(
        cut_kernel,
        in_specs=[HBM, ANY],
        out_specs=[VMEM] * 2,
        out_shape=[pltpu.VMEM((QUARTER, HALF), BF) for _ in range(2)],
        scratch_shapes=[pltpu.SemaphoreType.DMA((2 * CUT_COPIES,))],
        compiler_params=PARAMS,
        cost_estimate=cost(0, 8 << 20),
    )(far_away(w), after)


def project_kernel(*refs, rows, extra, parts):
    n, m = len(rows), len(parts)
    pieces, own_refs, sib_refs = refs[:n], refs[n : n + m], refs[n + m : n + 2 * m]
    outs, x_ref, sems = refs[n + 2 * m + extra : -2], refs[-2], refs[-1]
    core, _ = position()
    pairs, start = [], 0
    for piece, count in zip(pieces, rows):
        pairs.append((piece.at[:count], x_ref.at[start : start + count]))
        start += count
    run_copies(pairs, sems)
    half = start // 2
    x_own, x_other = x_ref[:, half_of(core, QUARTER)], x_ref[:, half_of(1 - core, QUARTER)]
    for i in range(m):
        total = jnp.dot(x_other, sib_refs[i][...], preferred_element_type=F32)
        total += jnp.dot(x_own, own_refs[i][...], preferred_element_type=F32)
        for k, out in enumerate(outs):
            out[:, i * HALF : (i + 1) * HALF] = total[k * half : (k + 1) * half].astype(out.dtype)


def project(pieces, own_w, sib_w, parts, dtype, after=()):
    rows = [TOK] * len(pieces)
    total = sum(rows)
    wide = len(parts) * HALF
    args = list(pieces) + [own_w[i] for i in parts] + [sib_w[i] for i in parts] + list(after)
    return pl.pallas_call(
        functools.partial(project_kernel, rows=rows, extra=len(after), parts=parts),
        in_specs=[ANY] * len(pieces) + [VMEM] * (2 * len(parts)) + [ANY] * len(after),
        out_specs=[VMEM] * 2,
        out_shape=[pltpu.VMEM((total // 2, wide), dtype) for _ in range(2)],
        scratch_shapes=[pltpu.VMEM((total, WIDE), BF), pltpu.SemaphoreType.DMA((len(pieces),))],
        compiler_params=pltpu.CompilerParams(vmem_limit_bytes=14 << 20),
        cost_estimate=cost(2 * total * WIDE * wide, 4 * WIDE * wide),
    )(*args)


def softmax_of(q, k):
    scores = lax.dot_general(q, k, (((1,), (1,)), ((), ())), preferred_element_type=F32) * (1.0 / math.sqrt(HS))
    scores = jnp.exp(scores - jnp.max(scores, axis=1, keepdims=True))
    return (scores / jnp.sum(scores, axis=1, keepdims=True)).astype(BF)


def weigh_kernel(near0, near1, far0, far1, own_ref, sib_ref, q_far, out_ref):
    core, _ = position()
    for head in range(HEADS // 2):
        cols = slice(head * HS, (head + 1) * HS)
        global_cols = pl.ds(pl.multiple_of(core * HALF + head * HS, HS), HS)
        q = jnp.concatenate([own_ref[TOK:, global_cols], sib_ref[TOK:, global_cols], q_far[:, cols]], axis=0)
        for batch, (near, far) in enumerate(((near0, far0), (near1, far1))):
            k = near[:, cols] + far[:, cols].astype(F32)
            out_ref[batch * (HEADS // 2) + head] = softmax_of(q, k.astype(BF))


def weigh(near, far, queries):
    args = [*near, *far, *queries]
    return pl.pallas_call(
        weigh_kernel,
        in_specs=[VMEM] * len(args),
        out_specs=VMEM,
        out_shape=pltpu.VMEM((HEADS, S, TOK), BF),
        compiler_params=PARAMS,
        cost_estimate=cost(2 * HEADS * S * TOK * HS, 4 << 20, HEADS * S * TOK),
    )(*args)


def update_kernel(weights_ref, near0, near1, far0, far1, gate_ref, out_ref):
    core, y_lo = position()
    place = y_lo * 2 + core
    for head in range(HEADS // 2):
        cols = slice(head * HS, (head + 1) * HS)
        near_cols = slice(HALF + head * HS, HALF + (head + 1) * HS)
        gate = gate_ref[:, pl.ds(pl.multiple_of(core * HALF + head * HS, HS), HS)]
        terms = []
        for _ in range(3):
            terms.append(gate.astype(BF))
            gate = gate - terms[-1].astype(F32)
        gate = jnp.concatenate([t.astype(F32) for t in terms] + [jnp.zeros((GATE_ROWS - 3, HS), F32)], axis=0).astype(BF)
        for batch, (near, far) in enumerate(((near0, far0), (near1, far1))):
            v = near[:, near_cols] + far[:, cols].astype(F32)
            first = batch * (HEADS // 2) + head
            update = jnp.dot(weights_ref[first], v.astype(BF), preferred_element_type=F32).astype(BF)
            for i in range(S // BLOCK):
                at = first * (S // BLOCK) + (place ^ i)
                out_ref[at, :BLOCK] = update[i * BLOCK : (i + 1) * BLOCK]
                out_ref[at, BLOCK:] = gate


def updates(weights, near, far, gate):
    args = [weights, *near, *far, gate]
    return pl.pallas_call(
        update_kernel,
        in_specs=[VMEM] * len(args),
        out_specs=VMEM,
        out_shape=pltpu.VMEM((SEG, BLOCK + GATE_ROWS, HS), BF),
        compiler_params=PARAMS,
        cost_estimate=cost(2 * HEADS * S * TOK * HS, 4 << 20),
    )(*args)


def scan_kernel(update_ref, out_ref):
    def step(i, carry):
        terms = update_ref[i, BLOCK:].astype(F32)
        gate = terms[0:1] + terms[1:2] + terms[2:3]
        carry = gate * carry + update_ref[i, :BLOCK].astype(F32)
        out_ref[i] = carry.astype(BF)
        return carry

    lax.fori_loop(0, SEG, step, jnp.zeros((BLOCK, HS), F32), unroll=8)


def scan(update):
    return pl.pallas_call(
        scan_kernel,
        in_specs=[VMEM],
        out_specs=VMEM,
        out_shape=pltpu.VMEM((SEG, BLOCK, HS), BF),
        compiler_params=PARAMS,
        cost_estimate=cost(2 * SEG * BLOCK * HS, 4 * SEG * BLOCK * HS),
    )(here(update))


def place_kernel(own_ref, other_ref, out_ref, sems):
    core, _ = position()
    pairs = []
    for batch, (ref, half) in enumerate(((own_ref, core), (other_ref, 1 - core))):
        for j in range(HEADS // 2):
            cols = pl.ds(pl.multiple_of(half * HALF + j * HS, HS), HS)
            pairs.append((ref.at[batch, j], out_ref.at[:, cols]))
    run_copies(pairs, sems)


def place(own, other):
    return pl.pallas_call(
        place_kernel,
        in_specs=[VMEM, VMEM],
        out_specs=ANY,
        out_shape=jax.ShapeDtypeStruct((S, HD), BF),
        scratch_shapes=[pltpu.SemaphoreType.DMA((HEADS,))],
        compiler_params=PARAMS,
        cost_estimate=cost(0, 4 * S * HD),
    )(here(own), here(other))


def spread(value):
    return lax.all_to_all(value, "seg", 0, 0, tiled=True)


def body(tokens, w_kv, q_state, decay):
    to_far, to_sib, to_sib_k, to_sib_v = sort_inputs(tokens[0], q_state, w_kv)
    sib_w = send(to_sib_k, SIB), send(to_sib_v, SIB)
    sib = send(to_sib, SIB)
    own_w = cut_weights(w_kv, to_sib)
    met, queries = join(send(to_far, OUT), to_sib, sib, own_w[0])
    away = [met, send(met, SIB)]
    queries = send(queries, OUT)

    first, second = project(away, own_w, sib_w, (0,), BF)
    far_k = send(first, BACK), send(second, OUT)
    first, second = project(away, own_w, sib_w, (1,), BF, (first,))
    far_v = send(first, BACK), send(second, OUT)
    near = project([to_sib, sib], own_w, sib_w, (0, 1), F32, (queries,))
    weights = weigh(near, far_k, (to_sib, sib, queries))
    states = spread(scan(spread(updates(weights, near, far_v, decay))))
    other = send(states, SIB)
    shape = (2, HEADS // 2, S, HS)
    return place(states.reshape(shape), other.reshape(shape))[None, None]


def solution(mesh):
    return jax.shard_map(
        body,
        mesh=mesh,
        in_specs=(P("fsdp", "seg", None), P("fsdp", None), P("fsdp", None), P("seg", None)),
        out_specs=P("fsdp", "seg", None, None),
        check_vma=False,
    )
```

time: 124 us -> 120 us (0.968)
  starting transfers between devices: 19.6 us -> 16.6 us
  Pallas kernels: 16.1 us -> 13.9 us
  blocking collectives: 75.6 us -> 77.5 us
    pallas_call x3, Pallas kernels: 10.1 us -> 5.11 us  [project(): pl.pallas_call(functools.partial(project_kernel, rows=rows, extra=len(aft...]
    ppermute x14 -> x11, starting transfers between devices: 19.6 us -> 16.6 us  [send(): return lax.ppermute(value, BOTH, pairs)]
    pallas_call x2 -> x5, Pallas kernels: 4.51 us -> 7.42 us  [the longest x1 2.67 us: sort_inputs(): pl.pallas_call(sort_kernel, in_specs=[HBM] * 3, out_specs=[VMEM] * 4, out...]
    all_to_all x2, blocking collectives: 75.6 us -> 77.5 us  [spread(): return lax.all_to_all(value, 'seg', 0, 0, tiled=True)]
    ppermute x14 -> x11, waiting for transfers between devices: 11.8 us -> 11.4 us  [send(): return lax.ppermute(value, BOTH, pairs)]
  transfers between devices with their start and end apart: 14 -> 11, of which waited for: 5 -> 4; matrix products, arithmetic and copies ran while one was open for 0% -> 0% of each run, Pallas kernels for 8% -> 8%
where the time goes in v4:
time: 120 us
  blocking collectives  77.5 us (65%)
  starting transfers between devices  16.6 us (14%)
  Pallas kernels  13.9 us (12%)
  waiting for transfers between devices  11.4 us (10%)
    all_to_all x2, blocking collectives, spread(): return lax.all_to_all(value, 'seg', 0, 0, tiled=True)  77.5 us
    ppermute x11, starting transfers between devices, send(): return lax.ppermute(value, BOTH, pairs)  16.6 us
    ppermute x11, waiting for transfers between devices, send(): return lax.ppermute(value, BOTH, pairs)  11.4 us
    pallas_call x3, Pallas kernels, project(): pl.pallas_call(functools.partial(project_kernel, rows=rows, extra=len(aft...  5.11 us
    pallas_call x1, Pallas kernels, sort_inputs(): pl.pallas_call(sort_kernel, in_specs=[HBM] * 3, out_specs=[VMEM] * 4, out...  2.67 us
  transfers between devices with their start and end apart: 11, of which 4 were waited for; matrix products, arithmetic and copies ran while one was open for 0% of the time, Pallas kernels for 8%

profile of v4, /device:TPU:1, one launch (start us, length us, event | category | flops | bytes accessed | tf_op | source)
XLA Modules:
  0.0 119.7 jit_solution(12347054276236486063)
XLA Ops:
  0.0 2.7 %shard_map.46 = (bf16[128,2048]{1,0:T(8,128)(2,1)S(1)}, bf16[192,2048]{1,0:T(8,128)(2,1)S(1)}, bf16[1024,1024]{1,0:T(8,128)(2,1)S(1)}, bf16[1024,1024]{1,0:T(8,128)(2,1)S(1)}) custom-call(bf16[128,4096]{1,0:T(8,128)(2,1)} %bitcast.6, bf16[64,2048]{1,0:T(8,128)(2,1)} %q_ref.1, bf16[1024,4096]{1,0:T(8,128)(2,1)} %w_ref.3), custom_call_target="tpu_custom_call" | custom-call | bytes 12582912 | tf_op jit(solution)/shard_map/pallas_call | solution.py:124
  2.7 3.3 %collective-permute-start.1 = (bf16[1024,1024]{1,0:T(8,128)(2,1)S(1)}, bf16[1024,1024]{1,0:T(8,128)(2,1)S(1)}, u32[]{:S(2)}, u32[]{:S(2)}) collective-permute-start(bf16[1024,1024]{1,0:T(8,128)(2,1)S(1)} %get-tuple-element.22), channel_id=1, source_target_pairs={{0,1},{1,0},{4,5},{5,4},{8,9},{9,8},{12,13},{13,12},{16,17},{17,16... | collective-permute-start | bytes 6291464 | tf_op jit(solution)/shard_map/ppermute | solution.py:43
  6.0 0.1 collective-permute-start.2
  6.1 0.4 collective-permute-start
  6.5 1.0 collective-permute-start.3
  7.5 2.2 %shard_map.47 = (bf16[1024,1024]{1,0:T(8,128)(2,1)S(1)}, bf16[1024,1024]{1,0:T(8,128)(2,1)S(1)}) custom-call(bf16[1024,4096]{1,0:T(8,128)(2,1)} %w_ref.3, bf16[192,2048]{1,0:T(8,128)(2,1)S(1)} %get-tuple-element.19.after_ref.own_ref.refs_0_), custom_call_target="tpu_custom_call" | custom-call | bytes 8388608 | tf_op jit(solution)/shard_map/pallas_call | solution.py:168
  9.8 5.1 %collective-permute-done.3.far_ref = bf16[128,2048]{1,0:T(8,128)(2,1)S(1)} collective-permute-done((bf16[128,2048]{1,0:T(8,128)(2,1)S(1)}, bf16[128,2048]{1,0:T(8,128)(2,1)S(1)}, u32[]{:S(2)}, u32[]{:S(2)}) %collective-permute-start.3) | collective-permute-done | bytes 524320 | tf_op jit(solution)/shard_map/ppermute | solution.py:43
  14.8 0.0 collective-permute-done.sib_ref.refs_1_
  14.8 0.1 shard_map.48
  15.0 2.3 %collective-permute-start.5 = (bf16[128,2048]{1,0:T(8,128)(2,1)S(1)}, bf16[128,2048]{1,0:T(8,128)(2,1)S(1)}, u32[]{:S(2)}, u32[]{:S(2)}) collective-permute-start(bf16[128,2048]{1,0:T(8,128)(2,1)S(1)} %get-tuple-element.28.refs_0_), channel_id=1, source_target_pairs={{0,1},{1,0},{4,5},{5,4},{8,9},{9,8},{12,13},{13,12},{16,17},{17,16... | collective-permute-start | bytes 1572872 | tf_op jit(solution)/shard_map/ppermute | solution.py:43
  17.2 0.0 collective-permute-start.4
  17.2 1.5 %collective-permute-done.5.refs_1_ = bf16[128,2048]{1,0:T(8,128)(2,1)S(1)} collective-permute-done((bf16[128,2048]{1,0:T(8,128)(2,1)S(1)}, bf16[128,2048]{1,0:T(8,128)(2,1)S(1)}, u32[]{:S(2)}, u32[]{:S(2)}) %collective-permute-start.5) | collective-permute-done | bytes 524320 | tf_op jit(solution)/shard_map/ppermute | solution.py:43
  18.8 0.0 collective-permute-done.1.refs_4_.refs_3_
  18.8 1.3 %shard_map.50 = (bf16[128,1024]{1,0:T(8,128)(2,1)S(1)}, bf16[128,1024]{1,0:T(8,128)(2,1)S(1)}) custom-call(bf16[128,2048]{1,0:T(8,128)(2,1)S(1)} %get-tuple-element.28.refs_0_, bf16[128,2048]{1,0:T(8,128)(2,1)S(1)} %collective-permute-done.5.refs_1_, bf16[1024,1024]{1,0:T(8,128)(2,1)S(1)} %get-tuple-element.20.after_ref.refs_2_, ...), custom_call_target="tpu_custom_call" | custom-call | flops 1073741824 | bytes 8388608 | tf_op jit(solution)/shard_map/pallas_call | solution.py:203
  20.1 0.1 collective-permute-start.6
  20.2 2.7 %collective-permute-start.7 = (bf16[128,1024]{1,0:T(8,128)(2,1)S(1)}, bf16[128,1024]{1,0:T(8,128)(2,1)S(1)}, u32[]{:S(2)}, u32[]{:S(2)}) collective-permute-start(bf16[128,1024]{1,0:T(8,128)(2,1)S(1)} %get-tuple-element.30), channel_id=1, source_target_pairs={{0,2},{1,131},{4,6},{5,135},{8,10},{9,139},{12,14},{13,143},{16,18... | collective-permute-start | bytes 786440 | tf_op jit(solution)/shard_map/ppermute | solution.py:43
  22.9 0.0 collective-permute-done.2.refs_5_.refs_3_
  22.9 1.3 %shard_map.52 = (bf16[128,1024]{1,0:T(8,128)(2,1)S(1)}, bf16[128,1024]{1,0:T(8,128)(2,1)S(1)}) custom-call(bf16[128,2048]{1,0:T(8,128)(2,1)S(1)} %get-tuple-element.28.refs_0_, bf16[128,2048]{1,0:T(8,128)(2,1)S(1)} %collective-permute-done.5.refs_1_, bf16[1024,1024]{1,0:T(8,128)(2,1)S(1)} %get-tuple-element.21.refs_3_.refs_2_, ...), custom_call_target="tpu_custom_call" | custom-call | flops 1073741824 | bytes 8388608 | tf_op jit(solution)/shard_map/pallas_call | solution.py:203
  24.2 0.1 collective-permute-start.8
  24.3 2.7 %collective-permute-start.9 = (bf16[128,1024]{1,0:T(8,128)(2,1)S(1)}, bf16[128,1024]{1,0:T(8,128)(2,1)S(1)}, u32[]{:S(2)}, u32[]{:S(2)}) collective-permute-start(bf16[128,1024]{1,0:T(8,128)(2,1)S(1)} %get-tuple-element.32), channel_id=1, source_target_pairs={{0,2},{1,131},{4,6},{5,135},{8,10},{9,139},{12,14},{13,143},{16,18... | collective-permute-start | bytes 786440 | tf_op jit(solution)/shard_map/ppermute | solution.py:43
  27.0 0.0 collective-permute-done.4.refs_6_.q_far
  27.0 2.4 %shard_map.49 = (f32[128,2048]{1,0:T(8,128)S(1)}, f32[128,2048]{1,0:T(8,128)S(1)}) custom-call(bf16[192,2048]{1,0:T(8,128)(2,1)S(1)} %get-tuple-element.19.after_ref.own_ref.refs_0_, bf16[192,2048]{1,0:T(8,128)(2,1)S(1)} %collective-permute-done.sib_ref.refs_1_, bf16[1024,1024]{1,0:T(8,128)(2,1)S(1)} %get-tuple-element.20.after_ref.refs_2_, ...), custom_call_target="tpu_custom_call" | custom-call | flops 2147483648 | bytes 16777216 | tf_op jit(solution)/shard_map/pallas_call | solution.py:203
  29.4 0.0 collective-permute-done.6.far0
  29.4 0.0 collective-permute-done.7.far1
  29.4 0.0 copy-start
  29.4 2.0 %shard_map.51.weights_ref = bf16[16,256,128]{2,1,0:T(8,128)(2,1)S(1)} custom-call(f32[128,2048]{1,0:T(8,128)S(1)} %get-tuple-element.26.near0, f32[128,2048]{1,0:T(8,128)S(1)} %get-tuple-element.27.near1, bf16[128,1024]{1,0:T(8,128)(2,1)S(1)} %collective-permute-done.6.far0, bf16[128,1024]{1,0:T(8,128)(2,1)S(1)} %collective-permute-done.7.far1, ...), custom_call_target="tpu_custom_call" | custom-call | flops 134217728 | bytes 4194304 | tf_op jit(solution)/shard_map/pallas_call | solution.py:233
  31.4 2.5 %collective-permute-done.8.far0 = bf16[128,1024]{1,0:T(8,128)(2,1)S(1)} collective-permute-done((bf16[128,1024]{1,0:T(8,128)(2,1)S(1)}, bf16[128,1024]{1,0:T(8,128)(2,1)S(1)}, u32[]{:S(2)}, u32[]{:S(2)}) %collective-permute-start.8) | collective-permute-done | bytes 262176 | tf_op jit(solution)/shard_map/ppermute | solution.py:43
  33.9 0.0 collective-permute-done.9.far1
  33.9 0.0 copy-done
  33.9 0.5 shard_map.53
  34.4 42.6 %all_to_all.10.update_ref = bf16[64,72,128]{2,1,0:T(8,128)(2,1)S(1)} all-to-all(bf16[64,72,128]{2,1,0:T(8,128)(2,1)S(1)} %shard_map.53), channel_id=1, replica_groups=mesh['seg'=64,'fsdp'=4] {'seg'}, dimensions={0} | all-to-all | bytes 2359296 | tf_op jit(solution)/shard_map/all_to_all | solution.py:322
  76.9 0.3 shard_map.54
  77.3 34.9 %all_to_all.11 = bf16[64,64,128]{2,1,0:T(8,128)(2,1)S(1)} all-to-all(bf16[64,64,128]{2,1,0:T(8,128)(2,1)S(1)} %shard_map.54), channel_id=1, replica_groups=mesh['seg'=64,'fsdp'=4] {'seg'}, dimensions={0} | all-to-all | bytes 2097152 | tf_op jit(solution)/shard_map/all_to_all | solution.py:322
  112.2 4.0 %collective-permute-start.10 = (bf16[64,64,128]{2,1,0:T(8,128)(2,1)S(1)}, bf16[64,64,128]{2,1,0:T(8,128)(2,1)S(1)}, u32[]{:S(2)}, u32[]{:S(2)}) collective-permute-start(bf16[64,64,128]{2,1,0:T(8,128)(2,1)S(1)} %all_to_all.11), channel_id=1, source_target_pairs={{0,1},{1,0},{4,5},{5,4},{8,9},{9,8},{12,13},{13,12},{16,17},{17,16... | collective-permute-start | bytes 3145736 | tf_op jit(solution)/shard_map/ppermute | solution.py:43
  116.1 2.3 %collective-permute-done.10 = bf16[64,64,128]{2,1,0:T(8,128)(2,1)S(1)} collective-permute-done((bf16[64,64,128]{2,1,0:T(8,128)(2,1)S(1)}, bf16[64,64,128]{2,1,0:T(8,128)(2,1)S(1)}, u32[]{:S(2)}, u32[]{:S(2)}) %collective-permute-start.10) | collective-permute-done | bytes 1048608 | tf_op jit(solution)/shard_map/ppermute | solution.py:43
  118.4 1.1 shard_map.55
Async XLA Ops:
  2.7 16.1 %collective-permute-start.1 = (bf16[1024,1024]{1,0:T(8,128)(2,1)S(1)}, bf16[1024,1024]{1,0:T(8,128)(2,1)S(1)}, u32[]{:S(2)}, u32[]{:S(2)}) collective-permute-start(bf16[1024,1024]{1,0:T(8,128)(2,1)S(1)} %get-tuple-element.22), channel_id=1, source_target_pairs={{0,1},{1,0},{4,5},{5,4},{8,9},{9,8},{12,13},{13,12},{16,17},{17,16... | collective-permute-start | bytes 6291464 | tf_op jit(solution)/shard_map/ppermute | solution.py:43
  6.0 16.9 %collective-permute-start.2 = (bf16[1024,1024]{1,0:T(8,128)(2,1)S(1)}, bf16[1024,1024]{1,0:T(8,128)(2,1)S(1)}, u32[]{:S(2)}, u32[]{:S(2)}) collective-permute-start(bf16[1024,1024]{1,0:T(8,128)(2,1)S(1)} %get-tuple-element.23), channel_id=1, source_target_pairs={{0,1},{1,0},{4,5},{5,4},{8,9},{9,8},{12,13},{13,12},{16,17},{17,16... | collective-permute-start | bytes 6291464 | tf_op jit(solution)/shard_map/ppermute | solution.py:43
  6.1 8.7 %collective-permute-start = (bf16[192,2048]{1,0:T(8,128)(2,1)S(1)}, bf16[192,2048]{1,0:T(8,128)(2,1)S(1)}, u32[]{:S(2)}, u32[]{:S(2)}) collective-permute-start(bf16[192,2048]{1,0:T(8,128)(2,1)S(1)} %get-tuple-element.19.after_ref.own_ref.refs_0_), channel_id=1, source_target_pairs={{0,1},{1,0},{4,5},{5,4},{8,9},{9,8},{12,13},{13,12},{16,17},{17,16... | collective-permute-start | bytes 2359304 | tf_op jit(solution)/shard_map/ppermute | solution.py:43
  6.5 8.3 %collective-permute-start.3 = (bf16[128,2048]{1,0:T(8,128)(2,1)S(1)}, bf16[128,2048]{1,0:T(8,128)(2,1)S(1)}, u32[]{:S(2)}, u32[]{:S(2)}) collective-permute-start(bf16[128,2048]{1,0:T(8,128)(2,1)S(1)} %get-tuple-element.24), channel_id=1, source_target_pairs={{0,2},{1,131},{4,6},{5,135},{8,10},{9,139},{12,14},{13,143},{16,18... | collective-permute-start | bytes 1572872 | tf_op jit(solution)/shard_map/ppermute | solution.py:43
  15.0 3.8 %collective-permute-start.5 = (bf16[128,2048]{1,0:T(8,128)(2,1)S(1)}, bf16[128,2048]{1,0:T(8,128)(2,1)S(1)}, u32[]{:S(2)}, u32[]{:S(2)}) collective-permute-start(bf16[128,2048]{1,0:T(8,128)(2,1)S(1)} %get-tuple-element.28.refs_0_), channel_id=1, source_target_pairs={{0,1},{1,0},{4,5},{5,4},{8,9},{9,8},{12,13},{13,12},{16,17},{17,16... | collective-permute-start | bytes 1572872 | tf_op jit(solution)/shard_map/ppermute | solution.py:43
  17.2 9.8 %collective-permute-start.4 = (bf16[128,1024]{1,0:T(8,128)(2,1)S(1)}, bf16[128,1024]{1,0:T(8,128)(2,1)S(1)}, u32[]{:S(2)}, u32[]{:S(2)}) collective-permute-start(bf16[128,1024]{1,0:T(8,128)(2,1)S(1)} %get-tuple-element.25), channel_id=1, source_target_pairs={{0,2},{1,131},{4,6},{5,135},{8,10},{9,139},{12,14},{13,143},{16,18... | collective-permute-start | bytes 786440 | tf_op jit(solution)/shard_map/ppermute | solution.py:43
  20.1 9.3 %collective-permute-start.6 = (bf16[128,1024]{1,0:T(8,128)(2,1)S(1)}, bf16[128,1024]{1,0:T(8,128)(2,1)S(1)}, u32[]{:S(2)}, u32[]{:S(2)}) collective-permute-start(bf16[128,1024]{1,0:T(8,128)(2,1)S(1)} %get-tuple-element.29.refs_4_), channel_id=1, source_target_pairs={{0,130},{1,3},{4,134},{5,7},{8,138},{9,11},{12,142},{13,15},{16,14... | collective-permute-start | bytes 786440 | tf_op jit(solution)/shard_map/ppermute | solution.py:43
  20.2 9.2 %collective-permute-start.7 = (bf16[128,1024]{1,0:T(8,128)(2,1)S(1)}, bf16[128,1024]{1,0:T(8,128)(2,1)S(1)}, u32[]{:S(2)}, u32[]{:S(2)}) collective-permute-start(bf16[128,1024]{1,0:T(8,128)(2,1)S(1)} %get-tuple-element.30), channel_id=1, source_target_pairs={{0,2},{1,131},{4,6},{5,135},{8,10},{9,139},{12,14},{13,143},{16,18... | collective-permute-start | bytes 786440 | tf_op jit(solution)/shard_map/ppermute | solution.py:43
  24.2 9.7 %collective-permute-start.8 = (bf16[128,1024]{1,0:T(8,128)(2,1)S(1)}, bf16[128,1024]{1,0:T(8,128)(2,1)S(1)}, u32[]{:S(2)}, u32[]{:S(2)}) collective-permute-start(bf16[128,1024]{1,0:T(8,128)(2,1)S(1)} %get-tuple-element.31), channel_id=1, source_target_pairs={{0,130},{1,3},{4,134},{5,7},{8,138},{9,11},{12,142},{13,15},{16,14... | collective-permute-start | bytes 786440 | tf_op jit(solution)/shard_map/ppermute | solution.py:43
  24.3 9.6 %collective-permute-start.9 = (bf16[128,1024]{1,0:T(8,128)(2,1)S(1)}, bf16[128,1024]{1,0:T(8,128)(2,1)S(1)}, u32[]{:S(2)}, u32[]{:S(2)}) collective-permute-start(bf16[128,1024]{1,0:T(8,128)(2,1)S(1)} %get-tuple-element.32), channel_id=1, source_target_pairs={{0,2},{1,131},{4,6},{5,135},{8,10},{9,139},{12,14},{13,143},{16,18... | collective-permute-start | bytes 786440 | tf_op jit(solution)/shard_map/ppermute | solution.py:43
  29.4 4.5 %copy-start = (f32[1,2048]{1,0:T(1,128)S(1)}, f32[1,2048]{1,0:T(1,128)}, u32[]{:S(2)}) copy-start(f32[1,2048]{1,0:T(1,128)} %gate_ref.1) | copy-start | bytes 24580
  112.2 6.3 %collective-permute-start.10 = (bf16[64,64,128]{2,1,0:T(8,128)(2,1)S(1)}, bf16[64,64,128]{2,1,0:T(8,128)(2,1)S(1)}, u32[]{:S(2)}, u32[]{:S(2)}) collective-permute-start(bf16[64,64,128]{2,1,0:T(8,128)(2,1)S(1)} %all_to_all.11), channel_id=1, source_target_pairs={{0,1},{1,0},{4,5},{5,4},{8,9},{9,8},{12,13},{13,12},{16,17},{17,16... | collective-permute-start | bytes 3145736 | tf_op jit(solution)/shard_map/ppermute | solution.py:43

commit v5 on v4

--- a/solution.py
+++ b/solution.py
@@ -274,15 +274,17 @@
     )(*args)
 
 
+ORDER = [seg for z in range(8) for seg in range(z, SEG, 8)]
+
+
 def scan_kernel(update_ref, out_ref):
-    def step(i, carry):
+    carry = jnp.zeros((BLOCK, HS), F32)
+    for seg in range(SEG):
+        i = ORDER.index(seg)
         terms = update_ref[i, BLOCK:].astype(F32)
         gate = terms[0:1] + terms[1:2] + terms[2:3]
         carry = gate * carry + update_ref[i, :BLOCK].astype(F32)
         out_ref[i] = carry.astype(BF)
-        return carry
-
-    lax.fori_loop(0, SEG, step, jnp.zeros((BLOCK, HS), F32), unroll=8)
 
 
 def scan(update):
@@ -296,30 +298,49 @@
     )(here(update))
 
 
-def place_kernel(own_ref, other_ref, out_ref, sems):
-    core, _ = position()
+def half_kernel(states_ref, out_ref, sems):
+    run_copies([(states_ref.at[HEADS // 2 * (S // BLOCK) :], out_ref)], sems)
+
+
+def other_half(states):
+    return pl.pallas_call(
+        half_kernel,
+        in_specs=[ANY],
+        out_specs=VMEM,
+        out_shape=pltpu.VMEM((SEG // 2, BLOCK, HS), BF),
+        scratch_shapes=[pltpu.SemaphoreType.DMA((1,))],
+        compiler_params=PARAMS,
+        cost_estimate=cost(0, 1 << 20),
+    )(states)
+
+
+def place_kernel(states_ref, *refs, own):
+    out_ref, sems = refs[-2:]
+    core, _ = position()
+    half = core if own else 1 - core
     pairs = []
-    for batch, (ref, half) in enumerate(((own_ref, core), (other_ref, 1 - core))):
-        for j in range(HEADS // 2):
-            cols = pl.ds(pl.multiple_of(half * HALF + j * HS, HS), HS)
-            pairs.append((ref.at[batch, j], out_ref.at[:, cols]))
+    for j in range(HEADS // 2):
+        cols = pl.ds(pl.multiple_of(half * HALF + j * HS, HS), HS)
+        pairs.append((states_ref.at[j], out_ref.at[:, cols]))
     run_copies(pairs, sems)
 
 
-def place(own, other):
-    return pl.pallas_call(
-        place_kernel,
-        in_specs=[VMEM, VMEM],
+def place(states, out):
+    first = out is None
+    return pl.pallas_call(
+        functools.partial(place_kernel, own=first),
+        in_specs=[VMEM] if first else [VMEM, ANY],
         out_specs=ANY,
         out_shape=jax.ShapeDtypeStruct((S, HD), BF),
-        scratch_shapes=[pltpu.SemaphoreType.DMA((HEADS,))],
-        compiler_params=PARAMS,
-        cost_estimate=cost(0, 4 * S * HD),
-    )(here(own), here(other))
+        input_output_aliases={} if first else {1: 0},
+        scratch_shapes=[pltpu.SemaphoreType.DMA((HEADS // 2,))],
+        compiler_params=PARAMS,
+        cost_estimate=cost(0, 2 * S * HD),
+    )(*([states] if first else [states, out]))
 
 
 def spread(value):
-    return lax.all_to_all(value, "seg", 0, 0, tiled=True)
+    return lax.all_to_all(value, "seg", 0, 0, tiled=True, axis_index_groups=[ORDER])
 
 
 def body(tokens, w_kv, q_state, decay):
@@ -338,9 +359,9 @@
     near = project([to_sib, sib], own_w, sib_w, (0, 1), F32, (queries,))
     weights = weigh(near, far_k, (to_sib, sib, queries))
     states = spread(scan(spread(updates(weights, near, far_v, decay))))
-    other = send(states, SIB)
-    shape = (2, HEADS // 2, S, HS)
-    return place(states.reshape(shape), other.reshape(shape))[None, None]
+    other = send(other_half(states), SIB)
+    out = place(states.reshape(HEADS, S, HS), None)
+    return place(other.reshape(HEADS // 2, S, HS), out)[None, None]
 
 
 def solution(mesh):

time: 120 us -> 118 us (0.983)
  waiting for transfers between devices: 11.4 us -> 9.82 us
  blocking collectives: 77.5 us -> 76 us
    ppermute x11, waiting for transfers between devices: 11.4 us -> 9.82 us  [send(): return lax.ppermute(value, BOTH, pairs)]
    all_to_all x2, blocking collectives: 77.5 us -> 76 us  [spread(): lax.all_to_all(value, 'seg', 0, 0, tiled=True, axis_index_groups=[ORDER])]
  transfers between devices with their start and end apart: 11 -> 11, of which waited for: 4 -> 4; matrix products, arithmetic and copies ran while one was open for 0% -> 0% of each run, Pallas kernels for 8% -> 9%
where the time goes in v5:
time: 118 us
  blocking collectives  76 us (64%)
  starting transfers between devices  17 us (14%)
  Pallas kernels  14.6 us (12%)
  waiting for transfers between devices  9.82 us (8%)
    all_to_all x2, blocking collectives, spread(): lax.all_to_all(value, 'seg', 0, 0, tiled=True, axis_index_groups=[ORDER])  76 us
    ppermute x11, starting transfers between devices, send(): return lax.ppermute(value, BOTH, pairs)  17 us
    ppermute x11, waiting for transfers between devices, send(): return lax.ppermute(value, BOTH, pairs)  9.82 us
    pallas_call x3, Pallas kernels, project(): pl.pallas_call(functools.partial(project_kernel, rows=rows, extra=len(aft...  5.11 us
    pallas_call x1, Pallas kernels, sort_inputs(): pl.pallas_call(sort_kernel, in_specs=[HBM] * 3, out_specs=[VMEM] * 4, out...  2.67 us
  transfers between devices with their start and end apart: 11, of which 4 were waited for; matrix products, arithmetic and copies ran while one was open for 0% of the time, Pallas kernels for 9%

profile of v5, /device:TPU:1, one launch (start us, length us, event | category | flops | bytes accessed | tf_op | source)
XLA Modules:
  0.0 117.7 jit_solution(3808751617444885014)
XLA Ops:
  0.0 2.7 %shard_map.46 = (bf16[128,2048]{1,0:T(8,128)(2,1)S(1)}, bf16[192,2048]{1,0:T(8,128)(2,1)S(1)}, bf16[1024,1024]{1,0:T(8,128)(2,1)S(1)}, bf16[1024,1024]{1,0:T(8,128)(2,1)S(1)}) custom-call(bf16[128,4096]{1,0:T(8,128)(2,1)} %bitcast.6, bf16[64,2048]{1,0:T(8,128)(2,1)} %q_ref.1, bf16[1024,4096]{1,0:T(8,128)(2,1)} %w_ref.3), custom_call_target="tpu_custom_call" | custom-call | bytes 12582912 | tf_op jit(solution)/shard_map/pallas_call | solution.py:124
  2.7 3.3 %collective-permute-start.1 = (bf16[1024,1024]{1,0:T(8,128)(2,1)S(1)}, bf16[1024,1024]{1,0:T(8,128)(2,1)S(1)}, u32[]{:S(2)}, u32[]{:S(2)}) collective-permute-start(bf16[1024,1024]{1,0:T(8,128)(2,1)S(1)} %get-tuple-element.22), channel_id=1, source_target_pairs={{0,1},{1,0},{4,5},{5,4},{8,9},{9,8},{12,13},{13,12},{16,17},{17,16... | collective-permute-start | bytes 6291464 | tf_op jit(solution)/shard_map/ppermute | solution.py:43
  6.0 0.1 collective-permute-start.2
  6.1 0.4 collective-permute-start
  6.5 1.0 collective-permute-start.3
  7.5 2.2 %shard_map.47 = (bf16[1024,1024]{1,0:T(8,128)(2,1)S(1)}, bf16[1024,1024]{1,0:T(8,128)(2,1)S(1)}) custom-call(bf16[1024,4096]{1,0:T(8,128)(2,1)} %w_ref.3, bf16[192,2048]{1,0:T(8,128)(2,1)S(1)} %get-tuple-element.19.after_ref.own_ref.refs_0_), custom_call_target="tpu_custom_call" | custom-call | bytes 8388608 | tf_op jit(solution)/shard_map/pallas_call | solution.py:168
  9.8 5.1 %collective-permute-done.3.far_ref = bf16[128,2048]{1,0:T(8,128)(2,1)S(1)} collective-permute-done((bf16[128,2048]{1,0:T(8,128)(2,1)S(1)}, bf16[128,2048]{1,0:T(8,128)(2,1)S(1)}, u32[]{:S(2)}, u32[]{:S(2)}) %collective-permute-start.3) | collective-permute-done | bytes 524320 | tf_op jit(solution)/shard_map/ppermute | solution.py:43
  14.8 0.0 collective-permute-done.sib_ref.refs_1_
  14.8 0.1 shard_map.48
  15.0 2.3 %collective-permute-start.5 = (bf16[128,2048]{1,0:T(8,128)(2,1)S(1)}, bf16[128,2048]{1,0:T(8,128)(2,1)S(1)}, u32[]{:S(2)}, u32[]{:S(2)}) collective-permute-start(bf16[128,2048]{1,0:T(8,128)(2,1)S(1)} %get-tuple-element.28.refs_0_), channel_id=1, source_target_pairs={{0,1},{1,0},{4,5},{5,4},{8,9},{9,8},{12,13},{13,12},{16,17},{17,16... | collective-permute-start | bytes 1572872 | tf_op jit(solution)/shard_map/ppermute | solution.py:43
  17.2 0.0 collective-permute-start.4
  17.2 1.5 %collective-permute-done.5.refs_1_ = bf16[128,2048]{1,0:T(8,128)(2,1)S(1)} collective-permute-done((bf16[128,2048]{1,0:T(8,128)(2,1)S(1)}, bf16[128,2048]{1,0:T(8,128)(2,1)S(1)}, u32[]{:S(2)}, u32[]{:S(2)}) %collective-permute-start.5) | collective-permute-done | bytes 524320 | tf_op jit(solution)/shard_map/ppermute | solution.py:43
  18.8 0.0 collective-permute-done.1.refs_4_.refs_3_
  18.8 1.3 %shard_map.50 = (bf16[128,1024]{1,0:T(8,128)(2,1)S(1)}, bf16[128,1024]{1,0:T(8,128)(2,1)S(1)}) custom-call(bf16[128,2048]{1,0:T(8,128)(2,1)S(1)} %get-tuple-element.28.refs_0_, bf16[128,2048]{1,0:T(8,128)(2,1)S(1)} %collective-permute-done.5.refs_1_, bf16[1024,1024]{1,0:T(8,128)(2,1)S(1)} %get-tuple-element.20.after_ref.refs_2_, ...), custom_call_target="tpu_custom_call" | custom-call | flops 1073741824 | bytes 8388608 | tf_op jit(solution)/shard_map/pallas_call | solution.py:203
  20.1 0.1 collective-permute-start.6
  20.2 2.7 %collective-permute-start.7 = (bf16[128,1024]{1,0:T(8,128)(2,1)S(1)}, bf16[128,1024]{1,0:T(8,128)(2,1)S(1)}, u32[]{:S(2)}, u32[]{:S(2)}) collective-permute-start(bf16[128,1024]{1,0:T(8,128)(2,1)S(1)} %get-tuple-element.30), channel_id=1, source_target_pairs={{0,2},{1,131},{4,6},{5,135},{8,10},{9,139},{12,14},{13,143},{16,18... | collective-permute-start | bytes 786440 | tf_op jit(solution)/shard_map/ppermute | solution.py:43
  22.9 0.0 collective-permute-done.2.refs_5_.refs_3_
  22.9 1.3 %shard_map.52 = (bf16[128,1024]{1,0:T(8,128)(2,1)S(1)}, bf16[128,1024]{1,0:T(8,128)(2,1)S(1)}) custom-call(bf16[128,2048]{1,0:T(8,128)(2,1)S(1)} %get-tuple-element.28.refs_0_, bf16[128,2048]{1,0:T(8,128)(2,1)S(1)} %collective-permute-done.5.refs_1_, bf16[1024,1024]{1,0:T(8,128)(2,1)S(1)} %get-tuple-element.21.refs_3_.refs_2_, ...), custom_call_target="tpu_custom_call" | custom-call | flops 1073741824 | bytes 8388608 | tf_op jit(solution)/shard_map/pallas_call | solution.py:203
  24.2 0.1 collective-permute-start.8
  24.3 2.7 %collective-permute-start.9 = (bf16[128,1024]{1,0:T(8,128)(2,1)S(1)}, bf16[128,1024]{1,0:T(8,128)(2,1)S(1)}, u32[]{:S(2)}, u32[]{:S(2)}) collective-permute-start(bf16[128,1024]{1,0:T(8,128)(2,1)S(1)} %get-tuple-element.32), channel_id=1, source_target_pairs={{0,2},{1,131},{4,6},{5,135},{8,10},{9,139},{12,14},{13,143},{16,18... | collective-permute-start | bytes 786440 | tf_op jit(solution)/shard_map/ppermute | solution.py:43
  27.0 0.0 collective-permute-done.4.refs_6_.q_far
  27.0 2.4 %shard_map.49 = (f32[128,2048]{1,0:T(8,128)S(1)}, f32[128,2048]{1,0:T(8,128)S(1)}) custom-call(bf16[192,2048]{1,0:T(8,128)(2,1)S(1)} %get-tuple-element.19.after_ref.own_ref.refs_0_, bf16[192,2048]{1,0:T(8,128)(2,1)S(1)} %collective-permute-done.sib_ref.refs_1_, bf16[1024,1024]{1,0:T(8,128)(2,1)S(1)} %get-tuple-element.20.after_ref.refs_2_, ...), custom_call_target="tpu_custom_call" | custom-call | flops 2147483648 | bytes 16777216 | tf_op jit(solution)/shard_map/pallas_call | solution.py:203
  29.4 0.0 collective-permute-done.6.far0
  29.4 0.0 collective-permute-done.7.far1
  29.4 0.0 copy-start
  29.4 2.0 %shard_map.51.weights_ref = bf16[16,256,128]{2,1,0:T(8,128)(2,1)S(1)} custom-call(f32[128,2048]{1,0:T(8,128)S(1)} %get-tuple-element.26.near0, f32[128,2048]{1,0:T(8,128)S(1)} %get-tuple-element.27.near1, bf16[128,1024]{1,0:T(8,128)(2,1)S(1)} %collective-permute-done.6.far0, bf16[128,1024]{1,0:T(8,128)(2,1)S(1)} %collective-permute-done.7.far1, ...), custom_call_target="tpu_custom_call" | custom-call | flops 134217728 | bytes 4194304 | tf_op jit(solution)/shard_map/pallas_call | solution.py:233
  31.4 2.5 %collective-permute-done.8.far0 = bf16[128,1024]{1,0:T(8,128)(2,1)S(1)} collective-permute-done((bf16[128,1024]{1,0:T(8,128)(2,1)S(1)}, bf16[128,1024]{1,0:T(8,128)(2,1)S(1)}, u32[]{:S(2)}, u32[]{:S(2)}) %collective-permute-start.8) | collective-permute-done | bytes 262176 | tf_op jit(solution)/shard_map/ppermute | solution.py:43
  33.9 0.0 collective-permute-done.9.far1
  33.9 0.0 copy-done
  33.9 0.5 shard_map.53
  34.4 41.5 %all_to_all.10.update_ref = bf16[64,72,128]{2,1,0:T(8,128)(2,1)S(1)} all-to-all(bf16[64,72,128]{2,1,0:T(8,128)(2,1)S(1)} %shard_map.53), channel_id=1, replica_groups={{0,32,64,96,128,160,192,224,4,36,68,100,132,164,196,228,8,40,72,104,136..., dimensions={0} | all-to-all | bytes 2359296 | tf_op jit(solution)/shard_map/all_to_all | solution.py:343
  75.8 0.3 shard_map.54
  76.1 34.5 %all_to_all.11.states_ref = bf16[64,64,128]{2,1,0:T(8,128)(2,1)S(1)} all-to-all(bf16[64,64,128]{2,1,0:T(8,128)(2,1)S(1)} %shard_map.54), channel_id=1, replica_groups={{0,32,64,96,128,160,192,224,4,36,68,100,132,164,196,228,8,40,72,104,136..., dimensions={0} | all-to-all | bytes 2097152 | tf_op jit(solution)/shard_map/all_to_all | solution.py:343
  110.7 4.4 %collective-permute-start.10 = (bf16[32,64,128]{2,1,0:T(8,128)(2,1)S(1)}, bf16[32,64,128]{2,1,0:T(8,128)(2,1)S(1)}, u32[]{:S(2)}, u32[]{:S(2)}) collective-permute-start(bf16[32,64,128]{2,1,0:T(8,128)(2,1)S(1)} %shard_map.55), channel_id=1, source_target_pairs={{0,1},{1,0},{4,5},{5,4},{8,9},{9,8},{12,13},{13,12},{16,17},{17,16... | collective-permute-start | bytes 1572872 | tf_op jit(solution)/shard_map/ppermute | solution.py:43
  115.1 0.8 shard_map.56.refs_0_
  116.0 0.7 collective-permute-done.10
  116.7 0.8 shard_map.57
  (1 shorter events, 0.0 us)
Async XLA Ops:
  2.7 16.1 %collective-permute-start.1 = (bf16[1024,1024]{1,0:T(8,128)(2,1)S(1)}, bf16[1024,1024]{1,0:T(8,128)(2,1)S(1)}, u32[]{:S(2)}, u32[]{:S(2)}) collective-permute-start(bf16[1024,1024]{1,0:T(8,128)(2,1)S(1)} %get-tuple-element.22), channel_id=1, source_target_pairs={{0,1},{1,0},{4,5},{5,4},{8,9},{9,8},{12,13},{13,12},{16,17},{17,16... | collective-permute-start | bytes 6291464 | tf_op jit(solution)/shard_map/ppermute | solution.py:43
  6.0 16.9 %collective-permute-start.2 = (bf16[1024,1024]{1,0:T(8,128)(2,1)S(1)}, bf16[1024,1024]{1,0:T(8,128)(2,1)S(1)}, u32[]{:S(2)}, u32[]{:S(2)}) collective-permute-start(bf16[1024,1024]{1,0:T(8,128)(2,1)S(1)} %get-tuple-element.23), channel_id=1, source_target_pairs={{0,1},{1,0},{4,5},{5,4},{8,9},{9,8},{12,13},{13,12},{16,17},{17,16... | collective-permute-start | bytes 6291464 | tf_op jit(solution)/shard_map/ppermute | solution.py:43
  6.1 8.7 %collective-permute-start = (bf16[192,2048]{1,0:T(8,128)(2,1)S(1)}, bf16[192,2048]{1,0:T(8,128)(2,1)S(1)}, u32[]{:S(2)}, u32[]{:S(2)}) collective-permute-start(bf16[192,2048]{1,0:T(8,128)(2,1)S(1)} %get-tuple-element.19.after_ref.own_ref.refs_0_), channel_id=1, source_target_pairs={{0,1},{1,0},{4,5},{5,4},{8,9},{9,8},{12,13},{13,12},{16,17},{17,16... | collective-permute-start | bytes 2359304 | tf_op jit(solution)/shard_map/ppermute | solution.py:43
  6.5 8.3 %collective-permute-start.3 = (bf16[128,2048]{1,0:T(8,128)(2,1)S(1)}, bf16[128,2048]{1,0:T(8,128)(2,1)S(1)}, u32[]{:S(2)}, u32[]{:S(2)}) collective-permute-start(bf16[128,2048]{1,0:T(8,128)(2,1)S(1)} %get-tuple-element.24), channel_id=1, source_target_pairs={{0,2},{1,131},{4,6},{5,135},{8,10},{9,139},{12,14},{13,143},{16,18... | collective-permute-start | bytes 1572872 | tf_op jit(solution)/shard_map/ppermute | solution.py:43
  15.0 3.8 %collective-permute-start.5 = (bf16[128,2048]{1,0:T(8,128)(2,1)S(1)}, bf16[128,2048]{1,0:T(8,128)(2,1)S(1)}, u32[]{:S(2)}, u32[]{:S(2)}) collective-permute-start(bf16[128,2048]{1,0:T(8,128)(2,1)S(1)} %get-tuple-element.28.refs_0_), channel_id=1, source_target_pairs={{0,1},{1,0},{4,5},{5,4},{8,9},{9,8},{12,13},{13,12},{16,17},{17,16... | collective-permute-start | bytes 1572872 | tf_op jit(solution)/shard_map/ppermute | solution.py:43
  17.2 9.8 %collective-permute-start.4 = (bf16[128,1024]{1,0:T(8,128)(2,1)S(1)}, bf16[128,1024]{1,0:T(8,128)(2,1)S(1)}, u32[]{:S(2)}, u32[]{:S(2)}) collective-permute-start(bf16[128,1024]{1,0:T(8,128)(2,1)S(1)} %get-tuple-element.25), channel_id=1, source_target_pairs={{0,2},{1,131},{4,6},{5,135},{8,10},{9,139},{12,14},{13,143},{16,18... | collective-permute-start | bytes 786440 | tf_op jit(solution)/shard_map/ppermute | solution.py:43
  20.1 9.3 %collective-permute-start.6 = (bf16[128,1024]{1,0:T(8,128)(2,1)S(1)}, bf16[128,1024]{1,0:T(8,128)(2,1)S(1)}, u32[]{:S(2)}, u32[]{:S(2)}) collective-permute-start(bf16[128,1024]{1,0:T(8,128)(2,1)S(1)} %get-tuple-element.29.refs_4_), channel_id=1, source_target_pairs={{0,130},{1,3},{4,134},{5,7},{8,138},{9,11},{12,142},{13,15},{16,14... | collective-permute-start | bytes 786440 | tf_op jit(solution)/shard_map/ppermute | solution.py:43
  20.2 9.2 %collective-permute-start.7 = (bf16[128,1024]{1,0:T(8,128)(2,1)S(1)}, bf16[128,1024]{1,0:T(8,128)(2,1)S(1)}, u32[]{:S(2)}, u32[]{:S(2)}) collective-permute-start(bf16[128,1024]{1,0:T(8,128)(2,1)S(1)} %get-tuple-element.30), channel_id=1, source_target_pairs={{0,2},{1,131},{4,6},{5,135},{8,10},{9,139},{12,14},{13,143},{16,18... | collective-permute-start | bytes 786440 | tf_op jit(solution)/shard_map/ppermute | solution.py:43
  24.2 9.7 %collective-permute-start.8 = (bf16[128,1024]{1,0:T(8,128)(2,1)S(1)}, bf16[128,1024]{1,0:T(8,128)(2,1)S(1)}, u32[]{:S(2)}, u32[]{:S(2)}) collective-permute-start(bf16[128,1024]{1,0:T(8,128)(2,1)S(1)} %get-tuple-element.31), channel_id=1, source_target_pairs={{0,130},{1,3},{4,134},{5,7},{8,138},{9,11},{12,142},{13,15},{16,14... | collective-permute-start | bytes 786440 | tf_op jit(solution)/shard_map/ppermute | solution.py:43
  24.3 9.6 %collective-permute-start.9 = (bf16[128,1024]{1,0:T(8,128)(2,1)S(1)}, bf16[128,1024]{1,0:T(8,128)(2,1)S(1)}, u32[]{:S(2)}, u32[]{:S(2)}) collective-permute-start(bf16[128,1024]{1,0:T(8,128)(2,1)S(1)} %get-tuple-element.32), channel_id=1, source_target_pairs={{0,2},{1,131},{4,6},{5,135},{8,10},{9,139},{12,14},{13,143},{16,18... | collective-permute-start | bytes 786440 | tf_op jit(solution)/shard_map/ppermute | solution.py:43
  29.4 4.5 %copy-start = (f32[1,2048]{1,0:T(1,128)S(1)}, f32[1,2048]{1,0:T(1,128)}, u32[]{:S(2)}) copy-start(f32[1,2048]{1,0:T(1,128)} %gate_ref.1) | copy-start | bytes 24580
  110.7 6.0 %collective-permute-start.10 = (bf16[32,64,128]{2,1,0:T(8,128)(2,1)S(1)}, bf16[32,64,128]{2,1,0:T(8,128)(2,1)S(1)}, u32[]{:S(2)}, u32[]{:S(2)}) collective-permute-start(bf16[32,64,128]{2,1,0:T(8,128)(2,1)S(1)} %shard_map.55), channel_id=1, source_target_pairs={{0,1},{1,0},{4,5},{5,4},{8,9},{9,8},{12,13},{13,12},{16,17},{17,16... | collective-permute-start | bytes 1572872 | tf_op jit(solution)/shard_map/ppermute | solution.py:43

commit v6 on v5

--- a/solution.py
+++ b/solution.py
@@ -186,13 +186,12 @@
         pairs.append((piece.at[:count], x_ref.at[start : start + count]))
         start += count
     run_copies(pairs, sems)
-    half = start // 2
     x_own, x_other = x_ref[:, half_of(core, QUARTER)], x_ref[:, half_of(1 - core, QUARTER)]
     for i in range(m):
         total = jnp.dot(x_other, sib_refs[i][...], preferred_element_type=F32)
         total += jnp.dot(x_own, own_refs[i][...], preferred_element_type=F32)
         for k, out in enumerate(outs):
-            out[:, i * HALF : (i + 1) * HALF] = total[k * half : (k + 1) * half].astype(out.dtype)
+            out[:, i * HALF : (i + 1) * HALF] = total[k * TOK : (k + 1) * TOK].astype(out.dtype)
 
 
 def project(pieces, own_w, sib_w, parts, dtype, after=()):
@@ -203,8 +202,8 @@
     return pl.pallas_call(
         functools.partial(project_kernel, rows=rows, extra=len(after), parts=parts),
         in_specs=[ANY] * len(pieces) + [VMEM] * (2 * len(parts)) + [ANY] * len(after),
-        out_specs=[VMEM] * 2,
-        out_shape=[pltpu.VMEM((total // 2, wide), dtype) for _ in range(2)],
+        out_specs=[VMEM] * len(pieces),
+        out_shape=[pltpu.VMEM((TOK, wide), dtype) for _ in pieces],
         scratch_shapes=[pltpu.VMEM((total, WIDE), BF), pltpu.SemaphoreType.DMA((len(pieces),))],
         compiler_params=pltpu.CompilerParams(vmem_limit_bytes=14 << 20),
         cost_estimate=cost(2 * total * WIDE * wide, 4 * WIDE * wide),
@@ -352,9 +351,11 @@
     away = [met, send(met, SIB)]
     queries = send(queries, OUT)
 
-    first, second = project(away, own_w, sib_w, (0,), BF)
-    far_k = send(first, BACK), send(second, OUT)
-    first, second = project(away, own_w, sib_w, (1,), BF, (first,))
+    (first,) = project(away[:1], own_w, sib_w, (0,), BF)
+    mine = send(first, BACK)
+    (second,) = project(away[1:], own_w, sib_w, (0,), BF, (first,))
+    far_k = mine, send(second, OUT)
+    first, second = project(away, own_w, sib_w, (1,), BF, (second,))
     far_v = send(first, BACK), send(second, OUT)
     near = project([to_sib, sib], own_w, sib_w, (0, 1), F32, (queries,))
     weights = weigh(near, far_k, (to_sib, sib, queries))

time: 118 us -> 117 us (level)
  blocking collectives: 76 us -> 74.2 us
    all_to_all x2, blocking collectives: 76 us -> 74.2 us  [spread(): lax.all_to_all(value, 'seg', 0, 0, tiled=True, axis_index_groups=[ORDER])]
    pallas_call x3 -> x4, Pallas kernels: 5.11 us -> 5.3 us  [project(): pl.pallas_call(functools.partial(project_kernel, rows=rows, extra=len(aft...]
  transfers between devices with their start and end apart: 11 -> 11, of which waited for: 4 -> 5; matrix products, arithmetic and copies ran while one was open for 0% -> 0% of each run, Pallas kernels for 9% -> 9%
where the time goes in v6:
time: 117 us
  blocking collectives  74.2 us (63%)
  starting transfers between devices  17.9 us (15%)
  Pallas kernels  14.8 us (13%)
  waiting for transfers between devices  9.63 us (8%)
    all_to_all x2, blocking collectives, spread(): lax.all_to_all(value, 'seg', 0, 0, tiled=True, axis_index_groups=[ORDER])  74.2 us
    ppermute x11, starting transfers between devices, send(): return lax.ppermute(value, BOTH, pairs)  17.9 us
    ppermute x11, waiting for transfers between devices, send(): return lax.ppermute(value, BOTH, pairs)  9.63 us
    pallas_call x4, Pallas kernels, project(): pl.pallas_call(functools.partial(project_kernel, rows=rows, extra=len(aft...  5.3 us
    pallas_call x1, Pallas kernels, sort_inputs(): pl.pallas_call(sort_kernel, in_specs=[HBM] * 3, out_specs=[VMEM] * 4, out...  2.67 us
  transfers between devices with their start and end apart: 11, of which 5 were waited for; matrix products, arithmetic and copies ran while one was open for 0% of the time, Pallas kernels for 9%

profile of v6, /device:TPU:1, one launch (start us, length us, event | category | flops | bytes accessed | tf_op | source)
XLA Modules:
  0.0 116.8 jit_solution(5432179907341091483)
XLA Ops:
  0.0 2.7 %shard_map.46 = (bf16[128,2048]{1,0:T(8,128)(2,1)S(1)}, bf16[192,2048]{1,0:T(8,128)(2,1)S(1)}, bf16[1024,1024]{1,0:T(8,128)(2,1)S(1)}, bf16[1024,1024]{1,0:T(8,128)(2,1)S(1)}) custom-call(bf16[128,4096]{1,0:T(8,128)(2,1)} %bitcast.6, bf16[64,2048]{1,0:T(8,128)(2,1)} %q_ref.1, bf16[1024,4096]{1,0:T(8,128)(2,1)} %w_ref.3), custom_call_target="tpu_custom_call" | custom-call | bytes 12582912 | tf_op jit(solution)/shard_map/pallas_call | solution.py:124
  2.7 3.3 %collective-permute-start.1 = (bf16[1024,1024]{1,0:T(8,128)(2,1)S(1)}, bf16[1024,1024]{1,0:T(8,128)(2,1)S(1)}, u32[]{:S(2)}, u32[]{:S(2)}) collective-permute-start(bf16[1024,1024]{1,0:T(8,128)(2,1)S(1)} %get-tuple-element.20), channel_id=1, source_target_pairs={{0,1},{1,0},{4,5},{5,4},{8,9},{9,8},{12,13},{13,12},{16,17},{17,16... | collective-permute-start | bytes 6291464 | tf_op jit(solution)/shard_map/ppermute | solution.py:43
  6.0 0.1 collective-permute-start.2
  6.1 0.4 collective-permute-start
  6.5 1.0 collective-permute-start.3
  7.5 2.2 %shard_map.47 = (bf16[1024,1024]{1,0:T(8,128)(2,1)S(1)}, bf16[1024,1024]{1,0:T(8,128)(2,1)S(1)}) custom-call(bf16[1024,4096]{1,0:T(8,128)(2,1)} %w_ref.3, bf16[192,2048]{1,0:T(8,128)(2,1)S(1)} %get-tuple-element.17.after_ref.own_ref.refs_0_), custom_call_target="tpu_custom_call" | custom-call | bytes 8388608 | tf_op jit(solution)/shard_map/pallas_call | solution.py:168
  9.8 5.1 %collective-permute-done.3.far_ref = bf16[128,2048]{1,0:T(8,128)(2,1)S(1)} collective-permute-done((bf16[128,2048]{1,0:T(8,128)(2,1)S(1)}, bf16[128,2048]{1,0:T(8,128)(2,1)S(1)}, u32[]{:S(2)}, u32[]{:S(2)}) %collective-permute-start.3) | collective-permute-done | bytes 524320 | tf_op jit(solution)/shard_map/ppermute | solution.py:43
  14.8 0.0 collective-permute-done.sib_ref.refs_1_
  14.8 0.1 shard_map.48
  15.0 2.3 %collective-permute-start.6 = (bf16[128,2048]{1,0:T(8,128)(2,1)S(1)}, bf16[128,2048]{1,0:T(8,128)(2,1)S(1)}, u32[]{:S(2)}, u32[]{:S(2)}) collective-permute-start(bf16[128,2048]{1,0:T(8,128)(2,1)S(1)} %get-tuple-element.26.refs_0_), channel_id=1, source_target_pairs={{0,1},{1,0},{4,5},{5,4},{8,9},{9,8},{12,13},{13,12},{16,17},{17,16... | collective-permute-start | bytes 1572872 | tf_op jit(solution)/shard_map/ppermute | solution.py:43
  17.2 0.0 collective-permute-start.4
  17.2 0.0 collective-permute-done.1.refs_4_.refs_2_
  17.2 0.8 shard_map.50.refs_3_
  18.0 1.5 %collective-permute-start.5 = (bf16[128,1024]{1,0:T(8,128)(2,1)S(1)}, bf16[128,1024]{1,0:T(8,128)(2,1)S(1)}, u32[]{:S(2)}, u32[]{:S(2)}) collective-permute-start(bf16[128,1024]{1,0:T(8,128)(2,1)S(1)} %shard_map.50.refs_3_), channel_id=1, source_target_pairs={{0,130},{1,3},{4,134},{5,7},{8,138},{9,11},{12,142},{13,15},{16,14... | collective-permute-start | bytes 786440 | tf_op jit(solution)/shard_map/ppermute | solution.py:43
  19.5 0.0 collective-permute-done.6.refs_0_.refs_1_
  19.5 0.8 shard_map.51.refs_4_
  20.3 1.3 %collective-permute-start.7 = (bf16[128,1024]{1,0:T(8,128)(2,1)S(1)}, bf16[128,1024]{1,0:T(8,128)(2,1)S(1)}, u32[]{:S(2)}, u32[]{:S(2)}) collective-permute-start(bf16[128,1024]{1,0:T(8,128)(2,1)S(1)} %shard_map.51.refs_4_), channel_id=1, source_target_pairs={{0,2},{1,131},{4,6},{5,135},{8,10},{9,139},{12,14},{13,143},{16,18... | collective-permute-start | bytes 786440 | tf_op jit(solution)/shard_map/ppermute | solution.py:43
  21.6 0.0 collective-permute-done.2.refs_5_.refs_3_
  21.6 1.3 %shard_map.53 = (bf16[128,1024]{1,0:T(8,128)(2,1)S(1)}, bf16[128,1024]{1,0:T(8,128)(2,1)S(1)}) custom-call(bf16[128,2048]{1,0:T(8,128)(2,1)S(1)} %get-tuple-element.26.refs_0_, bf16[128,2048]{1,0:T(8,128)(2,1)S(1)} %collective-permute-done.6.refs_0_.refs_1_, bf16[1024,1024]{1,0:T(8,128)(2,1)S(1)} %get-tuple-element.19.refs_3_.refs_2_, ...), custom_call_target="tpu_custom_call" | custom-call | flops 1073741824 | bytes 8388608 | tf_op jit(solution)/shard_map/pallas_call | solution.py:202
  23.0 0.3 collective-permute-start.8
  23.3 2.4 %collective-permute-start.9 = (bf16[128,1024]{1,0:T(8,128)(2,1)S(1)}, bf16[128,1024]{1,0:T(8,128)(2,1)S(1)}, u32[]{:S(2)}, u32[]{:S(2)}) collective-permute-start(bf16[128,1024]{1,0:T(8,128)(2,1)S(1)} %get-tuple-element.28), channel_id=1, source_target_pairs={{0,2},{1,131},{4,6},{5,135},{8,10},{9,139},{12,14},{13,143},{16,18... | collective-permute-start | bytes 786440 | tf_op jit(solution)/shard_map/ppermute | solution.py:43
  25.7 0.0 collective-permute-done.4.refs_6_.q_far
  25.7 2.4 %shard_map.49 = (f32[128,2048]{1,0:T(8,128)S(1)}, f32[128,2048]{1,0:T(8,128)S(1)}) custom-call(bf16[192,2048]{1,0:T(8,128)(2,1)S(1)} %get-tuple-element.17.after_ref.own_ref.refs_0_, bf16[192,2048]{1,0:T(8,128)(2,1)S(1)} %collective-permute-done.sib_ref.refs_1_, bf16[1024,1024]{1,0:T(8,128)(2,1)S(1)} %get-tuple-element.18.after_ref.refs_2_.refs_1_, ...), custom_call_target="tpu_custom_call" | custom-call | flops 2147483648 | bytes 16777216 | tf_op jit(solution)/shard_map/pallas_call | solution.py:202
  28.2 0.0 collective-permute-done.5.far0
  28.2 1.5 %collective-permute-done.7.far1 = bf16[128,1024]{1,0:T(8,128)(2,1)S(1)} collective-permute-done((bf16[128,1024]{1,0:T(8,128)(2,1)S(1)}, bf16[128,1024]{1,0:T(8,128)(2,1)S(1)}, u32[]{:S(2)}, u32[]{:S(2)}) %collective-permute-start.7) | collective-permute-done | bytes 262176 | tf_op jit(solution)/shard_map/ppermute | solution.py:43
  29.7 0.0 copy-start
  29.7 2.0 %shard_map.52.weights_ref = bf16[16,256,128]{2,1,0:T(8,128)(2,1)S(1)} custom-call(f32[128,2048]{1,0:T(8,128)S(1)} %get-tuple-element.24.near0, f32[128,2048]{1,0:T(8,128)S(1)} %get-tuple-element.25.near1, bf16[128,1024]{1,0:T(8,128)(2,1)S(1)} %collective-permute-done.5.far0, bf16[128,1024]{1,0:T(8,128)(2,1)S(1)} %collective-permute-done.7.far1, ...), custom_call_target="tpu_custom_call" | custom-call | flops 134217728 | bytes 4194304 | tf_op jit(solution)/shard_map/pallas_call | solution.py:232
  31.6 1.6 %collective-permute-done.8.far0 = bf16[128,1024]{1,0:T(8,128)(2,1)S(1)} collective-permute-done((bf16[128,1024]{1,0:T(8,128)(2,1)S(1)}, bf16[128,1024]{1,0:T(8,128)(2,1)S(1)}, u32[]{:S(2)}, u32[]{:S(2)}) %collective-permute-start.8) | collective-permute-done | bytes 262176 | tf_op jit(solution)/shard_map/ppermute | solution.py:43
  33.2 0.7 collective-permute-done.9.far1
  34.0 0.0 copy-done
  34.0 0.5 shard_map.54
  34.4 40.1 %all_to_all.10.update_ref = bf16[64,72,128]{2,1,0:T(8,128)(2,1)S(1)} all-to-all(bf16[64,72,128]{2,1,0:T(8,128)(2,1)S(1)} %shard_map.54), channel_id=1, replica_groups={{0,32,64,96,128,160,192,224,4,36,68,100,132,164,196,228,8,40,72,104,136..., dimensions={0} | all-to-all | bytes 2359296 | tf_op jit(solution)/shard_map/all_to_all | solution.py:342
  74.6 0.3 shard_map.55
  74.9 34.1 %all_to_all.11.states_ref = bf16[64,64,128]{2,1,0:T(8,128)(2,1)S(1)} all-to-all(bf16[64,64,128]{2,1,0:T(8,128)(2,1)S(1)} %shard_map.55), channel_id=1, replica_groups={{0,32,64,96,128,160,192,224,4,36,68,100,132,164,196,228,8,40,72,104,136..., dimensions={0} | all-to-all | bytes 2097152 | tf_op jit(solution)/shard_map/all_to_all | solution.py:342
  109.0 5.3 %collective-permute-start.10 = (bf16[32,64,128]{2,1,0:T(8,128)(2,1)S(1)}, bf16[32,64,128]{2,1,0:T(8,128)(2,1)S(1)}, u32[]{:S(2)}, u32[]{:S(2)}) collective-permute-start(bf16[32,64,128]{2,1,0:T(8,128)(2,1)S(1)} %shard_map.56), channel_id=1, source_target_pairs={{0,1},{1,0},{4,5},{5,4},{8,9},{9,8},{12,13},{13,12},{16,17},{17,16... | collective-permute-start | bytes 1572872 | tf_op jit(solution)/shard_map/ppermute | solution.py:43
  114.2 0.8 shard_map.57.refs_0_
  115.1 0.7 collective-permute-done.10
  115.8 0.8 shard_map.58
  (1 shorter events, 0.0 us)
Async XLA Ops:
  2.7 14.5 %collective-permute-start.1 = (bf16[1024,1024]{1,0:T(8,128)(2,1)S(1)}, bf16[1024,1024]{1,0:T(8,128)(2,1)S(1)}, u32[]{:S(2)}, u32[]{:S(2)}) collective-permute-start(bf16[1024,1024]{1,0:T(8,128)(2,1)S(1)} %get-tuple-element.20), channel_id=1, source_target_pairs={{0,1},{1,0},{4,5},{5,4},{8,9},{9,8},{12,13},{13,12},{16,17},{17,16... | collective-permute-start | bytes 6291464 | tf_op jit(solution)/shard_map/ppermute | solution.py:43
  6.0 15.6 %collective-permute-start.2 = (bf16[1024,1024]{1,0:T(8,128)(2,1)S(1)}, bf16[1024,1024]{1,0:T(8,128)(2,1)S(1)}, u32[]{:S(2)}, u32[]{:S(2)}) collective-permute-start(bf16[1024,1024]{1,0:T(8,128)(2,1)S(1)} %get-tuple-element.21), channel_id=1, source_target_pairs={{0,1},{1,0},{4,5},{5,4},{8,9},{9,8},{12,13},{13,12},{16,17},{17,16... | collective-permute-start | bytes 6291464 | tf_op jit(solution)/shard_map/ppermute | solution.py:43
  6.1 8.7 %collective-permute-start = (bf16[192,2048]{1,0:T(8,128)(2,1)S(1)}, bf16[192,2048]{1,0:T(8,128)(2,1)S(1)}, u32[]{:S(2)}, u32[]{:S(2)}) collective-permute-start(bf16[192,2048]{1,0:T(8,128)(2,1)S(1)} %get-tuple-element.17.after_ref.own_ref.refs_0_), channel_id=1, source_target_pairs={{0,1},{1,0},{4,5},{5,4},{8,9},{9,8},{12,13},{13,12},{16,17},{17,16... | collective-permute-start | bytes 2359304 | tf_op jit(solution)/shard_map/ppermute | solution.py:43
  6.5 8.3 %collective-permute-start.3 = (bf16[128,2048]{1,0:T(8,128)(2,1)S(1)}, bf16[128,2048]{1,0:T(8,128)(2,1)S(1)}, u32[]{:S(2)}, u32[]{:S(2)}) collective-permute-start(bf16[128,2048]{1,0:T(8,128)(2,1)S(1)} %get-tuple-element.22), channel_id=1, source_target_pairs={{0,2},{1,131},{4,6},{5,135},{8,10},{9,139},{12,14},{13,143},{16,18... | collective-permute-start | bytes 1572872 | tf_op jit(solution)/shard_map/ppermute | solution.py:43
  15.0 4.6 %collective-permute-start.6 = (bf16[128,2048]{1,0:T(8,128)(2,1)S(1)}, bf16[128,2048]{1,0:T(8,128)(2,1)S(1)}, u32[]{:S(2)}, u32[]{:S(2)}) collective-permute-start(bf16[128,2048]{1,0:T(8,128)(2,1)S(1)} %get-tuple-element.26.refs_0_), channel_id=1, source_target_pairs={{0,1},{1,0},{4,5},{5,4},{8,9},{9,8},{12,13},{13,12},{16,17},{17,16... | collective-permute-start | bytes 1572872 | tf_op jit(solution)/shard_map/ppermute | solution.py:43
  17.2 8.5 %collective-permute-start.4 = (bf16[128,1024]{1,0:T(8,128)(2,1)S(1)}, bf16[128,1024]{1,0:T(8,128)(2,1)S(1)}, u32[]{:S(2)}, u32[]{:S(2)}) collective-permute-start(bf16[128,1024]{1,0:T(8,128)(2,1)S(1)} %get-tuple-element.23), channel_id=1, source_target_pairs={{0,2},{1,131},{4,6},{5,135},{8,10},{9,139},{12,14},{13,143},{16,18... | collective-permute-start | bytes 786440 | tf_op jit(solution)/shard_map/ppermute | solution.py:43
  18.0 10.2 %collective-permute-start.5 = (bf16[128,1024]{1,0:T(8,128)(2,1)S(1)}, bf16[128,1024]{1,0:T(8,128)(2,1)S(1)}, u32[]{:S(2)}, u32[]{:S(2)}) collective-permute-start(bf16[128,1024]{1,0:T(8,128)(2,1)S(1)} %shard_map.50.refs_3_), channel_id=1, source_target_pairs={{0,130},{1,3},{4,134},{5,7},{8,138},{9,11},{12,142},{13,15},{16,14... | collective-permute-start | bytes 786440 | tf_op jit(solution)/shard_map/ppermute | solution.py:43
  20.3 9.3 %collective-permute-start.7 = (bf16[128,1024]{1,0:T(8,128)(2,1)S(1)}, bf16[128,1024]{1,0:T(8,128)(2,1)S(1)}, u32[]{:S(2)}, u32[]{:S(2)}) collective-permute-start(bf16[128,1024]{1,0:T(8,128)(2,1)S(1)} %shard_map.51.refs_4_), channel_id=1, source_target_pairs={{0,2},{1,131},{4,6},{5,135},{8,10},{9,139},{12,14},{13,143},{16,18... | collective-permute-start | bytes 786440 | tf_op jit(solution)/shard_map/ppermute | solution.py:43
  23.0 10.3 %collective-permute-start.8 = (bf16[128,1024]{1,0:T(8,128)(2,1)S(1)}, bf16[128,1024]{1,0:T(8,128)(2,1)S(1)}, u32[]{:S(2)}, u32[]{:S(2)}) collective-permute-start(bf16[128,1024]{1,0:T(8,128)(2,1)S(1)} %get-tuple-element.27), channel_id=1, source_target_pairs={{0,130},{1,3},{4,134},{5,7},{8,138},{9,11},{12,142},{13,15},{16,14... | collective-permute-start | bytes 786440 | tf_op jit(solution)/shard_map/ppermute | solution.py:43
  23.3 10.7 %collective-permute-start.9 = (bf16[128,1024]{1,0:T(8,128)(2,1)S(1)}, bf16[128,1024]{1,0:T(8,128)(2,1)S(1)}, u32[]{:S(2)}, u32[]{:S(2)}) collective-permute-start(bf16[128,1024]{1,0:T(8,128)(2,1)S(1)} %get-tuple-element.28), channel_id=1, source_target_pairs={{0,2},{1,131},{4,6},{5,135},{8,10},{9,139},{12,14},{13,143},{16,18... | collective-permute-start | bytes 786440 | tf_op jit(solution)/shard_map/ppermute | solution.py:43
  29.7 4.3 %copy-start = (f32[1,2048]{1,0:T(1,128)S(1)}, f32[1,2048]{1,0:T(1,128)}, u32[]{:S(2)}) copy-start(f32[1,2048]{1,0:T(1,128)} %gate_ref.1) | copy-start | bytes 24580
  109.0 6.8 %collective-permute-start.10 = (bf16[32,64,128]{2,1,0:T(8,128)(2,1)S(1)}, bf16[32,64,128]{2,1,0:T(8,128)(2,1)S(1)}, u32[]{:S(2)}, u32[]{:S(2)}) collective-permute-start(bf16[32,64,128]{2,1,0:T(8,128)(2,1)S(1)} %shard_map.56), channel_id=1, source_target_pairs={{0,1},{1,0},{4,5},{5,4},{8,9},{9,8},{12,13},{13,12},{16,17},{17,16... | collective-permute-start | bytes 1572872 | tf_op jit(solution)/shard_map/ppermute | solution.py:43

commit v7 on v6

--- a/solution.py
+++ b/solution.py
@@ -355,8 +355,10 @@
     mine = send(first, BACK)
     (second,) = project(away[1:], own_w, sib_w, (0,), BF, (first,))
     far_k = mine, send(second, OUT)
-    first, second = project(away, own_w, sib_w, (1,), BF, (second,))
-    far_v = send(first, BACK), send(second, OUT)
+    (first,) = project(away[:1], own_w, sib_w, (1,), BF, (second,))
+    mine = send(first, BACK)
+    (second,) = project(away[1:], own_w, sib_w, (1,), BF, (first,))
+    far_v = mine, send(second, OUT)
     near = project([to_sib, sib], own_w, sib_w, (0, 1), F32, (queries,))
     weights = weigh(near, far_k, (to_sib, sib, queries))
     states = spread(scan(spread(updates(weights, near, far_v, decay))))

time: 117 us -> 116 us (level)
  blocking collectives: 74.2 us -> 73 us
  starting transfers between devices: 17.9 us -> 16.7 us
    ppermute x11, starting transfers between devices: 17.9 us -> 16.7 us  [send(): return lax.ppermute(value, BOTH, pairs)]
    all_to_all x2, blocking collectives: 74.2 us -> 73 us  [spread(): lax.all_to_all(value, 'seg', 0, 0, tiled=True, axis_index_groups=[ORDER])]
    pallas_call x4 -> x5, Pallas kernels: 5.3 us -> 5.54 us  [project(): pl.pallas_call(functools.partial(project_kernel, rows=rows, extra=len(aft...]
where the time goes in v7:
time: 116 us
  blocking collectives  73 us (63%)
  starting transfers between devices  16.7 us (14%)
  Pallas kernels  15 us (13%)
  waiting for transfers between devices  10.6 us (9%)
    all_to_all x2, blocking collectives, spread(): lax.all_to_all(value, 'seg', 0, 0, tiled=True, axis_index_groups=[ORDER])  73 us
    ppermute x11, starting transfers between devices, send(): return lax.ppermute(value, BOTH, pairs)  16.7 us
    ppermute x11, waiting for transfers between devices, send(): return lax.ppermute(value, BOTH, pairs)  10.6 us
    pallas_call x5, Pallas kernels, project(): pl.pallas_call(functools.partial(project_kernel, rows=rows, extra=len(aft...  5.54 us
    pallas_call x1, Pallas kernels, sort_inputs(): pl.pallas_call(sort_kernel, in_specs=[HBM] * 3, out_specs=[VMEM] * 4, out...  2.67 us
  transfers between devices with their start and end apart: 11, of which 5 were waited for; matrix products, arithmetic and copies ran while one was open for 0% of the time, Pallas kernels for 9%

profile of v7, /device:TPU:1, one launch (start us, length us, event | category | flops | bytes accessed | tf_op | source)
XLA Modules:
  0.0 115.6 jit_solution(9615210052125311885)
XLA Ops:
  0.0 2.7 %shard_map.46 = (bf16[128,2048]{1,0:T(8,128)(2,1)S(1)}, bf16[192,2048]{1,0:T(8,128)(2,1)S(1)}, bf16[1024,1024]{1,0:T(8,128)(2,1)S(1)}, bf16[1024,1024]{1,0:T(8,128)(2,1)S(1)}) custom-call(bf16[128,4096]{1,0:T(8,128)(2,1)} %bitcast.6, bf16[64,2048]{1,0:T(8,128)(2,1)} %q_ref.1, bf16[1024,4096]{1,0:T(8,128)(2,1)} %w_ref.3), custom_call_target="tpu_custom_call" | custom-call | bytes 12582912 | tf_op jit(solution)/shard_map/pallas_call | solution.py:124
  2.7 3.3 %collective-permute-start.1 = (bf16[1024,1024]{1,0:T(8,128)(2,1)S(1)}, bf16[1024,1024]{1,0:T(8,128)(2,1)S(1)}, u32[]{:S(2)}, u32[]{:S(2)}) collective-permute-start(bf16[1024,1024]{1,0:T(8,128)(2,1)S(1)} %get-tuple-element.18), channel_id=1, source_target_pairs={{0,1},{1,0},{4,5},{5,4},{8,9},{9,8},{12,13},{13,12},{16,17},{17,16... | collective-permute-start | bytes 6291464 | tf_op jit(solution)/shard_map/ppermute | solution.py:43
  6.0 0.1 collective-permute-start.2
  6.1 0.4 collective-permute-start
  6.5 1.0 collective-permute-start.3
  7.5 2.2 %shard_map.47 = (bf16[1024,1024]{1,0:T(8,128)(2,1)S(1)}, bf16[1024,1024]{1,0:T(8,128)(2,1)S(1)}) custom-call(bf16[1024,4096]{1,0:T(8,128)(2,1)} %w_ref.3, bf16[192,2048]{1,0:T(8,128)(2,1)S(1)} %get-tuple-element.15.after_ref.own_ref.refs_0_), custom_call_target="tpu_custom_call" | custom-call | bytes 8388608 | tf_op jit(solution)/shard_map/pallas_call | solution.py:168
  9.8 5.1 %collective-permute-done.3.far_ref = bf16[128,2048]{1,0:T(8,128)(2,1)S(1)} collective-permute-done((bf16[128,2048]{1,0:T(8,128)(2,1)S(1)}, bf16[128,2048]{1,0:T(8,128)(2,1)S(1)}, u32[]{:S(2)}, u32[]{:S(2)}) %collective-permute-start.3) | collective-permute-done | bytes 524320 | tf_op jit(solution)/shard_map/ppermute | solution.py:43
  14.8 0.0 collective-permute-done.sib_ref.refs_1_
  14.8 0.1 shard_map.48
  15.0 2.3 %collective-permute-start.6 = (bf16[128,2048]{1,0:T(8,128)(2,1)S(1)}, bf16[128,2048]{1,0:T(8,128)(2,1)S(1)}, u32[]{:S(2)}, u32[]{:S(2)}) collective-permute-start(bf16[128,2048]{1,0:T(8,128)(2,1)S(1)} %get-tuple-element.24.refs_0_), channel_id=1, source_target_pairs={{0,1},{1,0},{4,5},{5,4},{8,9},{9,8},{12,13},{13,12},{16,17},{17,16... | collective-permute-start | bytes 1572872 | tf_op jit(solution)/shard_map/ppermute | solution.py:43
  17.2 0.0 collective-permute-start.4
  17.2 0.0 collective-permute-done.1.refs_4_.refs_2_
  17.2 0.8 shard_map.50.refs_3_
  18.0 1.5 %collective-permute-start.5 = (bf16[128,1024]{1,0:T(8,128)(2,1)S(1)}, bf16[128,1024]{1,0:T(8,128)(2,1)S(1)}, u32[]{:S(2)}, u32[]{:S(2)}) collective-permute-start(bf16[128,1024]{1,0:T(8,128)(2,1)S(1)} %shard_map.50.refs_3_), channel_id=1, source_target_pairs={{0,130},{1,3},{4,134},{5,7},{8,138},{9,11},{12,142},{13,15},{16,14... | collective-permute-start | bytes 786440 | tf_op jit(solution)/shard_map/ppermute | solution.py:43
  19.5 0.0 collective-permute-done.6.refs_0_
  19.5 0.8 shard_map.51.refs_3_
  20.3 1.3 %collective-permute-start.7 = (bf16[128,1024]{1,0:T(8,128)(2,1)S(1)}, bf16[128,1024]{1,0:T(8,128)(2,1)S(1)}, u32[]{:S(2)}, u32[]{:S(2)}) collective-permute-start(bf16[128,1024]{1,0:T(8,128)(2,1)S(1)} %shard_map.51.refs_3_), channel_id=1, source_target_pairs={{0,2},{1,131},{4,6},{5,135},{8,10},{9,139},{12,14},{13,143},{16,18... | collective-permute-start | bytes 786440 | tf_op jit(solution)/shard_map/ppermute | solution.py:43
  21.6 0.0 collective-permute-done.2.refs_5_.refs_2_
  21.6 0.8 shard_map.53.refs_3_
  22.4 0.8 shard_map.54
  23.2 0.1 collective-permute-start.9
  23.3 1.5 %collective-permute-start.8 = (bf16[128,1024]{1,0:T(8,128)(2,1)S(1)}, bf16[128,1024]{1,0:T(8,128)(2,1)S(1)}, u32[]{:S(2)}, u32[]{:S(2)}) collective-permute-start(bf16[128,1024]{1,0:T(8,128)(2,1)S(1)} %shard_map.53.refs_3_), channel_id=1, source_target_pairs={{0,130},{1,3},{4,134},{5,7},{8,138},{9,11},{12,142},{13,15},{16,14... | collective-permute-start | bytes 786440 | tf_op jit(solution)/shard_map/ppermute | solution.py:43
  24.8 0.0 collective-permute-done.4.refs_6_.q_far
  24.8 2.4 %shard_map.49 = (f32[128,2048]{1,0:T(8,128)S(1)}, f32[128,2048]{1,0:T(8,128)S(1)}) custom-call(bf16[192,2048]{1,0:T(8,128)(2,1)S(1)} %get-tuple-element.15.after_ref.own_ref.refs_0_, bf16[192,2048]{1,0:T(8,128)(2,1)S(1)} %collective-permute-done.sib_ref.refs_1_, bf16[1024,1024]{1,0:T(8,128)(2,1)S(1)} %get-tuple-element.16.after_ref.refs_2_.refs_1_, ...), custom_call_target="tpu_custom_call" | custom-call | flops 2147483648 | bytes 16777216 | tf_op jit(solution)/shard_map/pallas_call | solution.py:202
  27.2 0.4 collective-permute-done.5.far0
  27.6 1.6 %collective-permute-done.7.far1 = bf16[128,1024]{1,0:T(8,128)(2,1)S(1)} collective-permute-done((bf16[128,1024]{1,0:T(8,128)(2,1)S(1)}, bf16[128,1024]{1,0:T(8,128)(2,1)S(1)}, u32[]{:S(2)}, u32[]{:S(2)}) %collective-permute-start.7) | collective-permute-done | bytes 262176 | tf_op jit(solution)/shard_map/ppermute | solution.py:43
  29.3 0.0 copy-start
  29.3 2.0 %shard_map.52.weights_ref = bf16[16,256,128]{2,1,0:T(8,128)(2,1)S(1)} custom-call(f32[128,2048]{1,0:T(8,128)S(1)} %get-tuple-element.22.near0, f32[128,2048]{1,0:T(8,128)S(1)} %get-tuple-element.23.near1, bf16[128,1024]{1,0:T(8,128)(2,1)S(1)} %collective-permute-done.5.far0, bf16[128,1024]{1,0:T(8,128)(2,1)S(1)} %collective-permute-done.7.far1, ...), custom_call_target="tpu_custom_call" | custom-call | flops 134217728 | bytes 4194304 | tf_op jit(solution)/shard_map/pallas_call | solution.py:232
  31.2 2.7 %collective-permute-done.9.far1 = bf16[128,1024]{1,0:T(8,128)(2,1)S(1)} collective-permute-done((bf16[128,1024]{1,0:T(8,128)(2,1)S(1)}, bf16[128,1024]{1,0:T(8,128)(2,1)S(1)}, u32[]{:S(2)}, u32[]{:S(2)}) %collective-permute-start.9) | collective-permute-done | bytes 262176 | tf_op jit(solution)/shard_map/ppermute | solution.py:43
  34.0 0.0 collective-permute-done.8.far0
  34.0 0.0 copy-done
  34.0 0.5 shard_map.55
  34.4 38.8 %all_to_all.10.update_ref = bf16[64,72,128]{2,1,0:T(8,128)(2,1)S(1)} all-to-all(bf16[64,72,128]{2,1,0:T(8,128)(2,1)S(1)} %shard_map.55), channel_id=1, replica_groups={{0,32,64,96,128,160,192,224,4,36,68,100,132,164,196,228,8,40,72,104,136..., dimensions={0} | all-to-all | bytes 2359296 | tf_op jit(solution)/shard_map/all_to_all | solution.py:342
  73.2 0.3 shard_map.56
  73.5 34.2 %all_to_all.11.states_ref = bf16[64,64,128]{2,1,0:T(8,128)(2,1)S(1)} all-to-all(bf16[64,64,128]{2,1,0:T(8,128)(2,1)S(1)} %shard_map.56), channel_id=1, replica_groups={{0,32,64,96,128,160,192,224,4,36,68,100,132,164,196,228,8,40,72,104,136..., dimensions={0} | all-to-all | bytes 2097152 | tf_op jit(solution)/shard_map/all_to_all | solution.py:342
  107.8 5.2 %collective-permute-start.10 = (bf16[32,64,128]{2,1,0:T(8,128)(2,1)S(1)}, bf16[32,64,128]{2,1,0:T(8,128)(2,1)S(1)}, u32[]{:S(2)}, u32[]{:S(2)}) collective-permute-start(bf16[32,64,128]{2,1,0:T(8,128)(2,1)S(1)} %shard_map.57), channel_id=1, source_target_pairs={{0,1},{1,0},{4,5},{5,4},{8,9},{9,8},{12,13},{13,12},{16,17},{17,16... | collective-permute-start | bytes 1572872 | tf_op jit(solution)/shard_map/ppermute | solution.py:43
  113.0 0.8 shard_map.58.refs_0_
  113.9 0.7 collective-permute-done.10
  114.6 0.8 shard_map.59
  (1 shorter events, 0.0 us)
Async XLA Ops:
  2.7 14.5 %collective-permute-start.1 = (bf16[1024,1024]{1,0:T(8,128)(2,1)S(1)}, bf16[1024,1024]{1,0:T(8,128)(2,1)S(1)}, u32[]{:S(2)}, u32[]{:S(2)}) collective-permute-start(bf16[1024,1024]{1,0:T(8,128)(2,1)S(1)} %get-tuple-element.18), channel_id=1, source_target_pairs={{0,1},{1,0},{4,5},{5,4},{8,9},{9,8},{12,13},{13,12},{16,17},{17,16... | collective-permute-start | bytes 6291464 | tf_op jit(solution)/shard_map/ppermute | solution.py:43
  6.0 15.6 %collective-permute-start.2 = (bf16[1024,1024]{1,0:T(8,128)(2,1)S(1)}, bf16[1024,1024]{1,0:T(8,128)(2,1)S(1)}, u32[]{:S(2)}, u32[]{:S(2)}) collective-permute-start(bf16[1024,1024]{1,0:T(8,128)(2,1)S(1)} %get-tuple-element.19), channel_id=1, source_target_pairs={{0,1},{1,0},{4,5},{5,4},{8,9},{9,8},{12,13},{13,12},{16,17},{17,16... | collective-permute-start | bytes 6291464 | tf_op jit(solution)/shard_map/ppermute | solution.py:43
  6.1 8.7 %collective-permute-start = (bf16[192,2048]{1,0:T(8,128)(2,1)S(1)}, bf16[192,2048]{1,0:T(8,128)(2,1)S(1)}, u32[]{:S(2)}, u32[]{:S(2)}) collective-permute-start(bf16[192,2048]{1,0:T(8,128)(2,1)S(1)} %get-tuple-element.15.after_ref.own_ref.refs_0_), channel_id=1, source_target_pairs={{0,1},{1,0},{4,5},{5,4},{8,9},{9,8},{12,13},{13,12},{16,17},{17,16... | collective-permute-start | bytes 2359304 | tf_op jit(solution)/shard_map/ppermute | solution.py:43
  6.5 8.3 %collective-permute-start.3 = (bf16[128,2048]{1,0:T(8,128)(2,1)S(1)}, bf16[128,2048]{1,0:T(8,128)(2,1)S(1)}, u32[]{:S(2)}, u32[]{:S(2)}) collective-permute-start(bf16[128,2048]{1,0:T(8,128)(2,1)S(1)} %get-tuple-element.20), channel_id=1, source_target_pairs={{0,2},{1,131},{4,6},{5,135},{8,10},{9,139},{12,14},{13,143},{16,18... | collective-permute-start | bytes 1572872 | tf_op jit(solution)/shard_map/ppermute | solution.py:43
  15.0 4.6 %collective-permute-start.6 = (bf16[128,2048]{1,0:T(8,128)(2,1)S(1)}, bf16[128,2048]{1,0:T(8,128)(2,1)S(1)}, u32[]{:S(2)}, u32[]{:S(2)}) collective-permute-start(bf16[128,2048]{1,0:T(8,128)(2,1)S(1)} %get-tuple-element.24.refs_0_), channel_id=1, source_target_pairs={{0,1},{1,0},{4,5},{5,4},{8,9},{9,8},{12,13},{13,12},{16,17},{17,16... | collective-permute-start | bytes 1572872 | tf_op jit(solution)/shard_map/ppermute | solution.py:43
  17.2 7.5 %collective-permute-start.4 = (bf16[128,1024]{1,0:T(8,128)(2,1)S(1)}, bf16[128,1024]{1,0:T(8,128)(2,1)S(1)}, u32[]{:S(2)}, u32[]{:S(2)}) collective-permute-start(bf16[128,1024]{1,0:T(8,128)(2,1)S(1)} %get-tuple-element.21), channel_id=1, source_target_pairs={{0,2},{1,131},{4,6},{5,135},{8,10},{9,139},{12,14},{13,143},{16,18... | collective-permute-start | bytes 786440 | tf_op jit(solution)/shard_map/ppermute | solution.py:43
  18.0 9.6 %collective-permute-start.5 = (bf16[128,1024]{1,0:T(8,128)(2,1)S(1)}, bf16[128,1024]{1,0:T(8,128)(2,1)S(1)}, u32[]{:S(2)}, u32[]{:S(2)}) collective-permute-start(bf16[128,1024]{1,0:T(8,128)(2,1)S(1)} %shard_map.50.refs_3_), channel_id=1, source_target_pairs={{0,130},{1,3},{4,134},{5,7},{8,138},{9,11},{12,142},{13,15},{16,14... | collective-permute-start | bytes 786440 | tf_op jit(solution)/shard_map/ppermute | solution.py:43
  20.3 8.9 %collective-permute-start.7 = (bf16[128,1024]{1,0:T(8,128)(2,1)S(1)}, bf16[128,1024]{1,0:T(8,128)(2,1)S(1)}, u32[]{:S(2)}, u32[]{:S(2)}) collective-permute-start(bf16[128,1024]{1,0:T(8,128)(2,1)S(1)} %shard_map.51.refs_3_), channel_id=1, source_target_pairs={{0,2},{1,131},{4,6},{5,135},{8,10},{9,139},{12,14},{13,143},{16,18... | collective-permute-start | bytes 786440 | tf_op jit(solution)/shard_map/ppermute | solution.py:43
  23.2 10.8 %collective-permute-start.9 = (bf16[128,1024]{1,0:T(8,128)(2,1)S(1)}, bf16[128,1024]{1,0:T(8,128)(2,1)S(1)}, u32[]{:S(2)}, u32[]{:S(2)}) collective-permute-start(bf16[128,1024]{1,0:T(8,128)(2,1)S(1)} %shard_map.54), channel_id=1, source_target_pairs={{0,2},{1,131},{4,6},{5,135},{8,10},{9,139},{12,14},{13,143},{16,18... | collective-permute-start | bytes 786440 | tf_op jit(solution)/shard_map/ppermute | solution.py:43
  23.3 10.7 %collective-permute-start.8 = (bf16[128,1024]{1,0:T(8,128)(2,1)S(1)}, bf16[128,1024]{1,0:T(8,128)(2,1)S(1)}, u32[]{:S(2)}, u32[]{:S(2)}) collective-permute-start(bf16[128,1024]{1,0:T(8,128)(2,1)S(1)} %shard_map.53.refs_3_), channel_id=1, source_target_pairs={{0,130},{1,3},{4,134},{5,7},{8,138},{9,11},{12,142},{13,15},{16,14... | collective-permute-start | bytes 786440 | tf_op jit(solution)/shard_map/ppermute | solution.py:43
  29.3 4.7 %copy-start = (f32[1,2048]{1,0:T(1,128)S(1)}, f32[1,2048]{1,0:T(1,128)}, u32[]{:S(2)}) copy-start(f32[1,2048]{1,0:T(1,128)} %gate_ref.1) | copy-start | bytes 24580
  107.8 6.8 %collective-permute-start.10 = (bf16[32,64,128]{2,1,0:T(8,128)(2,1)S(1)}, bf16[32,64,128]{2,1,0:T(8,128)(2,1)S(1)}, u32[]{:S(2)}, u32[]{:S(2)}) collective-permute-start(bf16[32,64,128]{2,1,0:T(8,128)(2,1)S(1)} %shard_map.57), channel_id=1, source_target_pairs={{0,1},{1,0},{4,5},{5,4},{8,9},{9,8},{12,13},{13,12},{16,17},{17,16... | collective-permute-start | bytes 1572872 | tf_op jit(solution)/shard_map/ppermute | solution.py:43
